TPU v7x, 128 devices: a whole 4x4x4 slice. The times are simulated.
128 devices in a mesh: index: 16 (over x, z), reader: 8 (over y, core).
Axes of the slice: x: 4, y: 4, z: 4, core: 2. Of those that a mesh axis runs over, the one named last changes fastest.
Arguments:
- question_emb: bfloat16 [128, 768], P(('index', 'reader')), may hold values from -6 to 6
- probes: int32 [128, 32], P(('index', 'reader')), may hold values from 0 to 511, all different within a row
- codes: bfloat16 [512, 128, 768], P('index'), may hold values from -0.21875 to 0.21875
- code_scale: float32 [512, 128], P('index'), may hold values from 0.25 to 4
- question_state: bfloat16 [128, 2048], P(('index', 'reader')), may hold values from -6 to 6
- top_passages: int32 [128, 20], P(('index', 'reader')), may hold values from 0 to 4095, as said below
- soft_weight: float32 [128, 20], P(('index', 'reader')), may hold values from 0.02 to 0.5
- passage_home: int32 [4096], replicated, may hold values from 0 to 4095, as said below
- passage_states: bfloat16 [4096, 8, 2048], P('index'), may hold values from -6 to 6
- norm_gain: float32 [2048], replicated, may hold values from 0.25 to 1.75
- w_gate: bfloat16 [2048, 4096], P(None, 'index'), may hold values from -0.125 to 0.125
- w_up: bfloat16 [2048, 4096], P(None, 'index'), may hold values from -0.125 to 0.125
- w_out: bfloat16 [4096, 2048], P('index'), may hold values from -0.09375 to 0.09375
- cotangent: bfloat16 [128, 20, 8, 2048], P(('index', 'reader')), may hold values from -3 to 3
Outputs:
- probe_scores: float32 [128, 32, 128], P(('index', 'reader'))
- grad_out: float32 [4096, 2048], P('index', 'reader')
- grad_gain: float32 [2048], P(('index', 'reader'))
Inputs may be any that keep to these rules, and one draw needn't show every extreme that they name: `probes`: each question names 32 different clusters; every cluster is named by some question. A permutation: passage p's state is row passage_home[p] of passage_states, held by index shard passage_home[p] // 256. `top_passages`: each question names 20 different passages, at most 3 of them held by one index shard. For the questions of the devices with one reader index, some index shard holds exactly 3 passages of each of them.
All inputs are finite; a program needn't handle non-finite values.
Results may differ from a plain program's by a relative error of at most 0.022.
Values may be sent and summed in bfloat16 or wider, within the bound.
No kernel may reach another device: no remote copies, remote signals or barrier semaphores. Data moves between devices by JAX's collectives and lax.ppermute only.
A program may use at most 256 MiB of HBM per device.

v0:
```python
import functools
import math

import jax
import jax.numpy as jnp
from jax import lax
from jax.experimental import pallas as pl
from jax.experimental.pallas import tpu as pltpu
from jax.sharding import PartitionSpec as P

BF16 = jnp.bfloat16
F32 = jnp.float32
I32 = jnp.int32

CAP = 3
NI = 16
NR = 8
TOPK = 20
NPROBE = 32
LP = 8
D = 2048
FS = 256
ROWS = TOPK * LP
PASS_DEV = 256
CLUS_DEV = 32
GELU_C = math.sqrt(2.0 / math.pi)
BOTH = ("index", "reader")


def pairs_of(move):
    pairs = []
    for x in range(4):
        for z in range(4):
            for y in range(4):
                for c in range(2):
                    tx, tz = move(x, z, c)
                    pairs.append(((x * 4 + z) * 8 + y * 2 + c, (tx * 4 + tz) * 8 + y * 2 + c))
    return pairs


def ring_move(step):
    return lambda x, z, c: ((x + step) % 4, z) if c == 0 else (x, (z + step) % 4)


def pair_move(x, z, c):
    return (x, z ^ 1) if c == 0 else (x ^ 1, z)


def partner_move(x, z, c):
    return (x, 3 - z) if c == 0 else (3 - x, z)


def ring(v, step):
    return lax.ppermute(v, BOTH, pairs_of(ring_move(step)))


def pair(v):
    return lax.ppermute(v, BOTH, pairs_of(pair_move))


def partner(v):
    return lax.ppermute(v, BOTH, pairs_of(partner_move))


def plan_kernel(top_ref, probes_ref, home_ref, emb_ref, msg_ref, src_ref):
    shape = (NI, 8, 128)
    owner_id = lax.broadcasted_iota(I32, shape, 0)
    lane_id = lax.broadcasted_iota(I32, shape, 2)
    row_id = lax.broadcasted_iota(I32, shape, 1)
    vec = jnp.where(lane_id >= 8, 64, 0)
    owners = []
    for k in range(TOPK):
        loc = home_ref[top_ref[0, k]]
        owner = loc // PASS_DEV
        rank = jnp.int32(0)
        for earlier in owners:
            rank = rank + jnp.where(earlier == owner, 1, 0)
        owners.append(owner)
        src_ref[0, k] = owner * CAP + rank
        vec = jnp.where((owner_id == owner) & (lane_id == rank), loc % PASS_DEV, vec)
    for k in range(NPROBE):
        c = probes_ref[0, k]
        vec = jnp.where((owner_id == c // CLUS_DEV) & (lane_id == 8 + k), c % CLUS_DEV, vec)
    emb = jnp.broadcast_to(emb_ref[...][None], shape)
    msg_ref[...] = jnp.where(row_id == 6, vec.astype(F32), emb).astype(BF16)


def make_plan(top, probes, home, emb):
    emb8 = jnp.pad(emb.astype(F32).reshape(6, 128), ((0, 2), (0, 0)))
    smem = pl.BlockSpec(memory_space=pltpu.SMEM)
    vmem = pl.BlockSpec(memory_space=pltpu.VMEM)
    return pl.pallas_call(
        plan_kernel,
        out_shape=(
            jax.ShapeDtypeStruct((NI, 8, 128), BF16),
            jax.ShapeDtypeStruct((1, TOPK), I32),
        ),
        in_specs=[smem, smem, smem, vmem],
        out_specs=(vmem, smem),
        name="plan",
    )(top, probes, home, emb8)


def pick_kernel(slot_ref, states_ref, out_ref, sems):
    copies = []
    for i in range(NI * CAP):
        row = slot_ref[i // CAP, i % CAP]
        copy = pltpu.make_async_copy(states_ref.at[row], out_ref.at[i], sems.at[i])
        copy.start()
        copies.append(copy)
    for copy in copies:
        copy.wait()


def pick_slots(slots, states):
    return pl.pallas_call(
        pick_kernel,
        out_shape=jax.ShapeDtypeStruct((NI * CAP, LP, D), BF16),
        in_specs=[pl.BlockSpec(memory_space=pltpu.SMEM), pl.BlockSpec(memory_space=pl.ANY)],
        out_specs=pl.BlockSpec(memory_space=pl.ANY),
        scratch_shapes=[pltpu.SemaphoreType.DMA((NI * CAP,))],
        cost_estimate=pl.CostEstimate(flops=0, bytes_accessed=2 * NI * CAP * LP * D * 2, transcendentals=0),
        name="pick",
    )(slots, states)


def norm_kernel(src_ref, recv_ref, state_ref, gain_ref, out_ref, buf, sems):
    copies = []
    for k in range(TOPK):
        copy = pltpu.make_async_copy(recv_ref.at[src_ref[0, k]], buf.at[k], sems.at[k])
        copy.start()
        copies.append(copy)
    state = state_ref[...].astype(F32)
    gain = gain_ref[...]
    for k in range(TOPK // 2):
        copies[2 * k].wait()
        copies[2 * k + 1].wait()
        x = buf[2 * k : 2 * k + 2].astype(F32).reshape(2 * LP, D) + state
        inv = lax.rsqrt(jnp.mean(x * x, axis=-1, keepdims=True) + 1e-06)
        out_ref[2 * LP * k : 2 * LP * (k + 1), :] = (x * inv * gain).astype(BF16)


def norm_rows(src, recv, state, gain):
    vmem = pl.BlockSpec(memory_space=pltpu.VMEM)
    return pl.pallas_call(
        norm_kernel,
        out_shape=jax.ShapeDtypeStruct((ROWS, D), BF16),
        in_specs=[
            pl.BlockSpec(memory_space=pltpu.SMEM),
            pl.BlockSpec(memory_space=pl.ANY),
            vmem,
            vmem,
        ],
        out_specs=vmem,
        scratch_shapes=[pltpu.VMEM((TOPK, LP, D), BF16), pltpu.SemaphoreType.DMA((TOPK,))],
        name="norm",
    )(src, recv, state, gain)


NT = (((1,), (1,)), ((), ()))


def layer_kernel(blocks, tile, last, *refs):
    n_in = refs[:blocks]
    d_in = refs[blocks : 2 * blocks]
    wg_in, wu_in, wo_in, wp_in = refs[2 * blocks : 2 * blocks + 4]
    rest = refs[2 * blocks + 4 :]
    if last:
        acc_in, gacc_ref, gain_ref, own_ref, par_ref, gout_ref = rest[:6]
        rest = rest[6:]
    else:
        acc_ref, gout_ref = rest[:2]
        rest = rest[2:]
    nbuf, dbuf, wg, wu, wo, act, dgate, dup = rest[:8]
    rest = rest[8:]
    if last:
        acc_ref = rest[0]
        rest = rest[1:]
    sems = rest[0]
    count = [0]

    def start(src, dst):
        copy = pltpu.make_async_copy(src, dst, sems.at[count[0]])
        count[0] += 1
        copy.start()
        return copy

    first, second, third = [], [], []
    first.append(start(wg_in, wg.at[:, pl.ds(0, FS)]))
    first.append(start(wu_in, wu.at[:, pl.ds(0, FS)]))
    for j in range(4):
        first.append(start(wp_in.at[pl.ds(j * 1536, 512)], wg.at[pl.ds(j * 512, 512), pl.ds(FS, FS)]))
        first.append(start(wp_in.at[pl.ds(j * 1536 + 512, 512)], wu.at[pl.ds(j * 512, 512), pl.ds(FS, FS)]))
    for b in range(blocks):
        first.append(start(n_in[b], nbuf.at[pl.ds(b * ROWS, ROWS)]))
    second.append(start(wo_in, wo.at[pl.ds(0, FS)]))
    for j in range(4):
        for h in range(2):
            second.append(
                start(
                    wp_in.at[pl.ds(j * 1536 + 1024 + h * FS, FS)],
                    wo.at[pl.ds(FS, FS), pl.ds(j * 512 + h * FS, FS)],
                )
            )
    for b in range(blocks):
        second.append(start(d_in[b], dbuf.at[pl.ds(b * ROWS, ROWS)]))
    if last:
        third.append(start(acc_in, acc_ref))
    for copy in first + second:
        copy.wait()

    def body(t, carry):
        rows = pl.ds(pl.multiple_of(t * tile, 16), tile)
        n = nbuf[rows, :]
        gate = jnp.dot(n, wg[...], preferred_element_type=F32)
        up = jnp.dot(n, wu[...], preferred_element_type=F32)
        d_act = lax.dot_general(dbuf[rows, :], wo[...], NT, preferred_element_type=F32)
        inner = GELU_C * (gate + 0.044715 * gate * gate * gate)
        th = jnp.tanh(inner)
        half = 0.5 * (1.0 + th)
        gelu = gate * half
        slope = half + 0.5 * gate * (1.0 - th * th) * GELU_C * (1.0 + 3.0 * 0.044715 * gate * gate)
        act[rows, :] = (gelu * up).astype(BF16)
        dgate[rows, :] = (d_act * up * slope).astype(BF16)
        dup[rows, :] = (d_act * gelu).astype(BF16)
        return carry

    lax.fori_loop(0, blocks * ROWS // tile, body, 0)

    def gain_body(j, carry):
        cols = pl.ds(pl.multiple_of(j * 512, 512), 512)
        dn = lax.dot_general(dgate[...], wg[cols, :], NT, preferred_element_type=F32)
        dn = dn + lax.dot_general(dup[...], wu[cols, :], NT, preferred_element_type=F32)
        part = jnp.sum(dn * nbuf[:, cols].astype(F32), axis=0, keepdims=True)
        if last:
            part = (part + gacc_ref[:, cols]) / gain_ref[:, cols]
        gout_ref[:, cols] = part
        return carry

    lax.fori_loop(0, 4, gain_body, 0)
    for copy in third:
        copy.wait()
    act_t = act[...].T

    def out_body(r, carry):
        cols = pl.ds(pl.multiple_of(r * FS, FS), FS)
        part = jnp.dot(act_t, dbuf[:, cols], preferred_element_type=F32)
        if last:
            part = part + acc_ref[r]
            own_ref[r] = part[:FS]
            par_ref[r] = part[FS:].astype(BF16)
        else:
            acc_ref[r] = part
        return carry

    lax.fori_loop(0, NR, out_body, 0)


def layer(n_blocks, d_blocks, weights, tile, carried=None):
    blocks = len(n_blocks)
    rows = blocks * ROWS
    last = carried is not None
    any_ = pl.BlockSpec(memory_space=pl.ANY)
    vmem = pl.BlockSpec(memory_space=pltpu.VMEM)
    args = [*n_blocks, *d_blocks, *weights]
    in_specs = [any_] * len(args)
    if last:
        args += list(carried)
        in_specs += [any_, vmem, vmem]
        out_shape = (
            jax.ShapeDtypeStruct((NR, FS, FS), F32),
            jax.ShapeDtypeStruct((NR, FS, FS), BF16),
            jax.ShapeDtypeStruct((1, D), F32),
        )
    else:
        out_shape = (
            jax.ShapeDtypeStruct((NR, 2 * FS, FS), F32),
            jax.ShapeDtypeStruct((1, D), F32),
        )
    scratch = [
        pltpu.VMEM((rows, D), BF16),
        pltpu.VMEM((rows, D), BF16),
        pltpu.VMEM((D, 2 * FS), BF16),
        pltpu.VMEM((D, 2 * FS), BF16),
        pltpu.VMEM((2 * FS, D), BF16),
        pltpu.VMEM((rows, 2 * FS), BF16),
        pltpu.VMEM((rows, 2 * FS), BF16),
        pltpu.VMEM((rows, 2 * FS), BF16),
    ]
    if last:
        scratch.append(pltpu.VMEM((NR, 2 * FS, FS), F32))
    scratch.append(pltpu.SemaphoreType.DMA((2 * blocks + 20,)))
    return pl.pallas_call(
        functools.partial(layer_kernel, blocks, tile, last),
        out_shape=out_shape,
        in_specs=in_specs,
        out_specs=tuple(vmem for _ in out_shape),
        scratch_shapes=scratch,
        compiler_params=pltpu.CompilerParams(vmem_limit_bytes=40 * 1024 * 1024),
        cost_estimate=pl.CostEstimate(
            flops=12 * rows * D * 2 * FS, bytes_accessed=4 * rows * D + 6 * D * 2 * FS, transcendentals=rows * 512
        ),
        name="layer_last" if last else "layer_first",
    )(*args)


def shards(
    question_emb,
    probes,
    codes,
    code_scale,
    question_state,
    top_passages,
    soft_weight,
    passage_home,
    passage_states,
    norm_gain,
    w_gate,
    w_up,
    w_out,
    cotangent,
):
    dy0 = (soft_weight[:, :, None, None] * cotangent.astype(F32)).astype(BF16).reshape(ROWS, D)
    dyp = pair(dy0)
    dy_a = [dy0, ring(dy0, 1), ring(dy0, -1), ring(dy0, 2), dyp]
    y = lax.axis_index("reader") // 2
    piece = jnp.concatenate(
        [
            lax.dynamic_slice(w_gate, (y * 512, 0), (512, FS)),
            lax.dynamic_slice(w_up, (y * 512, 0), (512, FS)),
            lax.dynamic_slice(w_out, (0, y * 512), (FS, FS)),
            lax.dynamic_slice(w_out, (0, y * 512 + FS), (FS, FS)),
        ],
        axis=0,
    )
    piece = partner(piece)
    wp = lax.all_gather(
        piece, "reader", axis=0, tiled=True, axis_index_groups=[[0, 2, 4, 6], [1, 3, 5, 7]]
    )
    weights = (w_gate, w_up, w_out, wp)

    msg, src = make_plan(top_passages, probes, passage_home, question_emb)
    asked = lax.all_to_all(msg, "index", 0, 0, tiled=True)
    slots = asked[:, 6, :CAP].astype(I32)
    blocks = pick_slots(slots, passage_states)
    recv = lax.all_to_all(blocks, "index", 0, 0, tiled=True)
    gain_row = norm_gain.reshape(1, D)
    n0 = norm_rows(src, recv, question_state, gain_row)

    dy_b = [ring(dyp, 1), ring(dyp, -1), ring(dyp, 2)]
    np_ = pair(n0)
    n_a = [n0, ring(n0, 1), ring(n0, -1), ring(n0, 2), np_]
    n_b = [ring(np_, 1), ring(np_, -1), ring(np_, 2)]

    group_emb = asked[:, :6, :].reshape(NI, 768)
    every_score = (
        jnp.einsum("qe,cse->qcs", group_emb, codes, preferred_element_type=F32) * code_scale[None]
    )
    local = asked[:, 6, 8 : 8 + NPROBE].astype(I32)
    hot = (local[:, :, None] == jnp.arange(CLUS_DEV, dtype=I32)[None, None, :]).astype(F32)
    picked = jnp.einsum("qpc,qcs->qps", hot, every_score, precision=lax.Precision.HIGHEST)

    acc_a, gain_a = layer(n_a, dy_a, weights, 400)
    own, par, gain_part = layer(n_b, dy_b, weights, 240, (acc_a, gain_a, gain_row))

    from_partner = partner(par)
    tail = jnp.concatenate(
        [picked, gain_part.reshape(NI, 1, 128), jnp.zeros((NI, 7, 128), F32)], axis=1
    )
    tail = lax.all_to_all(tail, "index", 0, 0, tiled=True)
    tail = jnp.sum(tail, axis=0)
    probe_scores = tail[None, :NPROBE]
    gain128 = tail[NPROBE].reshape(NR, 1, 16)
    hi = gain128.astype(BF16)
    lo = (gain128 - hi.astype(F32)).astype(BF16)
    gain_rows = jnp.pad(jnp.concatenate([hi, lo], axis=2), ((0, 0), (0, 7), (0, FS - 32)))
    total = (own + from_partner.astype(F32)).astype(BF16)
    out = lax.all_to_all(jnp.concatenate([total, gain_rows], axis=1), "reader", 0, 0, tiled=True)
    out = jnp.sum(out.astype(F32), axis=0)
    grad_out = out[:FS]
    grad_gain = out[FS, :16] + out[FS, 16:32]
    return probe_scores, grad_out, grad_gain


def solution(mesh):
    return jax.shard_map(
        shards,
        mesh=mesh,
        in_specs=(
            P(("index", "reader"), None),
            P(("index", "reader"), None),
            P("index", None, None),
            P("index", None),
            P(("index", "reader"), None),
            P(("index", "reader"), None),
            P(("index", "reader"), None),
            P(),
            P("index", None, None),
            P(),
            P(None, "index"),
            P(None, "index"),
            P("index", None),
            P(("index", "reader"), None, None, None),
        ),
        out_specs=(
            P(("index", "reader"), None, None),
            P("index", "reader"),
            P(("index", "reader")),
        ),
        check_vma=False,
    )
```

profile of v0, /device:TPU:1, one launch (start us, length us, event | category | flops | bytes accessed | tf_op | source)
XLA Modules:
  0.0 256.5 jit_solution(5444305187367567783)
XLA Ops:
  9.4 3.4 %collective-permute-start.8 = (bf16[1536,256]{1,0:T(8,128)(2,1)S(1)}, bf16[1536,256]{1,0:T(8,128)(2,1)S(1)}, u32[]{:S(2)}, u32[]{:S(2)}) collective-permute-start(bf16[1536,256]{1,0:T(8,128)(2,1)S(1)} %pad_maximum_fusion.1), channel_id=1, source_target_pairs={{0,24},{1,97},{2,26},{3,99},{4,28},{5,101},{6,30},{7,103},{8,16},{... | collective-permute-start | bytes 2359304 | tf_op jit(solution)/shard_map/ppermute | solution.py:62
  12.8 9.7 %collective-permute-done.8 = bf16[1536,256]{1,0:T(8,128)(2,1)S(1)} collective-permute-done((bf16[1536,256]{1,0:T(8,128)(2,1)S(1)}, bf16[1536,256]{1,0:T(8,128)(2,1)S(1)}, u32[]{:S(2)}, u32[]{:S(2)}) %collective-permute-start.8) | collective-permute-done | bytes 786464 | tf_op jit(solution)/shard_map/ppermute | solution.py:62
  24.0 2.3 plan.1
  26.3 14.0 %all_to_all.20 = bf16[16,8,128]{2,1,0:T(8,128)(2,1)S(1)} all-to-all(bf16[16,8,128]{2,1,0:T(8,128)(2,1)} %get-tuple-element.10), channel_id=1, replica_groups=mesh['index'=16,'reader'=8] {'index'}, dimensions={0} | all-to-all | bytes 65536 | tf_op jit(solution)/shard_map/all_to_all | solution.py:343
  40.9 50.0 %pick.1 = bf16[48,8,2048]{2,1,0:T(8,128)(2,1)} custom-call(s32[16,3]{1,0:T(8,128)} %bitcast.26, bf16[256,8,2048]{2,1,0:T(8,128)(2,1)} %states_ref.1), custom_call_target="tpu_custom_call" | custom-call | bytes 3145728 | tf_op jit(solution)/shard_map/pick/pallas_call | solution.py:116
  90.9 4.5 %all-to-all-start.1 = ((bf16[48,8,2048]{2,1,0:T(8,128)(2,1)}), bf16[48,8,2048]{2,1,0:T(8,128)(2,1)}, u32[]{:S(2)}, u32[]{:S(2)}) async-start(bf16[48,8,2048]{2,1,0:T(8,128)(2,1)} %pick.1), calls=%async_computation.1 | async-start | bytes 3145728 | tf_op jit(solution)/shard_map/all_to_all | solution.py:346
  98.2 1.5 collective-permute-start.13
  99.7 1.5 collective-permute-start.14
  101.2 24.6 %collective-permute-done.4.refs_9_ = bf16[160,2048]{1,0:T(8,128)(2,1)} collective-permute-done((bf16[160,2048]{1,0:T(8,128)(2,1)S(1)}, bf16[160,2048]{1,0:T(8,128)(2,1)}, u32[]{:S(2)}, u32[]{:S(2)}) %collective-permute-start.4) | collective-permute-done | bytes 655392 | tf_op jit(solution)/shard_map/ppermute | solution.py:58
  127.0 3.8 %norm.1.refs_0_ = bf16[160,2048]{1,0:T(8,128)(2,1)} custom-call(s32[1,20]{1,0:T(1,128)} %get-tuple-element.11.src_ref, bf16[48,8,2048]{2,1,0:T(8,128)(2,1)} %all-to-all-done.1.recv_ref, bf16[1,2048]{1,0:T(2,128)(2,1)} %state_ref.1, f32[1,2048]{1,0:T(1,128)} %bitcast.19), custom_call_target="tpu_custom_call" | custom-call | tf_op jit(solution)/shard_map/norm/pallas_call | solution.py:145
  131.8 1.7 collective-permute-start.10
  135.6 2.3 collective-permute-done.14.refs_8_
  139.6 4.6 %convolution_multiply_fusion = f32[16,32,128]{2,0,1:T(8,128)S(1)} fusion(bf16[16,768,1]{1,0,2:T(8,128)(2,1)S(1)} %reshape.79, bf16[32,128,768]{2,1,0:T(8,128)(2,1)} %param.16, f32[32,128]{1,0:T(8,128)S(1)} %copy-done.16), kind=kOutput, calls=%fused_computation.3 | convolution fusion | flops 100728832 | bytes 6594560 | tf_op jit(solution)/shard_map/qe,cse->qcs/dot_general | solution.py:357
  145.0 3.3 %collective-permute-start.6 = (bf16[160,2048]{1,0:T(8,128)(2,1)}, bf16[160,2048]{1,0:T(8,128)(2,1)}, u32[]{:S(2)}, u32[]{:S(2)}) collective-permute-start(bf16[160,2048]{1,0:T(8,128)(2,1)} %collective-permute-done.4.refs_9_), channel_id=1, source_target_pairs={{0,96},{1,25},{2,98},{3,27},{4,100},{5,29},{6,102},{7,31},{8,104},... | collective-permute-start | bytes 1966088 | tf_op jit(solution)/shard_map/ppermute | solution.py:54
  149.0 9.9 %collective-permute-done.11.refs_3_ = bf16[160,2048]{1,0:T(8,128)(2,1)} collective-permute-done((bf16[160,2048]{1,0:T(8,128)(2,1)}, bf16[160,2048]{1,0:T(8,128)(2,1)}, u32[]{:S(2)}, u32[]{:S(2)}) %collective-permute-start.11) | collective-permute-done | bytes 655392 | tf_op jit(solution)/shard_map/ppermute | solution.py:54
  160.3 2.5 collective-permute-done.9.refs_1_
  162.8 2.5 collective-permute-start.3
  167.8 1.9 copy-done.5
  172.9 18.6 %layer_first.1 = (f32[8,512,256]{2,1,0:T(8,128)}, f32[1,2048]{1,0:T(1,128)S(1)}) custom-call(bf16[160,2048]{1,0:T(8,128)(2,1)S(1)} %copy-done, bf16[160,2048]{1,0:T(8,128)(2,1)} %collective-permute-done.9.refs_1_, bf16[160,2048]{1,0:T(8,128)(2,1)} %collective-permute-done.10.refs_2_, bf16[160,2048]{1,0:T(8,128)(2,1)} %collective-permute-done.11.refs_3_, ...), custom_call_target="tpu_custom_call" | custom-call | flops 10066329600 | bytes 12845056 | tf_op jit(solution)/shard_map/layer_first/pallas_call | solution.py:293
  192.7 12.6 %layer_last.1 = (f32[8,256,256]{2,1,0:T(8,128)S(1)}, bf16[8,256,256]{2,1,0:T(8,128)(2,1)}, f32[1,2048]{1,0:T(1,128)S(1)}) custom-call(bf16[160,2048]{1,0:T(8,128)(2,1)} %collective-permute-done.1.refs_0_, bf16[160,2048]{1,0:T(8,128)(2,1)} %collective-permute-done.2.refs_1_, bf16[160,2048]{1,0:T(8,128)(2,1)} %collective-permute-done.3.refs_2_, ...), custom_call_target="tpu_custom_call" | custom-call | flops 6039797760 | bytes 10223616 | tf_op jit(solution)/shard_map/layer_last/pallas_call | solution.py:293
  205.3 2.3 collective-permute-start.15
  208.1 17.3 %all_to_all.21 = f32[16,40,128]{2,1,0:T(8,128)S(1)} all-to-all(f32[16,40,128]{2,1,0:T(8,128)S(1)} %maximum_maximum_fusion), channel_id=1, replica_groups=mesh['index'=16,'reader'=8] {'index'}, dimensions={0} | all-to-all | bytes 655360 | tf_op jit(solution)/shard_map/all_to_all | solution.py:370
  228.1 4.6 %all-to-all-start.3 = ((bf16[8,264,256]{2,1,0:T(8,128)(2,1)}), bf16[8,264,256]{2,1,0:T(8,128)(2,1)S(1)}, u32[]{:S(2)}, u32[]{:S(2)}) async-start(bf16[8,264,256]{2,1,0:T(8,128)(2,1)} %pad_maximum_fusion), calls=%async_computation.3 | async-start | bytes 2162688 | tf_op jit(solution)/shard_map/all_to_all | solution.py:378
  233.3 14.8 %all-to-all-done.3 = bf16[8,264,256]{2,1,0:T(8,128)(2,1)S(1)} async-done(((bf16[8,264,256]{2,1,0:T(8,128)(2,1)}), bf16[8,264,256]{2,1,0:T(8,128)(2,1)S(1)}, u32[]{:S(2)}, u32[]{:S(2)}) %all-to-all-start.3) | async-done | bytes 1081376 | tf_op jit(solution)/shard_map/all_to_all | solution.py:378
  (86 shorter events, 27.9 us)
Async XLA Ops:
  7.2 158.2 %all-gather.2.cloned.1.call-start = ((), (), s32[]{:S(2)}) async-start(), calls=%async_computation.4 | async-start | bytes 3932160 | tf_op jit(solution)/shard_map/all_gather | solution.py:337
  9.4 13.1 %collective-permute-start.8 = (bf16[1536,256]{1,0:T(8,128)(2,1)S(1)}, bf16[1536,256]{1,0:T(8,128)(2,1)S(1)}, u32[]{:S(2)}, u32[]{:S(2)}) collective-permute-start(bf16[1536,256]{1,0:T(8,128)(2,1)S(1)} %pad_maximum_fusion.1), channel_id=1, source_target_pairs={{0,24},{1,97},{2,26},{3,99},{4,28},{5,101},{6,30},{7,103},{8,16},{... | collective-permute-start | bytes 2359304 | tf_op jit(solution)/shard_map/ppermute | solution.py:62
  90.9 36.0 %all-to-all-start.1 = ((bf16[48,8,2048]{2,1,0:T(8,128)(2,1)}), bf16[48,8,2048]{2,1,0:T(8,128)(2,1)}, u32[]{:S(2)}, u32[]{:S(2)}) async-start(bf16[48,8,2048]{2,1,0:T(8,128)(2,1)} %pick.1), calls=%async_computation.1 | async-start | bytes 3145728 | tf_op jit(solution)/shard_map/all_to_all | solution.py:346
  95.5 44.1 %copy-start.16 = (f32[32,128]{1,0:T(8,128)S(1)}, f32[32,128]{1,0:T(8,128)}, u32[]{:S(2)}) copy-start(f32[32,128]{1,0:T(8,128)} %param.17) | copy-start | bytes 49156
  95.7 30.0 %collective-permute-start.4 = (bf16[160,2048]{1,0:T(8,128)(2,1)S(1)}, bf16[160,2048]{1,0:T(8,128)(2,1)}, u32[]{:S(2)}, u32[]{:S(2)}) collective-permute-start(bf16[160,2048]{1,0:T(8,128)(2,1)S(1)} %fusion.refs_5_), channel_id=1, source_target_pairs={{0,8},{1,33},{2,10},{3,35},{4,12},{5,37},{6,14},{7,39},{8,0},{9,41... | collective-permute-start | bytes 1966088 | tf_op jit(solution)/shard_map/ppermute | solution.py:58
  97.0 34.0 %collective-permute-start.12 = (bf16[160,2048]{1,0:T(8,128)(2,1)S(1)}, bf16[160,2048]{1,0:T(8,128)(2,1)S(1)}, u32[]{:S(2)}, u32[]{:S(2)}) collective-permute-start(bf16[160,2048]{1,0:T(8,128)(2,1)S(1)} %fusion.refs_5_), channel_id=1, source_target_pairs={{0,32},{1,9},{2,34},{3,11},{4,36},{5,13},{6,38},{7,15},{8,40},{9,1... | collective-permute-start | bytes 1966088 | tf_op jit(solution)/shard_map/ppermute | solution.py:54
  98.2 35.4 %collective-permute-start.13 = (bf16[160,2048]{1,0:T(8,128)(2,1)S(1)}, bf16[160,2048]{1,0:T(8,128)(2,1)S(1)}, u32[]{:S(2)}, u32[]{:S(2)}) collective-permute-start(bf16[160,2048]{1,0:T(8,128)(2,1)S(1)} %fusion.refs_5_), channel_id=1, source_target_pairs={{0,96},{1,25},{2,98},{3,27},{4,100},{5,29},{6,102},{7,31},{8,104},... | collective-permute-start | bytes 1966088 | tf_op jit(solution)/shard_map/ppermute | solution.py:54
  99.7 38.1 %collective-permute-start.14 = (bf16[160,2048]{1,0:T(8,128)(2,1)S(1)}, bf16[160,2048]{1,0:T(8,128)(2,1)S(1)}, u32[]{:S(2)}, u32[]{:S(2)}) collective-permute-start(bf16[160,2048]{1,0:T(8,128)(2,1)S(1)} %fusion.refs_5_), channel_id=1, source_target_pairs={{0,64},{1,17},{2,66},{3,19},{4,68},{5,21},{6,70},{7,23},{8,72},{9,... | collective-permute-start | bytes 1966088 | tf_op jit(solution)/shard_map/ppermute | solution.py:54
  125.7 19.2 %collective-permute-start.5 = (bf16[160,2048]{1,0:T(8,128)(2,1)}, bf16[160,2048]{1,0:T(8,128)(2,1)S(1)}, u32[]{:S(2)}, u32[]{:S(2)}) collective-permute-start(bf16[160,2048]{1,0:T(8,128)(2,1)} %collective-permute-done.4.refs_9_), channel_id=1, source_target_pairs={{0,32},{1,9},{2,34},{3,11},{4,36},{5,13},{6,38},{7,15},{8,40},{9,1... | collective-permute-start | bytes 1966088 | tf_op jit(solution)/shard_map/ppermute | solution.py:54
  130.8 17.5 %collective-permute-start = (bf16[160,2048]{1,0:T(8,128)(2,1)}, bf16[160,2048]{1,0:T(8,128)(2,1)}, u32[]{:S(2)}, u32[]{:S(2)}) collective-permute-start(bf16[160,2048]{1,0:T(8,128)(2,1)} %norm.1.refs_0_), channel_id=1, source_target_pairs={{0,8},{1,33},{2,10},{3,35},{4,12},{5,37},{6,14},{7,39},{8,0},{9,41... | collective-permute-start | bytes 1966088 | tf_op jit(solution)/shard_map/ppermute | solution.py:58
  131.8 17.1 %collective-permute-start.10 = (bf16[160,2048]{1,0:T(8,128)(2,1)}, bf16[160,2048]{1,0:T(8,128)(2,1)}, u32[]{:S(2)}, u32[]{:S(2)}) collective-permute-start(bf16[160,2048]{1,0:T(8,128)(2,1)} %norm.1.refs_0_), channel_id=1, source_target_pairs={{0,96},{1,25},{2,98},{3,27},{4,100},{5,29},{6,102},{7,31},{8,104},... | collective-permute-start | bytes 1966088 | tf_op jit(solution)/shard_map/ppermute | solution.py:54
  134.4 24.5 %collective-permute-start.11 = (bf16[160,2048]{1,0:T(8,128)(2,1)}, bf16[160,2048]{1,0:T(8,128)(2,1)}, u32[]{:S(2)}, u32[]{:S(2)}) collective-permute-start(bf16[160,2048]{1,0:T(8,128)(2,1)} %norm.1.refs_0_), channel_id=1, source_target_pairs={{0,64},{1,17},{2,66},{3,19},{4,68},{5,21},{6,70},{7,23},{8,72},{9,... | collective-permute-start | bytes 1966088 | tf_op jit(solution)/shard_map/ppermute | solution.py:54
  138.6 24.1 %collective-permute-start.9 = (bf16[160,2048]{1,0:T(8,128)(2,1)}, bf16[160,2048]{1,0:T(8,128)(2,1)}, u32[]{:S(2)}, u32[]{:S(2)}) collective-permute-start(bf16[160,2048]{1,0:T(8,128)(2,1)} %norm.1.refs_0_), channel_id=1, source_target_pairs={{0,32},{1,9},{2,34},{3,11},{4,36},{5,13},{6,38},{7,15},{8,40},{9,1... | collective-permute-start | bytes 1966088 | tf_op jit(solution)/shard_map/ppermute | solution.py:54
  139.6 25.7 %copy-start = (bf16[160,2048]{1,0:T(8,128)(2,1)S(1)}, bf16[160,2048]{1,0:T(8,128)(2,1)}, u32[]{:S(2)}) copy-start(bf16[160,2048]{1,0:T(8,128)(2,1)} %norm.1.refs_0_) | copy-start | bytes 1966084
  139.6 25.7 %copy-start.1 = (bf16[256,2048]{1,0:T(8,128)(2,1)S(1)}, bf16[256,2048]{1,0:T(8,128)(2,1)}, u32[]{:S(2)}) copy-start(bf16[256,2048]{1,0:T(8,128)(2,1)} %refs_8_.1) | copy-start | bytes 3145732
  139.6 51.9 %copy-start.4 = (f32[2048]{0:T(1024)S(1)}, f32[2048]{0:T(1024)}, u32[]{:S(2)}) copy-start(f32[2048]{0:T(1024)} %param.23) | copy-start | bytes 24580
  145.0 46.5 %copy-start.6 = (bf16[160,2048]{1,0:T(8,128)(2,1)}, bf16[160,2048]{1,0:T(8,128)(2,1)S(1)}, u32[]{:S(2)}) copy-start(bf16[160,2048]{1,0:T(8,128)(2,1)S(1)} %collective-permute-done.5.refs_3_) | copy-start | bytes 1966084
  145.0 46.5 %collective-permute-start.6 = (bf16[160,2048]{1,0:T(8,128)(2,1)}, bf16[160,2048]{1,0:T(8,128)(2,1)}, u32[]{:S(2)}, u32[]{:S(2)}) collective-permute-start(bf16[160,2048]{1,0:T(8,128)(2,1)} %collective-permute-done.4.refs_9_), channel_id=1, source_target_pairs={{0,96},{1,25},{2,98},{3,27},{4,100},{5,29},{6,102},{7,31},{8,104},... | collective-permute-start | bytes 1966088 | tf_op jit(solution)/shard_map/ppermute | solution.py:54
  148.3 43.2 %collective-permute-start.7 = (bf16[160,2048]{1,0:T(8,128)(2,1)}, bf16[160,2048]{1,0:T(8,128)(2,1)}, u32[]{:S(2)}, u32[]{:S(2)}) collective-permute-start(bf16[160,2048]{1,0:T(8,128)(2,1)} %collective-permute-done.4.refs_9_), channel_id=1, source_target_pairs={{0,64},{1,17},{2,66},{3,19},{4,68},{5,21},{6,70},{7,23},{8,72},{9,... | collective-permute-start | bytes 1966088 | tf_op jit(solution)/shard_map/ppermute | solution.py:54
  149.0 42.6 %collective-permute-start.1 = (bf16[160,2048]{1,0:T(8,128)(2,1)}, bf16[160,2048]{1,0:T(8,128)(2,1)}, u32[]{:S(2)}, u32[]{:S(2)}) collective-permute-start(bf16[160,2048]{1,0:T(8,128)(2,1)} %collective-permute-done.refs_4_), channel_id=1, source_target_pairs={{0,32},{1,9},{2,34},{3,11},{4,36},{5,13},{6,38},{7,15},{8,40},{9,1... | collective-permute-start | bytes 1966088 | tf_op jit(solution)/shard_map/ppermute | solution.py:54
  158.9 32.6 %collective-permute-start.2 = (bf16[160,2048]{1,0:T(8,128)(2,1)}, bf16[160,2048]{1,0:T(8,128)(2,1)}, u32[]{:S(2)}, u32[]{:S(2)}) collective-permute-start(bf16[160,2048]{1,0:T(8,128)(2,1)} %collective-permute-done.refs_4_), channel_id=1, source_target_pairs={{0,96},{1,25},{2,98},{3,27},{4,100},{5,29},{6,102},{7,31},{8,104},... | collective-permute-start | bytes 1966088 | tf_op jit(solution)/shard_map/ppermute | solution.py:54
  162.8 28.8 %collective-permute-start.3 = (bf16[160,2048]{1,0:T(8,128)(2,1)}, bf16[160,2048]{1,0:T(8,128)(2,1)}, u32[]{:S(2)}, u32[]{:S(2)}) collective-permute-start(bf16[160,2048]{1,0:T(8,128)(2,1)} %collective-permute-done.refs_4_), channel_id=1, source_target_pairs={{0,64},{1,17},{2,66},{3,19},{4,68},{5,21},{6,70},{7,23},{8,72},{9,... | collective-permute-start | bytes 1966088 | tf_op jit(solution)/shard_map/ppermute | solution.py:54
  205.3 20.3 %collective-permute-start.15 = (bf16[8,256,256]{2,1,0:T(8,128)(2,1)}, bf16[8,256,256]{2,1,0:T(8,128)(2,1)}, u32[]{:S(2)}, u32[]{:S(2)}) collective-permute-start(bf16[8,256,256]{2,1,0:T(8,128)(2,1)} %get-tuple-element.16), channel_id=1, source_target_pairs={{0,24},{1,97},{2,26},{3,99},{4,28},{5,101},{6,30},{7,103},{8,16},{... | collective-permute-start | bytes 3145736 | tf_op jit(solution)/shard_map/ppermute | solution.py:62
  228.1 20.0 %all-to-all-start.3 = ((bf16[8,264,256]{2,1,0:T(8,128)(2,1)}), bf16[8,264,256]{2,1,0:T(8,128)(2,1)S(1)}, u32[]{:S(2)}, u32[]{:S(2)}) async-start(bf16[8,264,256]{2,1,0:T(8,128)(2,1)} %pad_maximum_fusion), calls=%async_computation.3 | async-start | bytes 2162688 | tf_op jit(solution)/shard_map/all_to_all | solution.py:378
  (14 other events, 36.2 us)
Sparse Core Ops, SparseCore 0:
  23.5 42.9 all-gather.1
where the time goes:
time: 257 us; the launch traced here: 256 us
  Pallas kernels  87.3 us (34%)
  waiting for transfers between devices  64.5 us (25%)
  starting transfers between devices  33.3 us (13%)
  blocking collectives  31.3 us (12%)
  local copies, waits for them, and re-layouts  15.7 us (6%)
  between operations  14.3 us (6%)
  other arithmetic  5.02 us (2%)
  matrix products  4.98 us (2%)
    pallas_call x1, Pallas kernels, pick_slots(): pl.pallas_call(pick_kernel, out_shape=jax.ShapeDtypeStruct((NI * CAP, LP,...  50 us
    pallas_call x2, Pallas kernels, layer(): pl.pallas_call(functools.partial(layer_kernel, blocks, tile, last), out_s...  31.2 us
    ppermute x2, waiting for transfers between devices, pair(): return lax.ppermute(v, BOTH, pairs_of(pair_move))  24.6 us
    all_to_all x1, blocking collectives, shards(): tail = lax.all_to_all(tail, 'index', 0, 0, tiled=True)  17.3 us
    ppermute x12, starting transfers between devices, ring(): return lax.ppermute(v, BOTH, pairs_of(ring_move(step)))  16.9 us
    ppermute x12, waiting for transfers between devices, ring(): return lax.ppermute(v, BOTH, pairs_of(ring_move(step)))  15.4 us
    all_to_all x1, waiting for transfers between devices, shards(): lax.all_to_all(jnp.concatenate([total, gain_rows], axis=1), 'reader', 0,...  14.8 us
    all_to_all x1, blocking collectives, shards(): asked = lax.all_to_all(msg, 'index', 0, 0, tiled=True)  14 us
  transfers between devices with their start and end apart: 19, of which 7 were waited for; matrix products, arithmetic and copies ran while one was open for 3% of the time, Pallas kernels for 29%

commit v1 on v0

--- a/solution.py
+++ b/solution.py
@@ -48,6 +48,19 @@
 
 def partner_move(x, z, c):
     return (x, 3 - z) if c == 0 else (3 - x, z)
+
+
+def column_pairs(step):
+    pairs = []
+    for i in range(NI):
+        for y in range(4):
+            for c in range(2):
+                pairs.append((i * 8 + y * 2 + c, i * 8 + (y + step) % 4 * 2 + c))
+    return pairs
+
+
+def column(v, step):
+    return lax.ppermute(v, BOTH, column_pairs(step))
 
 
 def ring(v, step):
@@ -101,7 +114,8 @@
     )(top, probes, home, emb8)
 
 
-def pick_kernel(slot_ref, states_ref, out_ref, sems):
+def pick_kernel(slot_ref, states_ref, *refs):
+    out_ref, sems = refs[(len(refs) - 2) // 2], refs[-1]
     copies = []
     for i in range(NI * CAP):
         row = slot_ref[i // CAP, i % CAP]
@@ -112,19 +126,26 @@
         copy.wait()
 
 
-def pick_slots(slots, states):
+def pick_slots(slots, states, *passed):
+    any_ = pl.BlockSpec(memory_space=pl.ANY)
     return pl.pallas_call(
         pick_kernel,
-        out_shape=jax.ShapeDtypeStruct((NI * CAP, LP, D), BF16),
-        in_specs=[pl.BlockSpec(memory_space=pltpu.SMEM), pl.BlockSpec(memory_space=pl.ANY)],
-        out_specs=pl.BlockSpec(memory_space=pl.ANY),
+        out_shape=(
+            jax.ShapeDtypeStruct((NI * CAP, LP, D), BF16),
+            *(jax.ShapeDtypeStruct(v.shape, v.dtype) for v in passed),
+        ),
+        in_specs=[pl.BlockSpec(memory_space=pltpu.SMEM), any_] + [any_] * len(passed),
+        out_specs=(pl.BlockSpec(memory_space=pltpu.VMEM), *(any_ for _ in passed)),
+        input_output_aliases={2 + i: 1 + i for i in range(len(passed))},
         scratch_shapes=[pltpu.SemaphoreType.DMA((NI * CAP,))],
+        compiler_params=pltpu.CompilerParams(vmem_limit_bytes=57 * 1024 * 1024),
         cost_estimate=pl.CostEstimate(flops=0, bytes_accessed=2 * NI * CAP * LP * D * 2, transcendentals=0),
         name="pick",
-    )(slots, states)
-
-
-def norm_kernel(src_ref, recv_ref, state_ref, gain_ref, out_ref, buf, sems):
+    )(slots, states, *passed)
+
+
+def norm_kernel(src_ref, recv_ref, state_ref, gain_ref, *refs):
+    out_ref, buf, sems = refs[-3:]
     copies = []
     for k in range(TOPK):
         copy = pltpu.make_async_copy(recv_ref.at[src_ref[0, k]], buf.at[k], sems.at[k])
@@ -140,7 +161,7 @@
         out_ref[2 * LP * k : 2 * LP * (k + 1), :] = (x * inv * gain).astype(BF16)
 
 
-def norm_rows(src, recv, state, gain):
+def norm_rows(src, recv, state, gain, *after):
     vmem = pl.BlockSpec(memory_space=pltpu.VMEM)
     return pl.pallas_call(
         norm_kernel,
@@ -150,21 +171,26 @@
             pl.BlockSpec(memory_space=pl.ANY),
             vmem,
             vmem,
+            *(pl.BlockSpec(memory_space=pl.ANY) for _ in after),
         ],
         out_specs=vmem,
         scratch_shapes=[pltpu.VMEM((TOPK, LP, D), BF16), pltpu.SemaphoreType.DMA((TOPK,))],
+        compiler_params=pltpu.CompilerParams(vmem_limit_bytes=8 * 1024 * 1024),
         name="norm",
-    )(src, recv, state, gain)
+    )(src, recv, state, gain, *after)
 
 
 NT = (((1,), (1,)), ((), ()))
 
 
 def layer_kernel(blocks, tile, last, *refs):
+    y = refs[0][0, 0]
+    refs = refs[1:]
     n_in = refs[:blocks]
     d_in = refs[blocks : 2 * blocks]
-    wg_in, wu_in, wo_in, wp_in = refs[2 * blocks : 2 * blocks + 4]
-    rest = refs[2 * blocks + 4 :]
+    wg_in, wu_in, wo_in = refs[2 * blocks : 2 * blocks + 3]
+    wp_in = refs[2 * blocks + 3 : 2 * blocks + 7]
+    rest = refs[2 * blocks + 7 :]
     if last:
         acc_in, gacc_ref, gain_ref, own_ref, par_ref, gout_ref = rest[:6]
         rest = rest[6:]
@@ -189,18 +215,17 @@
     first.append(start(wg_in, wg.at[:, pl.ds(0, FS)]))
     first.append(start(wu_in, wu.at[:, pl.ds(0, FS)]))
     for j in range(4):
-        first.append(start(wp_in.at[pl.ds(j * 1536, 512)], wg.at[pl.ds(j * 512, 512), pl.ds(FS, FS)]))
-        first.append(start(wp_in.at[pl.ds(j * 1536 + 512, 512)], wu.at[pl.ds(j * 512, 512), pl.ds(FS, FS)]))
+        part = pl.multiple_of((y + j) % 4 * 512, 512)
+        first.append(start(wp_in[j].at[pl.ds(0, 512)], wg.at[pl.ds(part, 512), pl.ds(FS, FS)]))
+        first.append(start(wp_in[j].at[pl.ds(512, 512)], wu.at[pl.ds(part, 512), pl.ds(FS, FS)]))
     for b in range(blocks):
         first.append(start(n_in[b], nbuf.at[pl.ds(b * ROWS, ROWS)]))
     second.append(start(wo_in, wo.at[pl.ds(0, FS)]))
     for j in range(4):
         for h in range(2):
+            part = pl.multiple_of((y + j) % 4 * 512 + h * FS, FS)
             second.append(
-                start(
-                    wp_in.at[pl.ds(j * 1536 + 1024 + h * FS, FS)],
-                    wo.at[pl.ds(FS, FS), pl.ds(j * 512 + h * FS, FS)],
-                )
+                start(wp_in[j].at[pl.ds(1024 + h * FS, FS)], wo.at[pl.ds(FS, FS), pl.ds(part, FS)])
             )
     for b in range(blocks):
         second.append(start(d_in[b], dbuf.at[pl.ds(b * ROWS, ROWS)]))
@@ -256,14 +281,14 @@
     lax.fori_loop(0, NR, out_body, 0)
 
 
-def layer(n_blocks, d_blocks, weights, tile, carried=None):
+def layer(y, n_blocks, d_blocks, weights, tile, carried=None):
     blocks = len(n_blocks)
     rows = blocks * ROWS
     last = carried is not None
     any_ = pl.BlockSpec(memory_space=pl.ANY)
     vmem = pl.BlockSpec(memory_space=pltpu.VMEM)
-    args = [*n_blocks, *d_blocks, *weights]
-    in_specs = [any_] * len(args)
+    args = [y, *n_blocks, *d_blocks, *weights]
+    in_specs = [pl.BlockSpec(memory_space=pltpu.SMEM)] + [any_] * (len(args) - 1)
     if last:
         args += list(carried)
         in_specs += [any_, vmem, vmem]
@@ -296,7 +321,7 @@
         in_specs=in_specs,
         out_specs=tuple(vmem for _ in out_shape),
         scratch_shapes=scratch,
-        compiler_params=pltpu.CompilerParams(vmem_limit_bytes=40 * 1024 * 1024),
+        compiler_params=pltpu.CompilerParams(vmem_limit_bytes=60 * 1024 * 1024),
         cost_estimate=pl.CostEstimate(
             flops=12 * rows * D * 2 * FS, bytes_accessed=4 * rows * D + 6 * D * 2 * FS, transcendentals=rows * 512
         ),
@@ -322,8 +347,10 @@
 ):
     dy0 = (soft_weight[:, :, None, None] * cotangent.astype(F32)).astype(BF16).reshape(ROWS, D)
     dyp = pair(dy0)
-    dy_a = [dy0, ring(dy0, 1), ring(dy0, -1), ring(dy0, 2), dyp]
+    dy_next = ring(dy0, 1)
+    dy_prev = ring(dy0, -1)
     y = lax.axis_index("reader") // 2
+    y_row = y.astype(I32).reshape(1, 1)
     piece = jnp.concatenate(
         [
             lax.dynamic_slice(w_gate, (y * 512, 0), (512, FS)),
@@ -334,20 +361,20 @@
         axis=0,
     )
     piece = partner(piece)
-    wp = lax.all_gather(
-        piece, "reader", axis=0, tiled=True, axis_index_groups=[[0, 2, 4, 6], [1, 3, 5, 7]]
-    )
-    weights = (w_gate, w_up, w_out, wp)
 
     msg, src = make_plan(top_passages, probes, passage_home, question_emb)
     asked = lax.all_to_all(msg, "index", 0, 0, tiled=True)
     slots = asked[:, 6, :CAP].astype(I32)
-    blocks = pick_slots(slots, passage_states)
+    blocks, piece, dyp, dy_next, dy_prev = pick_slots(
+        slots, passage_states, piece, dyp, dy_next, dy_prev
+    )
     recv = lax.all_to_all(blocks, "index", 0, 0, tiled=True)
+    dy_far = ring(dy0, 2)
+    dy_a = [dy0, dy_next, dy_prev, dy_far, dyp]
+    dy_b = [ring(dyp, 1), ring(dyp, -1), ring(dyp, 2)]
+    weights = (w_gate, w_up, w_out, piece, column(piece, -1), column(piece, 2), column(piece, 1))
     gain_row = norm_gain.reshape(1, D)
-    n0 = norm_rows(src, recv, question_state, gain_row)
-
-    dy_b = [ring(dyp, 1), ring(dyp, -1), ring(dyp, 2)]
+    n0 = norm_rows(src, recv, question_state, gain_row, dy_far, *dy_b)
     np_ = pair(n0)
     n_a = [n0, ring(n0, 1), ring(n0, -1), ring(n0, 2), np_]
     n_b = [ring(np_, 1), ring(np_, -1), ring(np_, 2)]
@@ -360,8 +387,8 @@
     hot = (local[:, :, None] == jnp.arange(CLUS_DEV, dtype=I32)[None, None, :]).astype(F32)
     picked = jnp.einsum("qpc,qcs->qps", hot, every_score, precision=lax.Precision.HIGHEST)
 
-    acc_a, gain_a = layer(n_a, dy_a, weights, 400)
-    own, par, gain_part = layer(n_b, dy_b, weights, 240, (acc_a, gain_a, gain_row))
+    acc_a, gain_a = layer(y_row, n_a, dy_a, weights, 400)
+    own, par, gain_part = layer(y_row, n_b, dy_b, weights, 240, (acc_a, gain_a, gain_row))
 
     from_partner = partner(par)
     tail = jnp.concatenate(

time: 257 us -> 193 us (0.75)
  Pallas kernels: 87.3 us -> 45.9 us
  between operations: 14.3 us -> 0.99 us
  waiting for transfers between devices: 64.5 us -> 58 us
  local copies, waits for them, and re-layouts: 15.7 us -> 9.21 us
  starting transfers between devices: 33.3 us -> 37.7 us
    pallas_call x1, Pallas kernels: 50 us -> 3.78 us  [pick_slots(): pl.pallas_call(pick_kernel, out_shape=(jax.ShapeDtypeStruct((NI * CAP, LP...]
    ppermute x12, waiting for transfers between devices: 15.4 us -> 40.6 us  [ring(): return lax.ppermute(v, BOTH, pairs_of(ring_move(step)))]
    ppermute x2, waiting for transfers between devices: 24.6 us -> 2.53 us  [pair(): return lax.ppermute(v, BOTH, pairs_of(pair_move))]
    ppermute x2, waiting for transfers between devices: 9.68 us -> 0.01 us  [partner(): return lax.ppermute(v, BOTH, pairs_of(partner_move))]
    unnamed x38 -> x40, local copies, waits for them, and re-layouts: 12.1 us -> 4.77 us
    pallas_call x2, Pallas kernels: 31.2 us -> 36.1 us  [layer(): pl.pallas_call(functools.partial(layer_kernel, blocks, tile, last), out_s...]
    ppermute x0 -> x3, starting transfers between devices: none -> 4.38 us  [column(): return lax.ppermute(v, BOTH, column_pairs(step))]
  transfers between devices with their start and end apart: 19 -> 21, of which waited for: 7 -> 7; matrix products, arithmetic and copies ran while one was open for 3% -> 5% of each run, Pallas kernels for 29% -> 14%
where the time goes in v1:
time: 193 us; the launch traced here: 192 us
  waiting for transfers between devices  58 us (30%)
  Pallas kernels  45.9 us (24%)
  starting transfers between devices  37.7 us (20%)
  blocking collectives  30.6 us (16%)
  local copies, waits for them, and re-layouts  9.21 us (5%)
  other arithmetic  5.26 us (3%)
  matrix products  4.86 us (3%)
    ppermute x12, waiting for transfers between devices, ring(): return lax.ppermute(v, BOTH, pairs_of(ring_move(step)))  40.6 us
    pallas_call x2, Pallas kernels, layer(): pl.pallas_call(functools.partial(layer_kernel, blocks, tile, last), out_s...  36.1 us
    all_to_all x1, blocking collectives, shards(): tail = lax.all_to_all(tail, 'index', 0, 0, tiled=True)  17.5 us
    ppermute x12, starting transfers between devices, ring(): return lax.ppermute(v, BOTH, pairs_of(ring_move(step)))  17.5 us
    all_to_all x1, waiting for transfers between devices, shards(): lax.all_to_all(jnp.concatenate([total, gain_rows], axis=1), 'reader', 0,...  14.8 us
    all_to_all x1, blocking collectives, shards(): asked = lax.all_to_all(msg, 'index', 0, 0, tiled=True)  13 us
    all_to_all x1, starting transfers between devices, shards(): recv = lax.all_to_all(blocks, 'index', 0, 0, tiled=True)  5.9 us
    unnamed x40, local copies, waits for them, and re-layouts  4.77 us
  transfers between devices with their start and end apart: 21, of which 7 were waited for; matrix products, arithmetic and copies ran while one was open for 5% of the time, Pallas kernels for 14%

profile of v1, /device:TPU:1, one launch (start us, length us, event | category | flops | bytes accessed | tf_op | source)
XLA Modules:
  0.0 192.4 jit_solution(13527419351184718123)
XLA Ops:
  2.9 3.4 %collective-permute-start = (bf16[1536,256]{1,0:T(8,128)(2,1)S(1)}, bf16[1536,256]{1,0:T(8,128)(2,1)}, u32[]{:S(2)}, u32[]{:S(2)}) collective-permute-start(bf16[1536,256]{1,0:T(8,128)(2,1)S(1)} %pad_maximum_fusion.1), channel_id=1, source_target_pairs={{0,24},{1,97},{2,26},{3,99},{4,28},{5,101},{6,30},{7,103},{8,16},{... | collective-permute-start | bytes 2359304 | tf_op jit(solution)/shard_map/ppermute | solution.py:75
  6.6 1.7 collective-permute-start.2
  8.3 2.2 %collective-permute-start.3 = (bf16[160,2048]{1,0:T(8,128)(2,1)S(1)}, bf16[160,2048]{1,0:T(8,128)(2,1)S(1)}, u32[]{:S(2)}, u32[]{:S(2)}) collective-permute-start(bf16[160,2048]{1,0:T(8,128)(2,1)S(1)} %fusion.refs_6_), channel_id=1, source_target_pairs={{0,96},{1,25},{2,98},{3,27},{4,100},{5,29},{6,102},{7,31},{8,104},... | collective-permute-start | bytes 1966088 | tf_op jit(solution)/shard_map/ppermute | solution.py:67
  11.1 2.3 %plan.1 = (bf16[16,8,128]{2,1,0:T(8,128)(2,1)}, s32[1,20]{1,0:T(1,128)}) custom-call(s32[1,20]{1,0:T(1,128)} %top_ref.1, s32[1,32]{1,0:T(1,128)} %probes_ref.1, s32[4096]{0:T(1024)} %home_ref.1, f32[8,128]{1,0:T(8,128)} %pad_convert_fusion.emb_ref), custom_call_target="tpu_custom_call" | custom-call | tf_op jit(solution)/shard_map/plan/pallas_call | solution.py:105
  13.4 13.0 %all_to_all.20 = bf16[16,8,128]{2,1,0:T(8,128)(2,1)S(1)} all-to-all(bf16[16,8,128]{2,1,0:T(8,128)(2,1)} %get-tuple-element.15), channel_id=1, replica_groups=mesh['index'=16,'reader'=8] {'index'}, dimensions={0} | all-to-all | bytes 65536 | tf_op jit(solution)/shard_map/all_to_all | solution.py:366
  28.2 3.8 %pick.1 = (bf16[48,8,2048]{2,1,0:T(8,128)(2,1)}, bf16[1536,256]{1,0:T(8,128)(2,1)}, bf16[160,2048]{1,0:T(8,128)(2,1)}, bf16[160,2048]{1,0:T(8,128)(2,1)}, bf16[160,2048]{1,0:T(8,128)(2,1)}) custom-call(s32[16,3]{1,0:T(8,128)} %bitcast.26, bf16[256,8,2048]{2,1,0:T(8,128)(2,1)} %states_ref.1, ...), custom_call_target="tpu_custom_call", output_to_operand_aliasing={{1}: (2, {}), {2}: (3, {}), {3}: (4, {}), {4}: (5, {})} | custom-call | bytes 3145728 | tf_op jit(solution)/shard_map/pick/pallas_call | solution.py:131
  32.0 5.9 %all-to-all-start.1 = ((bf16[48,8,2048]{2,1,0:T(8,128)(2,1)}), bf16[48,8,2048]{2,1,0:T(8,128)(2,1)S(1)}, u32[]{:S(2)}, u32[]{:S(2)}) async-start(bf16[48,8,2048]{2,1,0:T(8,128)(2,1)} %get-tuple-element.17), calls=%async_computation.1 | async-start | bytes 3145728 | tf_op jit(solution)/shard_map/all_to_all | solution.py:371
  37.9 2.9 %collective-permute-start.4 = (bf16[160,2048]{1,0:T(8,128)(2,1)S(1)}, bf16[160,2048]{1,0:T(8,128)(2,1)S(1)}, u32[]{:S(2)}, u32[]{:S(2)}) collective-permute-start(bf16[160,2048]{1,0:T(8,128)(2,1)S(1)} %fusion.refs_6_), channel_id=1, source_target_pairs={{0,64},{1,17},{2,66},{3,19},{4,68},{5,21},{6,70},{7,23},{8,72},{9,... | collective-permute-start | bytes 1966088 | tf_op jit(solution)/shard_map/ppermute | solution.py:67
  41.1 2.7 %collective-permute-start.12 = (bf16[1536,256]{1,0:T(8,128)(2,1)}, bf16[1536,256]{1,0:T(8,128)(2,1)}, u32[]{:S(2)}, u32[]{:S(2)}) collective-permute-start(bf16[1536,256]{1,0:T(8,128)(2,1)} %get-tuple-element.19.refs_14_.refs_10_), channel_id=1, source_target_pairs={{0,6},{1,7},{2,0},{3,1},{4,2},{5,3},{6,4},{7,5},{8,14},{9,15},{10,... | collective-permute-start | bytes 2359304 | tf_op jit(solution)/shard_map/ppermute | solution.py:63
  44.2 2.4 %collective-permute-start.6 = (bf16[160,2048]{1,0:T(8,128)(2,1)}, bf16[160,2048]{1,0:T(8,128)(2,1)S(1)}, u32[]{:S(2)}, u32[]{:S(2)}) collective-permute-start(bf16[160,2048]{1,0:T(8,128)(2,1)} %get-tuple-element.18.refs_10_), channel_id=1, source_target_pairs={{0,96},{1,25},{2,98},{3,27},{4,100},{5,29},{6,102},{7,31},{8,104},... | collective-permute-start | bytes 1966088 | tf_op jit(solution)/shard_map/ppermute | solution.py:67
  46.6 20.2 %collective-permute-done.4.refs_0_.refs_9_ = bf16[160,2048]{1,0:T(8,128)(2,1)S(1)} collective-permute-done((bf16[160,2048]{1,0:T(8,128)(2,1)S(1)}, bf16[160,2048]{1,0:T(8,128)(2,1)S(1)}, u32[]{:S(2)}, u32[]{:S(2)}) %collective-permute-start.4) | collective-permute-done | bytes 655392 | tf_op jit(solution)/shard_map/ppermute | solution.py:67
  68.7 4.2 %collective-permute-done.5.refs_1_.refs_4_ = bf16[160,2048]{1,0:T(8,128)(2,1)S(1)} collective-permute-done((bf16[160,2048]{1,0:T(8,128)(2,1)}, bf16[160,2048]{1,0:T(8,128)(2,1)S(1)}, u32[]{:S(2)}, u32[]{:S(2)}) %collective-permute-start.5) | collective-permute-done | bytes 655392 | tf_op jit(solution)/shard_map/ppermute | solution.py:67
  74.3 6.5 %collective-permute-done.7.refs_3_.refs_6_ = bf16[160,2048]{1,0:T(8,128)(2,1)S(1)} collective-permute-done((bf16[160,2048]{1,0:T(8,128)(2,1)}, bf16[160,2048]{1,0:T(8,128)(2,1)S(1)}, u32[]{:S(2)}, u32[]{:S(2)}) %collective-permute-start.7) | collective-permute-done | bytes 655392 | tf_op jit(solution)/shard_map/ppermute | solution.py:67
  82.8 3.7 %norm.1.refs_1_ = bf16[160,2048]{1,0:T(8,128)(2,1)} custom-call(s32[1,20]{1,0:T(1,128)S(1)} %copy-done.7, bf16[48,8,2048]{2,1,0:T(8,128)(2,1)S(1)} %all-to-all-done.1.recv_ref, bf16[1,2048]{1,0:T(2,128)(2,1)S(1)} %copy-done.5, f32[1,2048]{1,0:T(1,128)S(1)} %bitcast.21, bf16[160,2048]{1,0:T(8,128)(2,1)S(1)} %copy-done.4, ...), custom_call_target="tpu_custom_call" | custom-call | tf_op jit(solution)/shard_map/norm/pallas_call | solution.py:166
  88.1 1.9 %collective-permute-start.16 = (bf16[160,2048]{1,0:T(8,128)(2,1)}, bf16[160,2048]{1,0:T(8,128)(2,1)S(1)}, u32[]{:S(2)}, u32[]{:S(2)}) collective-permute-start(bf16[160,2048]{1,0:T(8,128)(2,1)} %norm.1.refs_1_), channel_id=1, source_target_pairs={{0,96},{1,25},{2,98},{3,27},{4,100},{5,29},{6,102},{7,31},{8,104},... | collective-permute-start | bytes 1966088 | tf_op jit(solution)/shard_map/ppermute | solution.py:67
  92.6 4.5 %convolution_multiply_fusion = f32[16,32,128]{2,0,1:T(8,128)S(1)} fusion(bf16[16,768,1]{1,0,2:T(8,128)(2,1)S(1)} %reshape.83, bf16[32,128,768]{2,1,0:T(8,128)(2,1)} %param.16, f32[32,128]{1,0:T(8,128)} %param.17), kind=kOutput, calls=%fused_computation.3 | convolution fusion | flops 100728832 | bytes 6594560 | tf_op jit(solution)/shard_map/qe,cse->qcs/dot_general | solution.py:384
  97.2 2.5 %collective-permute-done.8.refs_5_ = bf16[160,2048]{1,0:T(8,128)(2,1)S(1)} collective-permute-done((bf16[160,2048]{1,0:T(8,128)(2,1)}, bf16[160,2048]{1,0:T(8,128)(2,1)S(1)}, u32[]{:S(2)}, u32[]{:S(2)}) %collective-permute-start.8) | collective-permute-done | bytes 655392 | tf_op jit(solution)/shard_map/ppermute | solution.py:71
  99.7 1.9 collective-permute-start.10
  104.2 8.6 %collective-permute-done.17.refs_4_ = bf16[160,2048]{1,0:T(8,128)(2,1)} collective-permute-done((bf16[160,2048]{1,0:T(8,128)(2,1)}, bf16[160,2048]{1,0:T(8,128)(2,1)}, u32[]{:S(2)}, u32[]{:S(2)}) %collective-permute-start.17) | collective-permute-done | bytes 655392 | tf_op jit(solution)/shard_map/ppermute | solution.py:67
  112.7 20.6 %layer_first.1 = (f32[8,512,256]{2,1,0:T(8,128)}, f32[1,2048]{1,0:T(1,128)}) custom-call(s32[1,1]{1,0:T(1,128)} %bitcast.1.refs_0_, bf16[160,2048]{1,0:T(8,128)(2,1)} %norm.1.refs_1_, bf16[160,2048]{1,0:T(8,128)(2,1)} %copy-done.17, bf16[160,2048]{1,0:T(8,128)(2,1)} %copy-done.19, bf16[160,2048]{1,0:T(8,128)(2,1)} %collective-permute-done.17.refs_4_, ...), custom_call_target="tpu_custom_call" | custom-call | flops 10066329600 | bytes 12845056 | tf_op jit(solution)/shard_map/layer_first/pallas_call | solution.py:318
  134.2 15.5 %layer_last.1 = (f32[8,256,256]{2,1,0:T(8,128)}, bf16[8,256,256]{2,1,0:T(8,128)(2,1)}, f32[1,2048]{1,0:T(1,128)}) custom-call(s32[1,1]{1,0:T(1,128)} %bitcast.1.refs_0_, bf16[160,2048]{1,0:T(8,128)(2,1)} %collective-permute-done.9.refs_1_, bf16[160,2048]{1,0:T(8,128)(2,1)} %copy-done.18, bf16[160,2048]{1,0:T(8,128)(2,1)} %collective-permute-done.11.refs_3_, ...), custom_call_target="tpu_custom_call" | custom-call | flops 6039797760 | bytes 10223616 | tf_op jit(solution)/shard_map/layer_last/pallas_call | solution.py:318
  152.0 17.5 %all_to_all.21 = f32[16,40,128]{2,1,0:T(8,128)S(1)} all-to-all(f32[16,40,128]{2,1,0:T(8,128)S(1)} %maximum_maximum_fusion), channel_id=1, replica_groups=mesh['index'=16,'reader'=8] {'index'}, dimensions={0} | all-to-all | bytes 655360 | tf_op jit(solution)/shard_map/all_to_all | solution.py:397
  171.1 4.5 %all-to-all-start.3 = ((bf16[8,264,256]{2,1,0:T(8,128)(2,1)}), bf16[8,264,256]{2,1,0:T(8,128)(2,1)S(1)}, u32[]{:S(2)}, u32[]{:S(2)}) async-start(bf16[8,264,256]{2,1,0:T(8,128)(2,1)} %pad_maximum_fusion), calls=%async_computation.3 | async-start | bytes 2162688 | tf_op jit(solution)/shard_map/all_to_all | solution.py:405
  176.2 14.8 %all-to-all-done.3 = bf16[8,264,256]{2,1,0:T(8,128)(2,1)S(1)} async-done(((bf16[8,264,256]{2,1,0:T(8,128)(2,1)}), bf16[8,264,256]{2,1,0:T(8,128)(2,1)S(1)}, u32[]{:S(2)}, u32[]{:S(2)}) %all-to-all-start.3) | async-done | bytes 1081376 | tf_op jit(solution)/shard_map/all_to_all | solution.py:405
  (91 shorter events, 24.1 us)
Async XLA Ops:
  2.9 24.2 %collective-permute-start = (bf16[1536,256]{1,0:T(8,128)(2,1)S(1)}, bf16[1536,256]{1,0:T(8,128)(2,1)}, u32[]{:S(2)}, u32[]{:S(2)}) collective-permute-start(bf16[1536,256]{1,0:T(8,128)(2,1)S(1)} %pad_maximum_fusion.1), channel_id=1, source_target_pairs={{0,24},{1,97},{2,26},{3,99},{4,28},{5,101},{6,30},{7,103},{8,16},{... | collective-permute-start | bytes 2359304 | tf_op jit(solution)/shard_map/ppermute | solution.py:75
  6.5 31.4 %copy-start.12 = (bf16[160,2048]{1,0:T(8,128)(2,1)}, bf16[160,2048]{1,0:T(8,128)(2,1)S(1)}, u32[]{:S(2)}) copy-start(bf16[160,2048]{1,0:T(8,128)(2,1)S(1)} %fusion.refs_6_) | copy-start | bytes 1966084
  6.5 20.6 %collective-permute-start.1 = (bf16[160,2048]{1,0:T(8,128)(2,1)S(1)}, bf16[160,2048]{1,0:T(8,128)(2,1)}, u32[]{:S(2)}, u32[]{:S(2)}) collective-permute-start(bf16[160,2048]{1,0:T(8,128)(2,1)S(1)} %fusion.refs_6_), channel_id=1, source_target_pairs={{0,8},{1,33},{2,10},{3,35},{4,12},{5,37},{6,14},{7,39},{8,0},{9,41... | collective-permute-start | bytes 1966088 | tf_op jit(solution)/shard_map/ppermute | solution.py:71
  6.6 20.5 %collective-permute-start.2 = (bf16[160,2048]{1,0:T(8,128)(2,1)S(1)}, bf16[160,2048]{1,0:T(8,128)(2,1)S(1)}, u32[]{:S(2)}, u32[]{:S(2)}) collective-permute-start(bf16[160,2048]{1,0:T(8,128)(2,1)S(1)} %fusion.refs_6_), channel_id=1, source_target_pairs={{0,32},{1,9},{2,34},{3,11},{4,36},{5,13},{6,38},{7,15},{8,40},{9,1... | collective-permute-start | bytes 1966088 | tf_op jit(solution)/shard_map/ppermute | solution.py:67
  8.3 18.8 %collective-permute-start.3 = (bf16[160,2048]{1,0:T(8,128)(2,1)S(1)}, bf16[160,2048]{1,0:T(8,128)(2,1)S(1)}, u32[]{:S(2)}, u32[]{:S(2)}) collective-permute-start(bf16[160,2048]{1,0:T(8,128)(2,1)S(1)} %fusion.refs_6_), channel_id=1, source_target_pairs={{0,96},{1,25},{2,98},{3,27},{4,100},{5,29},{6,102},{7,31},{8,104},... | collective-permute-start | bytes 1966088 | tf_op jit(solution)/shard_map/ppermute | solution.py:67
  32.0 48.8 %copy-start.5 = (bf16[1,2048]{1,0:T(2,128)(2,1)S(1)}, bf16[1,2048]{1,0:T(2,128)(2,1)}, u32[]{:S(2)}) copy-start(bf16[1,2048]{1,0:T(2,128)(2,1)} %state_ref.1) | copy-start | bytes 12292
  32.0 48.8 %copy-start.6 = (f32[2048]{0:T(1024)S(1)}, f32[2048]{0:T(1024)}, u32[]{:S(2)}) copy-start(f32[2048]{0:T(1024)} %param.23) | copy-start | bytes 24580
  32.0 48.8 %all-to-all-start.1 = ((bf16[48,8,2048]{2,1,0:T(8,128)(2,1)}), bf16[48,8,2048]{2,1,0:T(8,128)(2,1)S(1)}, u32[]{:S(2)}, u32[]{:S(2)}) async-start(bf16[48,8,2048]{2,1,0:T(8,128)(2,1)} %get-tuple-element.17), calls=%async_computation.1 | async-start | bytes 3145728 | tf_op jit(solution)/shard_map/all_to_all | solution.py:371
  37.9 28.9 %collective-permute-start.4 = (bf16[160,2048]{1,0:T(8,128)(2,1)S(1)}, bf16[160,2048]{1,0:T(8,128)(2,1)S(1)}, u32[]{:S(2)}, u32[]{:S(2)}) collective-permute-start(bf16[160,2048]{1,0:T(8,128)(2,1)S(1)} %fusion.refs_6_), channel_id=1, source_target_pairs={{0,64},{1,17},{2,66},{3,19},{4,68},{5,21},{6,70},{7,23},{8,72},{9,... | collective-permute-start | bytes 1966088 | tf_op jit(solution)/shard_map/ppermute | solution.py:67
  40.9 32.1 %collective-permute-start.5 = (bf16[160,2048]{1,0:T(8,128)(2,1)}, bf16[160,2048]{1,0:T(8,128)(2,1)S(1)}, u32[]{:S(2)}, u32[]{:S(2)}) collective-permute-start(bf16[160,2048]{1,0:T(8,128)(2,1)} %get-tuple-element.18.refs_10_), channel_id=1, source_target_pairs={{0,32},{1,9},{2,34},{3,11},{4,36},{5,13},{6,38},{7,15},{8,40},{9,1... | collective-permute-start | bytes 1966088 | tf_op jit(solution)/shard_map/ppermute | solution.py:67
  41.1 46.9 %collective-permute-start.12 = (bf16[1536,256]{1,0:T(8,128)(2,1)}, bf16[1536,256]{1,0:T(8,128)(2,1)}, u32[]{:S(2)}, u32[]{:S(2)}) collective-permute-start(bf16[1536,256]{1,0:T(8,128)(2,1)} %get-tuple-element.19.refs_14_.refs_10_), channel_id=1, source_target_pairs={{0,6},{1,7},{2,0},{3,1},{4,2},{5,3},{6,4},{7,5},{8,14},{9,15},{10,... | collective-permute-start | bytes 2359304 | tf_op jit(solution)/shard_map/ppermute | solution.py:63
  43.9 46.1 %collective-permute-start.13 = (bf16[1536,256]{1,0:T(8,128)(2,1)}, bf16[1536,256]{1,0:T(8,128)(2,1)}, u32[]{:S(2)}, u32[]{:S(2)}) collective-permute-start(bf16[1536,256]{1,0:T(8,128)(2,1)} %get-tuple-element.19.refs_14_.refs_10_), channel_id=1, source_target_pairs={{0,4},{1,5},{2,6},{3,7},{4,0},{5,1},{6,2},{7,3},{8,12},{9,13},{10,... | collective-permute-start | bytes 2359304 | tf_op jit(solution)/shard_map/ppermute | solution.py:63
  44.2 30.1 %collective-permute-start.6 = (bf16[160,2048]{1,0:T(8,128)(2,1)}, bf16[160,2048]{1,0:T(8,128)(2,1)S(1)}, u32[]{:S(2)}, u32[]{:S(2)}) collective-permute-start(bf16[160,2048]{1,0:T(8,128)(2,1)} %get-tuple-element.18.refs_10_), channel_id=1, source_target_pairs={{0,96},{1,25},{2,98},{3,27},{4,100},{5,29},{6,102},{7,31},{8,104},... | collective-permute-start | bytes 1966088 | tf_op jit(solution)/shard_map/ppermute | solution.py:67
  67.6 13.1 %collective-permute-start.7 = (bf16[160,2048]{1,0:T(8,128)(2,1)}, bf16[160,2048]{1,0:T(8,128)(2,1)S(1)}, u32[]{:S(2)}, u32[]{:S(2)}) collective-permute-start(bf16[160,2048]{1,0:T(8,128)(2,1)} %get-tuple-element.18.refs_10_), channel_id=1, source_target_pairs={{0,64},{1,17},{2,66},{3,19},{4,68},{5,21},{6,70},{7,23},{8,72},{9,... | collective-permute-start | bytes 1966088 | tf_op jit(solution)/shard_map/ppermute | solution.py:67
  73.0 28.6 %collective-permute-start.14 = (bf16[1536,256]{1,0:T(8,128)(2,1)}, bf16[1536,256]{1,0:T(8,128)(2,1)}, u32[]{:S(2)}, u32[]{:S(2)}) collective-permute-start(bf16[1536,256]{1,0:T(8,128)(2,1)} %get-tuple-element.19.refs_14_.refs_10_), channel_id=1, source_target_pairs={{0,2},{1,3},{2,4},{3,5},{4,6},{5,7},{6,0},{7,1},{8,10},{9,11},{10,... | collective-permute-start | bytes 2359304 | tf_op jit(solution)/shard_map/ppermute | solution.py:63
  86.5 13.1 %collective-permute-start.8 = (bf16[160,2048]{1,0:T(8,128)(2,1)}, bf16[160,2048]{1,0:T(8,128)(2,1)S(1)}, u32[]{:S(2)}, u32[]{:S(2)}) collective-permute-start(bf16[160,2048]{1,0:T(8,128)(2,1)} %norm.1.refs_1_), channel_id=1, source_target_pairs={{0,8},{1,33},{2,10},{3,35},{4,12},{5,37},{6,14},{7,39},{8,0},{9,41... | collective-permute-start | bytes 1966088 | tf_op jit(solution)/shard_map/ppermute | solution.py:71
  87.3 15.2 %collective-permute-start.15 = (bf16[160,2048]{1,0:T(8,128)(2,1)}, bf16[160,2048]{1,0:T(8,128)(2,1)S(1)}, u32[]{:S(2)}, u32[]{:S(2)}) collective-permute-start(bf16[160,2048]{1,0:T(8,128)(2,1)} %norm.1.refs_1_), channel_id=1, source_target_pairs={{0,32},{1,9},{2,34},{3,11},{4,36},{5,13},{6,38},{7,15},{8,40},{9,1... | collective-permute-start | bytes 1966088 | tf_op jit(solution)/shard_map/ppermute | solution.py:67
  88.1 16.1 %collective-permute-start.16 = (bf16[160,2048]{1,0:T(8,128)(2,1)}, bf16[160,2048]{1,0:T(8,128)(2,1)S(1)}, u32[]{:S(2)}, u32[]{:S(2)}) collective-permute-start(bf16[160,2048]{1,0:T(8,128)(2,1)} %norm.1.refs_1_), channel_id=1, source_target_pairs={{0,96},{1,25},{2,98},{3,27},{4,100},{5,29},{6,102},{7,31},{8,104},... | collective-permute-start | bytes 1966088 | tf_op jit(solution)/shard_map/ppermute | solution.py:67
  90.0 22.7 %collective-permute-start.17 = (bf16[160,2048]{1,0:T(8,128)(2,1)}, bf16[160,2048]{1,0:T(8,128)(2,1)}, u32[]{:S(2)}, u32[]{:S(2)}) collective-permute-start(bf16[160,2048]{1,0:T(8,128)(2,1)} %norm.1.refs_1_), channel_id=1, source_target_pairs={{0,64},{1,17},{2,66},{3,19},{4,68},{5,21},{6,70},{7,23},{8,72},{9,... | collective-permute-start | bytes 1966088 | tf_op jit(solution)/shard_map/ppermute | solution.py:67
  99.7 33.6 %collective-permute-start.10 = (bf16[160,2048]{1,0:T(8,128)(2,1)S(1)}, bf16[160,2048]{1,0:T(8,128)(2,1)S(1)}, u32[]{:S(2)}, u32[]{:S(2)}) collective-permute-start(bf16[160,2048]{1,0:T(8,128)(2,1)S(1)} %collective-permute-done.8.refs_5_), channel_id=1, source_target_pairs={{0,96},{1,25},{2,98},{3,27},{4,100},{5,29},{6,102},{7,31},{8,104},... | collective-permute-start | bytes 1966088 | tf_op jit(solution)/shard_map/ppermute | solution.py:67
  101.6 31.7 %collective-permute-start.11 = (bf16[160,2048]{1,0:T(8,128)(2,1)S(1)}, bf16[160,2048]{1,0:T(8,128)(2,1)}, u32[]{:S(2)}, u32[]{:S(2)}) collective-permute-start(bf16[160,2048]{1,0:T(8,128)(2,1)S(1)} %collective-permute-done.8.refs_5_), channel_id=1, source_target_pairs={{0,64},{1,17},{2,66},{3,19},{4,68},{5,21},{6,70},{7,23},{8,72},{9,... | collective-permute-start | bytes 1966088 | tf_op jit(solution)/shard_map/ppermute | solution.py:67
  102.5 30.8 %collective-permute-start.9 = (bf16[160,2048]{1,0:T(8,128)(2,1)S(1)}, bf16[160,2048]{1,0:T(8,128)(2,1)}, u32[]{:S(2)}, u32[]{:S(2)}) collective-permute-start(bf16[160,2048]{1,0:T(8,128)(2,1)S(1)} %collective-permute-done.8.refs_5_), channel_id=1, source_target_pairs={{0,32},{1,9},{2,34},{3,11},{4,36},{5,13},{6,38},{7,15},{8,40},{9,1... | collective-permute-start | bytes 1966088 | tf_op jit(solution)/shard_map/ppermute | solution.py:67
  149.7 20.1 %collective-permute-start.18 = (bf16[8,256,256]{2,1,0:T(8,128)(2,1)}, bf16[8,256,256]{2,1,0:T(8,128)(2,1)S(1)}, u32[]{:S(2)}, u32[]{:S(2)}) collective-permute-start(bf16[8,256,256]{2,1,0:T(8,128)(2,1)} %get-tuple-element.26), channel_id=1, source_target_pairs={{0,24},{1,97},{2,26},{3,99},{4,28},{5,101},{6,30},{7,103},{8,16},{... | collective-permute-start | bytes 3145736 | tf_op jit(solution)/shard_map/ppermute | solution.py:75
  171.1 19.9 %all-to-all-start.3 = ((bf16[8,264,256]{2,1,0:T(8,128)(2,1)}), bf16[8,264,256]{2,1,0:T(8,128)(2,1)S(1)}, u32[]{:S(2)}, u32[]{:S(2)}) async-start(bf16[8,264,256]{2,1,0:T(8,128)(2,1)} %pad_maximum_fusion), calls=%async_computation.3 | async-start | bytes 2162688 | tf_op jit(solution)/shard_map/all_to_all | solution.py:405
  (17 other events, 108.6 us)

commit v2 on v1

--- a/solution.py
+++ b/solution.py
@@ -13,6 +13,10 @@
 I32 = jnp.int32
 
 CAP = 3
+FIRST_TILE = 400
+LAST_TILE = 480
+READY_VMEM = 20
+LAYER_VMEM = 26
 NI = 16
 NR = 8
 TOPK = 20
@@ -183,26 +187,13 @@
 NT = (((1,), (1,)), ((), ()))
 
 
-def layer_kernel(blocks, tile, last, *refs):
+def ready_kernel(sizes, *refs):
     y = refs[0][0, 0]
-    refs = refs[1:]
-    n_in = refs[:blocks]
-    d_in = refs[blocks : 2 * blocks]
-    wg_in, wu_in, wo_in = refs[2 * blocks : 2 * blocks + 3]
-    wp_in = refs[2 * blocks + 3 : 2 * blocks + 7]
-    rest = refs[2 * blocks + 7 :]
-    if last:
-        acc_in, gacc_ref, gain_ref, own_ref, par_ref, gout_ref = rest[:6]
-        rest = rest[6:]
-    else:
-        acc_ref, gout_ref = rest[:2]
-        rest = rest[2:]
-    nbuf, dbuf, wg, wu, wo, act, dgate, dup = rest[:8]
-    rest = rest[8:]
-    if last:
-        acc_ref = rest[0]
-        rest = rest[1:]
-    sems = rest[0]
+    blocks = sum(sizes)
+    d_in = refs[1 : 1 + blocks]
+    wg_in, wu_in, wo_in = refs[1 + blocks : 4 + blocks]
+    wp_in = refs[4 + blocks : 8 + blocks]
+    wg, wu, da, db, pa, pb, wo, sems = refs[8 + blocks :]
     count = [0]
 
     def start(src, dst):
@@ -211,35 +202,86 @@
         copy.start()
         return copy
 
-    first, second, third = [], [], []
-    first.append(start(wg_in, wg.at[:, pl.ds(0, FS)]))
-    first.append(start(wu_in, wu.at[:, pl.ds(0, FS)]))
-    for j in range(4):
-        part = pl.multiple_of((y + j) % 4 * 512, 512)
-        first.append(start(wp_in[j].at[pl.ds(0, 512)], wg.at[pl.ds(part, 512), pl.ds(FS, FS)]))
-        first.append(start(wp_in[j].at[pl.ds(512, 512)], wu.at[pl.ds(part, 512), pl.ds(FS, FS)]))
-    for b in range(blocks):
-        first.append(start(n_in[b], nbuf.at[pl.ds(b * ROWS, ROWS)]))
-    second.append(start(wo_in, wo.at[pl.ds(0, FS)]))
+    parts = [pl.multiple_of((y + j) % 4 * 512, 512) for j in range(4)]
+    first = [start(wo_in, wo.at[pl.ds(0, FS)])]
     for j in range(4):
         for h in range(2):
-            part = pl.multiple_of((y + j) % 4 * 512 + h * FS, FS)
-            second.append(
-                start(wp_in[j].at[pl.ds(1024 + h * FS, FS)], wo.at[pl.ds(FS, FS), pl.ds(part, FS)])
-            )
+            cols = pl.ds(pl.multiple_of(parts[j] + h * FS, FS), FS)
+            first.append(start(wp_in[j].at[pl.ds(1024 + h * FS, FS)], wo.at[pl.ds(FS, FS), cols]))
+    for b in range(sizes[0]):
+        first.append(start(d_in[b], da.at[pl.ds(b * ROWS, ROWS)]))
+    second = [start(d_in[sizes[0] + b], db.at[pl.ds(b * ROWS, ROWS)]) for b in range(sizes[1])]
+    third = [start(wg_in, wg.at[:, pl.ds(0, FS)]), start(wu_in, wu.at[:, pl.ds(0, FS)])]
+    for j in range(4):
+        rows = pl.ds(parts[j], 512)
+        third.append(start(wp_in[j].at[pl.ds(0, 512)], wg.at[rows, pl.ds(FS, FS)]))
+        third.append(start(wp_in[j].at[pl.ds(512, 512)], wu.at[rows, pl.ds(FS, FS)]))
+    for copy in first:
+        copy.wait()
+    pa[...] = lax.dot_general(da[...], wo[...], NT, preferred_element_type=F32)
+    for copy in second:
+        copy.wait()
+    pb[...] = lax.dot_general(db[...], wo[...], NT, preferred_element_type=F32)
+    for copy in third:
+        copy.wait()
+
+
+def make_ready(y, d_a, d_b, weights):
+    any_ = pl.BlockSpec(memory_space=pl.ANY)
+    vmem = pl.BlockSpec(memory_space=pltpu.VMEM)
+    sizes = (len(d_a), len(d_b))
+    rows = [n * ROWS for n in sizes]
+    out_shape = (
+        jax.ShapeDtypeStruct((D, 2 * FS), BF16),
+        jax.ShapeDtypeStruct((D, 2 * FS), BF16),
+        jax.ShapeDtypeStruct((rows[0], D), BF16),
+        jax.ShapeDtypeStruct((rows[1], D), BF16),
+        jax.ShapeDtypeStruct((rows[0], 2 * FS), F32),
+        jax.ShapeDtypeStruct((rows[1], 2 * FS), F32),
+    )
+    args = [y, *d_a, *d_b, *weights]
+    return pl.pallas_call(
+        functools.partial(ready_kernel, sizes),
+        out_shape=out_shape,
+        in_specs=[pl.BlockSpec(memory_space=pltpu.SMEM)] + [any_] * (len(args) - 1),
+        out_specs=tuple(vmem for _ in out_shape),
+        scratch_shapes=[pltpu.VMEM((2 * FS, D), BF16), pltpu.SemaphoreType.DMA((27,))],
+        compiler_params=pltpu.CompilerParams(vmem_limit_bytes=READY_VMEM * 1024 * 1024),
+        cost_estimate=pl.CostEstimate(
+            flops=2 * sum(rows) * D * 2 * FS, bytes_accessed=24 * 1024 * 1024, transcendentals=0
+        ),
+        name="ready",
+    )(*args)
+
+
+def layer_kernel(blocks, tile, last, *refs):
+    n_in = refs[:blocks]
+    wg, wu, dbuf, pre = refs[blocks : blocks + 4]
+    rest = refs[blocks + 4 :]
+    if last:
+        acc_in, gacc_ref, gain_ref, own_out, par_out, gout_ref = rest[:6]
+        rest = rest[6:]
+    else:
+        acc_out, gout_ref = rest[:2]
+        rest = rest[2:]
+    nbuf, gate_buf, act, dgate, dup, acc, par, sems, out_sems = rest
+
+    copies = []
     for b in range(blocks):
-        second.append(start(d_in[b], dbuf.at[pl.ds(b * ROWS, ROWS)]))
+        copies.append(pltpu.make_async_copy(n_in[b], nbuf.at[pl.ds(b * ROWS, ROWS)], sems.at[b]))
+        copies[-1].start()
     if last:
-        third.append(start(acc_in, acc_ref))
-    for copy in first + second:
-        copy.wait()
-
-    def body(t, carry):
-        rows = pl.ds(pl.multiple_of(t * tile, 16), tile)
-        n = nbuf[rows, :]
-        gate = jnp.dot(n, wg[...], preferred_element_type=F32)
-        up = jnp.dot(n, wu[...], preferred_element_type=F32)
-        d_act = lax.dot_general(dbuf[rows, :], wo[...], NT, preferred_element_type=F32)
+        acc_copy = pltpu.make_async_copy(acc_in, acc, sems.at[blocks])
+        acc_copy.start()
+    tiles = [slice(t * tile, (t + 1) * tile) for t in range(blocks * ROWS // tile)]
+    for copy in copies:
+        copy.wait()
+    for rows in tiles:
+        gate_buf[rows, :] = jnp.dot(nbuf[rows, :], wg[...], preferred_element_type=F32)
+    for rows in tiles:
+        up = jnp.dot(nbuf[rows, :], wu[...], preferred_element_type=F32)
+        gate = gate_buf[rows, :]
+        d_act = pre[rows, :]
         inner = GELU_C * (gate + 0.044715 * gate * gate * gate)
         th = jnp.tanh(inner)
         half = 0.5 * (1.0 + th)
@@ -248,47 +290,46 @@
         act[rows, :] = (gelu * up).astype(BF16)
         dgate[rows, :] = (d_act * up * slope).astype(BF16)
         dup[rows, :] = (d_act * gelu).astype(BF16)
-        return carry
-
-    lax.fori_loop(0, blocks * ROWS // tile, body, 0)
-
-    def gain_body(j, carry):
-        cols = pl.ds(pl.multiple_of(j * 512, 512), 512)
+    if last:
+        acc_copy.wait()
+    act_t = act[...].T
+    leaving = []
+    for r in range(NR):
+        cols = slice(r * FS, (r + 1) * FS)
+        part = jnp.dot(act_t, dbuf[:, cols], preferred_element_type=F32)
+        if last:
+            part = part + acc[r]
+            acc[r, :FS] = part[:FS]
+            par[r] = part[FS:].astype(BF16)
+            leaving.append(pltpu.make_async_copy(acc.at[r, pl.ds(0, FS)], own_out.at[r], out_sems.at[2 * r]))
+            leaving.append(pltpu.make_async_copy(par.at[r], par_out.at[r], out_sems.at[2 * r + 1]))
+            leaving[-2].start()
+            leaving[-1].start()
+        else:
+            acc[r] = part
+            leaving.append(pltpu.make_async_copy(acc.at[r], acc_out.at[r], out_sems.at[r]))
+            leaving[-1].start()
+
+    for j in range(4):
+        cols = slice(j * 512, (j + 1) * 512)
         dn = lax.dot_general(dgate[...], wg[cols, :], NT, preferred_element_type=F32)
         dn = dn + lax.dot_general(dup[...], wu[cols, :], NT, preferred_element_type=F32)
         part = jnp.sum(dn * nbuf[:, cols].astype(F32), axis=0, keepdims=True)
         if last:
             part = (part + gacc_ref[:, cols]) / gain_ref[:, cols]
         gout_ref[:, cols] = part
-        return carry
-
-    lax.fori_loop(0, 4, gain_body, 0)
-    for copy in third:
-        copy.wait()
-    act_t = act[...].T
-
-    def out_body(r, carry):
-        cols = pl.ds(pl.multiple_of(r * FS, FS), FS)
-        part = jnp.dot(act_t, dbuf[:, cols], preferred_element_type=F32)
-        if last:
-            part = part + acc_ref[r]
-            own_ref[r] = part[:FS]
-            par_ref[r] = part[FS:].astype(BF16)
-        else:
-            acc_ref[r] = part
-        return carry
-
-    lax.fori_loop(0, NR, out_body, 0)
-
-
-def layer(y, n_blocks, d_blocks, weights, tile, carried=None):
+    for copy in leaving:
+        copy.wait()
+
+
+def layer(n_blocks, ready, tile, carried=None):
     blocks = len(n_blocks)
     rows = blocks * ROWS
     last = carried is not None
     any_ = pl.BlockSpec(memory_space=pl.ANY)
     vmem = pl.BlockSpec(memory_space=pltpu.VMEM)
-    args = [y, *n_blocks, *d_blocks, *weights]
-    in_specs = [pl.BlockSpec(memory_space=pltpu.SMEM)] + [any_] * (len(args) - 1)
+    args = [*n_blocks, *ready]
+    in_specs = [any_] * blocks + [vmem] * len(ready)
     if last:
         args += list(carried)
         in_specs += [any_, vmem, vmem]
@@ -302,28 +343,25 @@
             jax.ShapeDtypeStruct((NR, 2 * FS, FS), F32),
             jax.ShapeDtypeStruct((1, D), F32),
         )
-    scratch = [
-        pltpu.VMEM((rows, D), BF16),
-        pltpu.VMEM((rows, D), BF16),
-        pltpu.VMEM((D, 2 * FS), BF16),
-        pltpu.VMEM((D, 2 * FS), BF16),
-        pltpu.VMEM((2 * FS, D), BF16),
-        pltpu.VMEM((rows, 2 * FS), BF16),
-        pltpu.VMEM((rows, 2 * FS), BF16),
-        pltpu.VMEM((rows, 2 * FS), BF16),
-    ]
-    if last:
-        scratch.append(pltpu.VMEM((NR, 2 * FS, FS), F32))
-    scratch.append(pltpu.SemaphoreType.DMA((2 * blocks + 20,)))
     return pl.pallas_call(
         functools.partial(layer_kernel, blocks, tile, last),
         out_shape=out_shape,
         in_specs=in_specs,
-        out_specs=tuple(vmem for _ in out_shape),
-        scratch_shapes=scratch,
-        compiler_params=pltpu.CompilerParams(vmem_limit_bytes=60 * 1024 * 1024),
+        out_specs=(*(any_ for _ in out_shape[1:]), vmem),
+        scratch_shapes=[
+            pltpu.VMEM((rows, D), BF16),
+            pltpu.VMEM((rows, 2 * FS), F32),
+            pltpu.VMEM((rows, 2 * FS), BF16),
+            pltpu.VMEM((rows, 2 * FS), BF16),
+            pltpu.VMEM((rows, 2 * FS), BF16),
+            pltpu.VMEM((NR, 2 * FS, FS), F32),
+            pltpu.VMEM((NR, FS, FS), BF16),
+            pltpu.SemaphoreType.DMA((blocks + 1,)),
+            pltpu.SemaphoreType.DMA((2 * NR,)),
+        ],
+        compiler_params=pltpu.CompilerParams(vmem_limit_bytes=LAYER_VMEM * 1024 * 1024),
         cost_estimate=pl.CostEstimate(
-            flops=12 * rows * D * 2 * FS, bytes_accessed=4 * rows * D + 6 * D * 2 * FS, transcendentals=rows * 512
+            flops=10 * rows * D * 2 * FS, bytes_accessed=4 * rows * D, transcendentals=rows * 512
         ),
         name="layer_last" if last else "layer_first",
     )(*args)
@@ -349,6 +387,7 @@
     dyp = pair(dy0)
     dy_next = ring(dy0, 1)
     dy_prev = ring(dy0, -1)
+    dy_far = ring(dy0, 2)
     y = lax.axis_index("reader") // 2
     y_row = y.astype(I32).reshape(1, 1)
     piece = jnp.concatenate(
@@ -365,16 +404,15 @@
     msg, src = make_plan(top_passages, probes, passage_home, question_emb)
     asked = lax.all_to_all(msg, "index", 0, 0, tiled=True)
     slots = asked[:, 6, :CAP].astype(I32)
-    blocks, piece, dyp, dy_next, dy_prev = pick_slots(
-        slots, passage_states, piece, dyp, dy_next, dy_prev
+    blocks, piece, dyp, dy_next, dy_prev, dy_far = pick_slots(
+        slots, passage_states, piece, dyp, dy_next, dy_prev, dy_far
     )
     recv = lax.all_to_all(blocks, "index", 0, 0, tiled=True)
-    dy_far = ring(dy0, 2)
     dy_a = [dy0, dy_next, dy_prev, dy_far, dyp]
     dy_b = [ring(dyp, 1), ring(dyp, -1), ring(dyp, 2)]
     weights = (w_gate, w_up, w_out, piece, column(piece, -1), column(piece, 2), column(piece, 1))
     gain_row = norm_gain.reshape(1, D)
-    n0 = norm_rows(src, recv, question_state, gain_row, dy_far, *dy_b)
+    n0 = norm_rows(src, recv, question_state, gain_row, *dy_b)
     np_ = pair(n0)
     n_a = [n0, ring(n0, 1), ring(n0, -1), ring(n0, 2), np_]
     n_b = [ring(np_, 1), ring(np_, -1), ring(np_, 2)]
@@ -387,8 +425,11 @@
     hot = (local[:, :, None] == jnp.arange(CLUS_DEV, dtype=I32)[None, None, :]).astype(F32)
     picked = jnp.einsum("qpc,qcs->qps", hot, every_score, precision=lax.Precision.HIGHEST)
 
-    acc_a, gain_a = layer(y_row, n_a, dy_a, weights, 400)
-    own, par, gain_part = layer(y_row, n_b, dy_b, weights, 240, (acc_a, gain_a, gain_row))
+    wg2, wu2, d_rows_a, d_rows_b, d_act_a, d_act_b = make_ready(y_row, dy_a, dy_b, weights)
+    acc_a, gain_a = layer(n_a, (wg2, wu2, d_rows_a, d_act_a), FIRST_TILE)
+    own, par, gain_part = layer(
+        n_b, (wg2, wu2, d_rows_b, d_act_b), LAST_TILE, (acc_a, gain_a, gain_row)
+    )
 
     from_partner = partner(par)
     tail = jnp.concatenate(

time: 193 us -> 183 us (0.948)
  waiting for transfers between devices: 58 us -> 47.4 us
  Pallas kernels: 45.9 us -> 38.3 us
  starting transfers between devices: 37.7 us -> 44.6 us
  blocking collectives: 30.6 us -> 34.8 us
  local copies, waits for them, and re-layouts: 9.21 us -> 7.16 us
    ppermute x12, waiting for transfers between devices: 40.6 us -> 26.6 us  [ring(): return lax.ppermute(v, BOTH, pairs_of(ring_move(step)))]
    pallas_call x2, Pallas kernels: 36.1 us -> 24.2 us  [layer(): pl.pallas_call(functools.partial(layer_kernel, blocks, tile, last), out_s...]
    all_to_all x1, blocking collectives: 13 us -> 18.4 us  [shards(): asked = lax.all_to_all(msg, 'index', 0, 0, tiled=True)]
    pallas_call x0 -> x1, Pallas kernels: none -> 5.23 us  [make_ready(): pl.pallas_call(functools.partial(ready_kernel, sizes), out_shape=out_shap...]
    all_to_all x1, starting transfers between devices: 4.47 us -> 8.2 us  [shards(): lax.all_to_all(jnp.concatenate([total, gain_rows], axis=1), 'reader', 0,...]
    all_to_all x1, starting transfers between devices: 5.9 us -> 8.26 us  [shards(): recv = lax.all_to_all(blocks, 'index', 0, 0, tiled=True)]
    ppermute x2, starting transfers between devices: 4.53 us -> 6.84 us  [partner(): return lax.ppermute(v, BOTH, pairs_of(partner_move))]
    ppermute x2, waiting for transfers between devices: 2.53 us -> 4.5 us  [pair(): return lax.ppermute(v, BOTH, pairs_of(pair_move))]
where the time goes in v2:
time: 183 us
  waiting for transfers between devices  47.4 us (26%)
  starting transfers between devices  44.6 us (24%)
  Pallas kernels  38.3 us (21%)
  blocking collectives  34.8 us (19%)
  local copies, waits for them, and re-layouts  7.16 us (4%)
  matrix products  4.86 us (3%)
  other arithmetic  4.66 us (3%)
    ppermute x12, waiting for transfers between devices, ring(): return lax.ppermute(v, BOTH, pairs_of(ring_move(step)))  26.6 us
    pallas_call x2, Pallas kernels, layer(): pl.pallas_call(functools.partial(layer_kernel, blocks, tile, last), out_s...  24.2 us
    all_to_all x1, blocking collectives, shards(): asked = lax.all_to_all(msg, 'index', 0, 0, tiled=True)  18.4 us
    all_to_all x1, blocking collectives, shards(): tail = lax.all_to_all(tail, 'index', 0, 0, tiled=True)  16.5 us
    ppermute x12, starting transfers between devices, ring(): return lax.ppermute(v, BOTH, pairs_of(ring_move(step)))  15.9 us
    all_to_all x1, waiting for transfers between devices, shards(): lax.all_to_all(jnp.concatenate([total, gain_rows], axis=1), 'reader', 0,...  14.8 us
    all_to_all x1, starting transfers between devices, shards(): recv = lax.all_to_all(blocks, 'index', 0, 0, tiled=True)  8.26 us
    all_to_all x1, starting transfers between devices, shards(): lax.all_to_all(jnp.concatenate([total, gain_rows], axis=1), 'reader', 0,...  8.2 us
  transfers between devices with their start and end apart: 21, of which 7 were waited for; matrix products, arithmetic and copies ran while one was open for 5% of the time, Pallas kernels for 14%

profile of v2, /device:TPU:1, one launch (start us, length us, event | category | flops | bytes accessed | tf_op | source)
XLA Modules:
  0.0 182.8 jit_solution(14839991306512061527)
XLA Ops:
  2.9 3.4 %collective-permute-start = (bf16[1536,256]{1,0:T(8,128)(2,1)S(1)}, bf16[1536,256]{1,0:T(8,128)(2,1)S(1)}, u32[]{:S(2)}, u32[]{:S(2)}) collective-permute-start(bf16[1536,256]{1,0:T(8,128)(2,1)S(1)} %pad_maximum_fusion.1), channel_id=1, source_target_pairs={{0,24},{1,97},{2,26},{3,99},{4,28},{5,101},{6,30},{7,103},{8,16},{... | collective-permute-start | bytes 2359304 | tf_op jit(solution)/shard_map/ppermute | solution.py:79
  7.3 1.7 collective-permute-start.2
  9.0 2.1 %collective-permute-start.3 = (bf16[160,2048]{1,0:T(8,128)(2,1)}, bf16[160,2048]{1,0:T(8,128)(2,1)S(1)}, u32[]{:S(2)}, u32[]{:S(2)}) collective-permute-start(bf16[160,2048]{1,0:T(8,128)(2,1)} %fusion.refs_1_), channel_id=1, source_target_pairs={{0,96},{1,25},{2,98},{3,27},{4,100},{5,29},{6,102},{7,31},{8,104},... | collective-permute-start | bytes 1966088 | tf_op jit(solution)/shard_map/ppermute | solution.py:71
  13.0 2.3 %plan.1 = (bf16[16,8,128]{2,1,0:T(8,128)(2,1)}, s32[1,20]{1,0:T(1,128)}) custom-call(s32[1,20]{1,0:T(1,128)} %top_ref.1, s32[1,32]{1,0:T(1,128)} %probes_ref.1, s32[4096]{0:T(1024)} %home_ref.1, f32[8,128]{1,0:T(8,128)} %pad_convert_fusion.emb_ref), custom_call_target="tpu_custom_call" | custom-call | tf_op jit(solution)/shard_map/plan/pallas_call | solution.py:109
  15.3 18.4 %all_to_all.20 = bf16[16,8,128]{2,1,0:T(8,128)(2,1)S(1)} all-to-all(bf16[16,8,128]{2,1,0:T(8,128)(2,1)} %get-tuple-element.22), channel_id=1, replica_groups=mesh['index'=16,'reader'=8] {'index'}, dimensions={0} | all-to-all | bytes 65536 | tf_op jit(solution)/shard_map/all_to_all | solution.py:405
  35.8 3.7 %pick.1 = (bf16[48,8,2048]{2,1,0:T(8,128)(2,1)}, bf16[1536,256]{1,0:T(8,128)(2,1)}, bf16[160,2048]{1,0:T(8,128)(2,1)}, bf16[160,2048]{1,0:T(8,128)(2,1)}, bf16[1...) custom-call(s32[16,3]{1,0:T(8,128)} %bitcast.27, ...), custom_call_target="tpu_custom_call", output_to_operand_aliasing={{1}: (2, {}), {2}: (3, {}), {3}: (4, {}), {4}: (5, {}), {5}... | custom-call | bytes 3145728 | tf_op jit(solution)/shard_map/pick/pallas_call | solution.py:135
  39.6 8.3 %all-to-all-start.1 = ((bf16[48,8,2048]{2,1,0:T(8,128)(2,1)}), bf16[48,8,2048]{2,1,0:T(8,128)(2,1)S(1)}, u32[]{:S(2)}, u32[]{:S(2)}) async-start(bf16[48,8,2048]{2,1,0:T(8,128)(2,1)} %get-tuple-element.24), calls=%async_computation.1 | async-start | bytes 3145728 | tf_op jit(solution)/shard_map/all_to_all | solution.py:410
  47.9 1.4 collective-permute-start.5
  49.3 2.7 %collective-permute-start.12 = (bf16[1536,256]{1,0:T(8,128)(2,1)S(1)}, bf16[1536,256]{1,0:T(8,128)(2,1)}, u32[]{:S(2)}, u32[]{:S(2)}) collective-permute-start(bf16[1536,256]{1,0:T(8,128)(2,1)S(1)} %copy-done.1), channel_id=1, source_target_pairs={{0,6},{1,7},{2,0},{3,1},{4,2},{5,3},{6,4},{7,5},{8,14},{9,15},{10,... | collective-permute-start | bytes 2359304 | tf_op jit(solution)/shard_map/ppermute | solution.py:67
  53.7 1.7 collective-permute-start.7
  55.3 20.5 %collective-permute-done.5.refs_0_.refs_6_ = bf16[160,2048]{1,0:T(8,128)(2,1)S(1)} collective-permute-done((bf16[160,2048]{1,0:T(8,128)(2,1)S(1)}, bf16[160,2048]{1,0:T(8,128)(2,1)S(1)}, u32[]{:S(2)}, u32[]{:S(2)}) %collective-permute-start.5) | collective-permute-done | bytes 655392 | tf_op jit(solution)/shard_map/ppermute | solution.py:71
  78.1 5.1 %collective-permute-done.7.refs_2_.refs_8_ = bf16[160,2048]{1,0:T(8,128)(2,1)} collective-permute-done((bf16[160,2048]{1,0:T(8,128)(2,1)S(1)}, bf16[160,2048]{1,0:T(8,128)(2,1)}, u32[]{:S(2)}, u32[]{:S(2)}) %collective-permute-start.7) | collective-permute-done | bytes 655392 | tf_op jit(solution)/shard_map/ppermute | solution.py:71
  84.3 2.9 %norm.1.refs_0_ = bf16[160,2048]{1,0:T(8,128)(2,1)S(1)} custom-call(s32[1,20]{1,0:T(1,128)S(1)} %copy-done.16, bf16[48,8,2048]{2,1,0:T(8,128)(2,1)S(1)} %all-to-all-done.1.recv_ref, bf16[1,2048]{1,0:T(2,128)(2,1)S(1)} %copy-done.14, f32[1,2048]{1,0:T(1,128)S(1)} %bitcast.20, bf16[160,2048]{1,0:T(8,128)(2,1)S(1)} %copy-done.9, ...), custom_call_target="tpu_custom_call" | custom-call | tf_op jit(solution)/shard_map/norm/pallas_call | solution.py:170
  87.7 2.3 %collective-permute-start.16 = (bf16[160,2048]{1,0:T(8,128)(2,1)S(1)}, bf16[160,2048]{1,0:T(8,128)(2,1)S(1)}, u32[]{:S(2)}, u32[]{:S(2)}) collective-permute-start(bf16[160,2048]{1,0:T(8,128)(2,1)S(1)} %norm.1.refs_0_), channel_id=1, source_target_pairs={{0,96},{1,25},{2,98},{3,27},{4,100},{5,29},{6,102},{7,31},{8,104},... | collective-permute-start | bytes 1966088 | tf_op jit(solution)/shard_map/ppermute | solution.py:71
  91.2 4.5 %convolution_multiply_fusion = f32[16,32,128]{2,0,1:T(8,128)S(1)} fusion(bf16[16,768,1]{1,0,2:T(8,128)(2,1)S(1)} %reshape.83, bf16[32,128,768]{2,1,0:T(8,128)(2,1)} %param.16, f32[32,128]{1,0:T(8,128)S(1)} %copy-done.20), kind=kOutput, calls=%fused_computation.3 | convolution fusion | flops 100728832 | bytes 6594560 | tf_op jit(solution)/shard_map/qe,cse->qcs/dot_general | solution.py:422
  97.1 5.2 %ready.1 = (bf16[2048,512]{1,0:T(8,128)(2,1)S(1)}, bf16[2048,512]{1,0:T(8,128)(2,1)S(1)}, bf16[800,2048]{1,0:T(8,128)(2,1)S(1)}, bf16[480,2048]{1,0:T(8,128)(2,1...) custom-call(s32[1,1]{1,0:T(1,128)} %bitcast.5.refs_0_, bf16[160,2048]{1,0:T(8,128)(2,1)} %fusion.refs_1_, ...), custom_call_target="tpu_custom_call" | custom-call | flops 2684354560 | bytes 25165824 | tf_op jit(solution)/shard_map/ready/pallas_call | solution.py:243
  102.4 4.5 %collective-permute-done.8.refs_4_ = bf16[160,2048]{1,0:T(8,128)(2,1)S(1)} collective-permute-done((bf16[160,2048]{1,0:T(8,128)(2,1)S(1)}, bf16[160,2048]{1,0:T(8,128)(2,1)S(1)}, u32[]{:S(2)}, u32[]{:S(2)}) %collective-permute-start.8) | collective-permute-done | bytes 655392 | tf_op jit(solution)/shard_map/ppermute | solution.py:75
  107.6 2.0 %collective-permute-start.11 = (bf16[160,2048]{1,0:T(8,128)(2,1)S(1)}, bf16[160,2048]{1,0:T(8,128)(2,1)S(1)}, u32[]{:S(2)}, u32[]{:S(2)}) collective-permute-start(bf16[160,2048]{1,0:T(8,128)(2,1)S(1)} %collective-permute-done.8.refs_4_), channel_id=1, source_target_pairs={{0,64},{1,17},{2,66},{3,19},{4,68},{5,21},{6,70},{7,23},{8,72},{9,... | collective-permute-start | bytes 1966088 | tf_op jit(solution)/shard_map/ppermute | solution.py:71
  111.1 14.4 %layer_first.1 = (f32[8,512,256]{2,1,0:T(8,128)S(1)}, f32[1,2048]{1,0:T(1,128)S(1)}) custom-call(bf16[160,2048]{1,0:T(8,128)(2,1)S(1)} %norm.1.refs_0_, bf16[160,2048]{1,0:T(8,128)(2,1)S(1)} %collective-permute-done.15.refs_1_, bf16[160,2048]{1,0:T(8,128)(2,1)S(1)} %collective-permute-done.16.refs_2_, bf16[160,2048]{1,0:T(8,128)(2,1)S(1)} %collective-permute-done.17.refs_3_, ...), custom_call_target="tpu_custom_call" | custom-call | flops 8388608000 | bytes 6553600 | tf_op jit(solution)/shard_map/layer_first/pallas_call | solution.py:346
  126.0 9.8 %layer_last.1 = (f32[8,256,256]{2,1,0:T(8,128)S(1)}, bf16[8,256,256]{2,1,0:T(8,128)(2,1)}, f32[1,2048]{1,0:T(1,128)S(1)}) custom-call(bf16[160,2048]{1,0:T(8,128)(2,1)S(1)} %collective-permute-done.9.refs_0_, bf16[160,2048]{1,0:T(8,128)(2,1)S(1)} %collective-permute-done.10.refs_1_, bf16[160,2048]{1,0:T(8,128)(2,1)S(1)} %collective-permute-done.11.refs_2_, ...), custom_call_target="tpu_custom_call" | custom-call | flops 5033164800 | bytes 3932160 | tf_op jit(solution)/shard_map/layer_last/pallas_call | solution.py:346
  135.8 3.4 %collective-permute-start.18 = (bf16[8,256,256]{2,1,0:T(8,128)(2,1)}, bf16[8,256,256]{2,1,0:T(8,128)(2,1)S(1)}, u32[]{:S(2)}, u32[]{:S(2)}) collective-permute-start(bf16[8,256,256]{2,1,0:T(8,128)(2,1)} %get-tuple-element.40), channel_id=1, source_target_pairs={{0,24},{1,97},{2,26},{3,99},{4,28},{5,101},{6,30},{7,103},{8,16},{... | collective-permute-start | bytes 3145736 | tf_op jit(solution)/shard_map/ppermute | solution.py:79
  139.7 16.5 %all_to_all.21 = f32[16,40,128]{2,1,0:T(8,128)S(1)} all-to-all(f32[16,40,128]{2,1,0:T(8,128)S(1)} %maximum_maximum_fusion), channel_id=1, replica_groups=mesh['index'=16,'reader'=8] {'index'}, dimensions={0} | all-to-all | bytes 655360 | tf_op jit(solution)/shard_map/all_to_all | solution.py:438
  157.7 8.2 %all-to-all-start.3 = ((bf16[8,264,256]{2,1,0:T(8,128)(2,1)}), bf16[8,264,256]{2,1,0:T(8,128)(2,1)S(1)}, u32[]{:S(2)}, u32[]{:S(2)}) async-start(bf16[8,264,256]{2,1,0:T(8,128)(2,1)} %pad_maximum_fusion), calls=%async_computation.3 | async-start | bytes 2162688 | tf_op jit(solution)/shard_map/all_to_all | solution.py:446
  166.5 14.8 %all-to-all-done.3 = bf16[8,264,256]{2,1,0:T(8,128)(2,1)S(1)} async-done(((bf16[8,264,256]{2,1,0:T(8,128)(2,1)}), bf16[8,264,256]{2,1,0:T(8,128)(2,1)S(1)}, u32[]{:S(2)}, u32[]{:S(2)}) %all-to-all-start.3) | async-done | bytes 1081376 | tf_op jit(solution)/shard_map/all_to_all | solution.py:446
  (98 shorter events, 22.0 us)
Async XLA Ops:
  2.9 31.5 %collective-permute-start = (bf16[1536,256]{1,0:T(8,128)(2,1)S(1)}, bf16[1536,256]{1,0:T(8,128)(2,1)S(1)}, u32[]{:S(2)}, u32[]{:S(2)}) collective-permute-start(bf16[1536,256]{1,0:T(8,128)(2,1)S(1)} %pad_maximum_fusion.1), channel_id=1, source_target_pairs={{0,24},{1,97},{2,26},{3,99},{4,28},{5,101},{6,30},{7,103},{8,16},{... | collective-permute-start | bytes 2359304 | tf_op jit(solution)/shard_map/ppermute | solution.py:79
  7.3 27.0 %collective-permute-start.1 = (bf16[160,2048]{1,0:T(8,128)(2,1)}, bf16[160,2048]{1,0:T(8,128)(2,1)S(1)}, u32[]{:S(2)}, u32[]{:S(2)}) collective-permute-start(bf16[160,2048]{1,0:T(8,128)(2,1)} %fusion.refs_1_), channel_id=1, source_target_pairs={{0,8},{1,33},{2,10},{3,35},{4,12},{5,37},{6,14},{7,39},{8,0},{9,41... | collective-permute-start | bytes 1966088 | tf_op jit(solution)/shard_map/ppermute | solution.py:75
  7.3 27.0 %collective-permute-start.2 = (bf16[160,2048]{1,0:T(8,128)(2,1)}, bf16[160,2048]{1,0:T(8,128)(2,1)S(1)}, u32[]{:S(2)}, u32[]{:S(2)}) collective-permute-start(bf16[160,2048]{1,0:T(8,128)(2,1)} %fusion.refs_1_), channel_id=1, source_target_pairs={{0,32},{1,9},{2,34},{3,11},{4,36},{5,13},{6,38},{7,15},{8,40},{9,1... | collective-permute-start | bytes 1966088 | tf_op jit(solution)/shard_map/ppermute | solution.py:71
  9.0 25.4 %collective-permute-start.3 = (bf16[160,2048]{1,0:T(8,128)(2,1)}, bf16[160,2048]{1,0:T(8,128)(2,1)S(1)}, u32[]{:S(2)}, u32[]{:S(2)}) collective-permute-start(bf16[160,2048]{1,0:T(8,128)(2,1)} %fusion.refs_1_), channel_id=1, source_target_pairs={{0,96},{1,25},{2,98},{3,27},{4,100},{5,29},{6,102},{7,31},{8,104},... | collective-permute-start | bytes 1966088 | tf_op jit(solution)/shard_map/ppermute | solution.py:71
  11.1 23.3 %collective-permute-start.4 = (bf16[160,2048]{1,0:T(8,128)(2,1)}, bf16[160,2048]{1,0:T(8,128)(2,1)}, u32[]{:S(2)}, u32[]{:S(2)}) collective-permute-start(bf16[160,2048]{1,0:T(8,128)(2,1)} %fusion.refs_1_), channel_id=1, source_target_pairs={{0,64},{1,17},{2,66},{3,19},{4,68},{5,21},{6,70},{7,23},{8,72},{9,... | collective-permute-start | bytes 1966088 | tf_op jit(solution)/shard_map/ppermute | solution.py:71
  39.6 43.6 %copy-start.14 = (bf16[1,2048]{1,0:T(2,128)(2,1)S(1)}, bf16[1,2048]{1,0:T(2,128)(2,1)}, u32[]{:S(2)}) copy-start(bf16[1,2048]{1,0:T(2,128)(2,1)} %state_ref.1) | copy-start | bytes 12292
  39.6 43.6 %copy-start.15 = (f32[2048]{0:T(1024)S(1)}, f32[2048]{0:T(1024)}, u32[]{:S(2)}) copy-start(f32[2048]{0:T(1024)} %param.23) | copy-start | bytes 24580
  39.6 43.6 %copy-start.16 = (s32[1,20]{1,0:T(1,128)S(1)}, s32[1,20]{1,0:T(1,128)}, u32[]{:S(2)}) copy-start(s32[1,20]{1,0:T(1,128)} %get-tuple-element.23.src_ref) | copy-start | bytes 244
  39.6 43.6 %all-to-all-start.1 = ((bf16[48,8,2048]{2,1,0:T(8,128)(2,1)}), bf16[48,8,2048]{2,1,0:T(8,128)(2,1)S(1)}, u32[]{:S(2)}, u32[]{:S(2)}) async-start(bf16[48,8,2048]{2,1,0:T(8,128)(2,1)} %get-tuple-element.24), calls=%async_computation.1 | async-start | bytes 3145728 | tf_op jit(solution)/shard_map/all_to_all | solution.py:410
  47.9 27.9 %collective-permute-start.5 = (bf16[160,2048]{1,0:T(8,128)(2,1)S(1)}, bf16[160,2048]{1,0:T(8,128)(2,1)S(1)}, u32[]{:S(2)}, u32[]{:S(2)}) collective-permute-start(bf16[160,2048]{1,0:T(8,128)(2,1)S(1)} %copy-done.3), channel_id=1, source_target_pairs={{0,32},{1,9},{2,34},{3,11},{4,36},{5,13},{6,38},{7,15},{8,40},{9,1... | collective-permute-start | bytes 1966088 | tf_op jit(solution)/shard_map/ppermute | solution.py:71
  49.3 40.7 %collective-permute-start.12 = (bf16[1536,256]{1,0:T(8,128)(2,1)S(1)}, bf16[1536,256]{1,0:T(8,128)(2,1)}, u32[]{:S(2)}, u32[]{:S(2)}) collective-permute-start(bf16[1536,256]{1,0:T(8,128)(2,1)S(1)} %copy-done.1), channel_id=1, source_target_pairs={{0,6},{1,7},{2,0},{3,1},{4,2},{5,3},{6,4},{7,5},{8,14},{9,15},{10,... | collective-permute-start | bytes 2359304 | tf_op jit(solution)/shard_map/ppermute | solution.py:67
  52.1 38.0 %collective-permute-start.13 = (bf16[1536,256]{1,0:T(8,128)(2,1)S(1)}, bf16[1536,256]{1,0:T(8,128)(2,1)}, u32[]{:S(2)}, u32[]{:S(2)}) collective-permute-start(bf16[1536,256]{1,0:T(8,128)(2,1)S(1)} %copy-done.1), channel_id=1, source_target_pairs={{0,4},{1,5},{2,6},{3,7},{4,0},{5,1},{6,2},{7,3},{8,12},{9,13},{10,... | collective-permute-start | bytes 2359304 | tf_op jit(solution)/shard_map/ppermute | solution.py:67
  52.3 25.8 %collective-permute-start.6 = (bf16[160,2048]{1,0:T(8,128)(2,1)S(1)}, bf16[160,2048]{1,0:T(8,128)(2,1)}, u32[]{:S(2)}, u32[]{:S(2)}) collective-permute-start(bf16[160,2048]{1,0:T(8,128)(2,1)S(1)} %copy-done.3), channel_id=1, source_target_pairs={{0,96},{1,25},{2,98},{3,27},{4,100},{5,29},{6,102},{7,31},{8,104},... | collective-permute-start | bytes 1966088 | tf_op jit(solution)/shard_map/ppermute | solution.py:71
  53.7 29.6 %collective-permute-start.7 = (bf16[160,2048]{1,0:T(8,128)(2,1)S(1)}, bf16[160,2048]{1,0:T(8,128)(2,1)}, u32[]{:S(2)}, u32[]{:S(2)}) collective-permute-start(bf16[160,2048]{1,0:T(8,128)(2,1)S(1)} %copy-done.3), channel_id=1, source_target_pairs={{0,64},{1,17},{2,66},{3,19},{4,68},{5,21},{6,70},{7,23},{8,72},{9,... | collective-permute-start | bytes 1966088 | tf_op jit(solution)/shard_map/ppermute | solution.py:71
  76.7 20.4 %collective-permute-start.14 = (bf16[1536,256]{1,0:T(8,128)(2,1)S(1)}, bf16[1536,256]{1,0:T(8,128)(2,1)}, u32[]{:S(2)}, u32[]{:S(2)}) collective-permute-start(bf16[1536,256]{1,0:T(8,128)(2,1)S(1)} %copy-done.1), channel_id=1, source_target_pairs={{0,2},{1,3},{2,4},{3,5},{4,6},{5,7},{6,0},{7,1},{8,10},{9,11},{10,... | collective-permute-start | bytes 2359304 | tf_op jit(solution)/shard_map/ppermute | solution.py:67
  87.3 22.4 %collective-permute-start.15 = (bf16[160,2048]{1,0:T(8,128)(2,1)S(1)}, bf16[160,2048]{1,0:T(8,128)(2,1)S(1)}, u32[]{:S(2)}, u32[]{:S(2)}) collective-permute-start(bf16[160,2048]{1,0:T(8,128)(2,1)S(1)} %norm.1.refs_0_), channel_id=1, source_target_pairs={{0,32},{1,9},{2,34},{3,11},{4,36},{5,13},{6,38},{7,15},{8,40},{9,1... | collective-permute-start | bytes 1966088 | tf_op jit(solution)/shard_map/ppermute | solution.py:71
  87.7 22.9 %collective-permute-start.16 = (bf16[160,2048]{1,0:T(8,128)(2,1)S(1)}, bf16[160,2048]{1,0:T(8,128)(2,1)S(1)}, u32[]{:S(2)}, u32[]{:S(2)}) collective-permute-start(bf16[160,2048]{1,0:T(8,128)(2,1)S(1)} %norm.1.refs_0_), channel_id=1, source_target_pairs={{0,96},{1,25},{2,98},{3,27},{4,100},{5,29},{6,102},{7,31},{8,104},... | collective-permute-start | bytes 1966088 | tf_op jit(solution)/shard_map/ppermute | solution.py:71
  90.0 21.0 %collective-permute-start.17 = (bf16[160,2048]{1,0:T(8,128)(2,1)S(1)}, bf16[160,2048]{1,0:T(8,128)(2,1)S(1)}, u32[]{:S(2)}, u32[]{:S(2)}) collective-permute-start(bf16[160,2048]{1,0:T(8,128)(2,1)S(1)} %norm.1.refs_0_), channel_id=1, source_target_pairs={{0,64},{1,17},{2,66},{3,19},{4,68},{5,21},{6,70},{7,23},{8,72},{9,... | collective-permute-start | bytes 1966088 | tf_op jit(solution)/shard_map/ppermute | solution.py:71
  90.0 16.8 %collective-permute-start.8 = (bf16[160,2048]{1,0:T(8,128)(2,1)S(1)}, bf16[160,2048]{1,0:T(8,128)(2,1)S(1)}, u32[]{:S(2)}, u32[]{:S(2)}) collective-permute-start(bf16[160,2048]{1,0:T(8,128)(2,1)S(1)} %norm.1.refs_0_), channel_id=1, source_target_pairs={{0,8},{1,33},{2,10},{3,35},{4,12},{5,37},{6,14},{7,39},{8,0},{9,41... | collective-permute-start | bytes 1966088 | tf_op jit(solution)/shard_map/ppermute | solution.py:75
  106.8 18.6 %collective-permute-start.10 = (bf16[160,2048]{1,0:T(8,128)(2,1)S(1)}, bf16[160,2048]{1,0:T(8,128)(2,1)S(1)}, u32[]{:S(2)}, u32[]{:S(2)}) collective-permute-start(bf16[160,2048]{1,0:T(8,128)(2,1)S(1)} %collective-permute-done.8.refs_4_), channel_id=1, source_target_pairs={{0,96},{1,25},{2,98},{3,27},{4,100},{5,29},{6,102},{7,31},{8,104},... | collective-permute-start | bytes 1966088 | tf_op jit(solution)/shard_map/ppermute | solution.py:71
  107.6 17.8 %collective-permute-start.11 = (bf16[160,2048]{1,0:T(8,128)(2,1)S(1)}, bf16[160,2048]{1,0:T(8,128)(2,1)S(1)}, u32[]{:S(2)}, u32[]{:S(2)}) collective-permute-start(bf16[160,2048]{1,0:T(8,128)(2,1)S(1)} %collective-permute-done.8.refs_4_), channel_id=1, source_target_pairs={{0,64},{1,17},{2,66},{3,19},{4,68},{5,21},{6,70},{7,23},{8,72},{9,... | collective-permute-start | bytes 1966088 | tf_op jit(solution)/shard_map/ppermute | solution.py:71
  109.7 16.3 %collective-permute-start.9 = (bf16[160,2048]{1,0:T(8,128)(2,1)S(1)}, bf16[160,2048]{1,0:T(8,128)(2,1)S(1)}, u32[]{:S(2)}, u32[]{:S(2)}) collective-permute-start(bf16[160,2048]{1,0:T(8,128)(2,1)S(1)} %collective-permute-done.8.refs_4_), channel_id=1, source_target_pairs={{0,32},{1,9},{2,34},{3,11},{4,36},{5,13},{6,38},{7,15},{8,40},{9,1... | collective-permute-start | bytes 1966088 | tf_op jit(solution)/shard_map/ppermute | solution.py:71
  135.8 20.6 %collective-permute-start.18 = (bf16[8,256,256]{2,1,0:T(8,128)(2,1)}, bf16[8,256,256]{2,1,0:T(8,128)(2,1)S(1)}, u32[]{:S(2)}, u32[]{:S(2)}) collective-permute-start(bf16[8,256,256]{2,1,0:T(8,128)(2,1)} %get-tuple-element.40), channel_id=1, source_target_pairs={{0,24},{1,97},{2,26},{3,99},{4,28},{5,101},{6,30},{7,103},{8,16},{... | collective-permute-start | bytes 3145736 | tf_op jit(solution)/shard_map/ppermute | solution.py:79
  157.7 23.6 %all-to-all-start.3 = ((bf16[8,264,256]{2,1,0:T(8,128)(2,1)}), bf16[8,264,256]{2,1,0:T(8,128)(2,1)S(1)}, u32[]{:S(2)}, u32[]{:S(2)}) async-start(bf16[8,264,256]{2,1,0:T(8,128)(2,1)} %pad_maximum_fusion), calls=%async_computation.3 | async-start | bytes 2162688 | tf_op jit(solution)/shard_map/all_to_all | solution.py:446
  (20 other events, 151.6 us)

commit v3 on v2

--- a/solution.py
+++ b/solution.py
@@ -71,6 +71,11 @@
     return lax.ppermute(v, BOTH, pairs_of(ring_move(step)))
 
 
+def relayed(prev, following):
+    half = ROWS // 2
+    return [ring(prev[:half], 1), ring(following[half:], -1)]
+
+
 def pair(v):
     return lax.ppermute(v, BOTH, pairs_of(pair_move))
 
@@ -79,7 +84,17 @@
     return lax.ppermute(v, BOTH, pairs_of(partner_move))
 
 
-def plan_kernel(top_ref, probes_ref, home_ref, emb_ref, msg_ref, src_ref):
+def plan_kernel(top_ref, probes_ref, home_ref, y_ref, emb_ref, wg_ref, wu_ref, wo_ref, msg_ref, src_ref, piece_ref, sems):
+    part = pl.multiple_of(y_ref[0, 0] * 512, 512)
+    cuts = [
+        (wg_ref.at[pl.ds(part, 512)], piece_ref.at[pl.ds(0, 512)]),
+        (wu_ref.at[pl.ds(part, 512)], piece_ref.at[pl.ds(512, 512)]),
+        (wo_ref.at[:, pl.ds(part, FS)], piece_ref.at[pl.ds(1024, FS)]),
+        (wo_ref.at[:, pl.ds(pl.multiple_of(part + FS, FS), FS)], piece_ref.at[pl.ds(1024 + FS, FS)]),
+    ]
+    cuts = [pltpu.make_async_copy(src, dst, sems.at[i]) for i, (src, dst) in enumerate(cuts)]
+    for copy in cuts:
+        copy.start()
     shape = (NI, 8, 128)
     owner_id = lax.broadcasted_iota(I32, shape, 0)
     lane_id = lax.broadcasted_iota(I32, shape, 2)
@@ -100,9 +115,12 @@
         vec = jnp.where((owner_id == c // CLUS_DEV) & (lane_id == 8 + k), c % CLUS_DEV, vec)
     emb = jnp.broadcast_to(emb_ref[...][None], shape)
     msg_ref[...] = jnp.where(row_id == 6, vec.astype(F32), emb).astype(BF16)
-
-
-def make_plan(top, probes, home, emb):
+    for copy in cuts:
+        copy.wait()
+
+
+def make_plan(top, probes, home, y, emb, w_gate, w_up, w_out):
+    any_ = pl.BlockSpec(memory_space=pl.ANY)
     emb8 = jnp.pad(emb.astype(F32).reshape(6, 128), ((0, 2), (0, 0)))
     smem = pl.BlockSpec(memory_space=pltpu.SMEM)
     vmem = pl.BlockSpec(memory_space=pltpu.VMEM)
@@ -111,11 +129,52 @@
         out_shape=(
             jax.ShapeDtypeStruct((NI, 8, 128), BF16),
             jax.ShapeDtypeStruct((1, TOPK), I32),
+            jax.ShapeDtypeStruct((1536, FS), BF16),
         ),
-        in_specs=[smem, smem, smem, vmem],
-        out_specs=(vmem, smem),
+        in_specs=[smem, smem, smem, smem, vmem, any_, any_, any_],
+        out_specs=(vmem, smem, vmem),
+        scratch_shapes=[pltpu.SemaphoreType.DMA((4,))],
+        compiler_params=pltpu.CompilerParams(vmem_limit_bytes=60 * 1024 * 1024),
         name="plan",
-    )(top, probes, home, emb8)
+    )(top, probes, home, y, emb8, w_gate, w_up, w_out)
+
+
+def ask_kernel(asked_ref, *refs):
+    slot_ref = refs[len(refs) // 2]
+    slot_ref[...] = asked_ref[:, 6, :].astype(F32).astype(I32)
+
+
+def read_asked(asked, *passed):
+    any_ = pl.BlockSpec(memory_space=pl.ANY)
+    vmem = pl.BlockSpec(memory_space=pltpu.VMEM)
+    return pl.pallas_call(
+        ask_kernel,
+        out_shape=(
+            jax.ShapeDtypeStruct((NI, 128), I32),
+            *(jax.ShapeDtypeStruct(v.shape, v.dtype) for v in passed),
+        ),
+        in_specs=[vmem] + [any_] * len(passed),
+        out_specs=(vmem, *(any_ for _ in passed)),
+        input_output_aliases={1 + i: 1 + i for i in range(len(passed))},
+        name="ask",
+    )(asked, *passed)
+
+
+def send_kernel(*refs):
+    pass
+
+
+def send_after(value, *passed):
+    any_ = pl.BlockSpec(memory_space=pl.ANY)
+    args = (value, *passed)
+    return pl.pallas_call(
+        send_kernel,
+        out_shape=tuple(jax.ShapeDtypeStruct(v.shape, v.dtype) for v in args),
+        in_specs=[any_] * len(args),
+        out_specs=tuple(any_ for _ in args),
+        input_output_aliases={i: i for i in range(len(args))},
+        name="send",
+    )(*args)
 
 
 def pick_kernel(slot_ref, states_ref, *refs):
@@ -179,7 +238,7 @@
         ],
         out_specs=vmem,
         scratch_shapes=[pltpu.VMEM((TOPK, LP, D), BF16), pltpu.SemaphoreType.DMA((TOPK,))],
-        compiler_params=pltpu.CompilerParams(vmem_limit_bytes=8 * 1024 * 1024),
+        compiler_params=pltpu.CompilerParams(vmem_limit_bytes=57 * 1024 * 1024),
         name="norm",
     )(src, recv, state, gain, *after)
 
@@ -187,9 +246,9 @@
 NT = (((1,), (1,)), ((), ()))
 
 
-def ready_kernel(sizes, *refs):
+def ready_kernel(n_a, n_b, *refs):
     y = refs[0][0, 0]
-    blocks = sum(sizes)
+    blocks = n_a + n_b
     d_in = refs[1 : 1 + blocks]
     wg_in, wu_in, wo_in = refs[1 + blocks : 4 + blocks]
     wp_in = refs[4 + blocks : 8 + blocks]
@@ -208,9 +267,14 @@
         for h in range(2):
             cols = pl.ds(pl.multiple_of(parts[j] + h * FS, FS), FS)
             first.append(start(wp_in[j].at[pl.ds(1024 + h * FS, FS)], wo.at[pl.ds(FS, FS), cols]))
-    for b in range(sizes[0]):
-        first.append(start(d_in[b], da.at[pl.ds(b * ROWS, ROWS)]))
-    second = [start(d_in[sizes[0] + b], db.at[pl.ds(b * ROWS, ROWS)]) for b in range(sizes[1])]
+    at = 0
+    for ref in d_in[:n_a]:
+        first.append(start(ref, da.at[pl.ds(at, ref.shape[0])]))
+        at += ref.shape[0]
+    second, at = [], 0
+    for ref in d_in[n_a:]:
+        second.append(start(ref, db.at[pl.ds(at, ref.shape[0])]))
+        at += ref.shape[0]
     third = [start(wg_in, wg.at[:, pl.ds(0, FS)]), start(wu_in, wu.at[:, pl.ds(0, FS)])]
     for j in range(4):
         rows = pl.ds(parts[j], 512)
@@ -229,8 +293,7 @@
 def make_ready(y, d_a, d_b, weights):
     any_ = pl.BlockSpec(memory_space=pl.ANY)
     vmem = pl.BlockSpec(memory_space=pltpu.VMEM)
-    sizes = (len(d_a), len(d_b))
-    rows = [n * ROWS for n in sizes]
+    rows = [sum(v.shape[0] for v in d_a), sum(v.shape[0] for v in d_b)]
     out_shape = (
         jax.ShapeDtypeStruct((D, 2 * FS), BF16),
         jax.ShapeDtypeStruct((D, 2 * FS), BF16),
@@ -241,15 +304,13 @@
     )
     args = [y, *d_a, *d_b, *weights]
     return pl.pallas_call(
-        functools.partial(ready_kernel, sizes),
+        functools.partial(ready_kernel, len(d_a), len(d_b)),
         out_shape=out_shape,
         in_specs=[pl.BlockSpec(memory_space=pltpu.SMEM)] + [any_] * (len(args) - 1),
         out_specs=tuple(vmem for _ in out_shape),
-        scratch_shapes=[pltpu.VMEM((2 * FS, D), BF16), pltpu.SemaphoreType.DMA((27,))],
+        scratch_shapes=[pltpu.VMEM((2 * FS, D), BF16), pltpu.SemaphoreType.DMA((19 + len(d_a) + len(d_b),))],
         compiler_params=pltpu.CompilerParams(vmem_limit_bytes=READY_VMEM * 1024 * 1024),
-        cost_estimate=pl.CostEstimate(
-            flops=2 * sum(rows) * D * 2 * FS, bytes_accessed=24 * 1024 * 1024, transcendentals=0
-        ),
+        cost_estimate=pl.CostEstimate(flops=1000, bytes_accessed=1000, transcendentals=0),
         name="ready",
     )(*args)
 
@@ -367,6 +428,24 @@
     )(*args)
 
 
+def merge_kernel(own_ref, other_ref, rows_ref, out_ref):
+    for r in range(NR):
+        out_ref[r, :FS] = (own_ref[r] + other_ref[r].astype(F32)).astype(BF16)
+        out_ref[r, FS:] = rows_ref[r]
+
+
+def merge(own, other, rows):
+    vmem = pl.BlockSpec(memory_space=pltpu.VMEM)
+    return pl.pallas_call(
+        merge_kernel,
+        out_shape=jax.ShapeDtypeStruct((NR, FS + 16, FS), BF16),
+        in_specs=[vmem] * 3,
+        out_specs=vmem,
+        compiler_params=pltpu.CompilerParams(vmem_limit_bytes=16 * 1024 * 1024),
+        name="merge",
+    )(own, other, rows)
+
+
 def shards(
     question_emb,
     probes,
@@ -385,38 +464,24 @@
 ):
     dy0 = (soft_weight[:, :, None, None] * cotangent.astype(F32)).astype(BF16).reshape(ROWS, D)
     dyp = pair(dy0)
-    dy_next = ring(dy0, 1)
-    dy_prev = ring(dy0, -1)
-    dy_far = ring(dy0, 2)
-    y = lax.axis_index("reader") // 2
-    y_row = y.astype(I32).reshape(1, 1)
-    piece = jnp.concatenate(
-        [
-            lax.dynamic_slice(w_gate, (y * 512, 0), (512, FS)),
-            lax.dynamic_slice(w_up, (y * 512, 0), (512, FS)),
-            lax.dynamic_slice(w_out, (0, y * 512), (FS, FS)),
-            lax.dynamic_slice(w_out, (0, y * 512 + FS), (FS, FS)),
-        ],
-        axis=0,
+    dy_m = ring(dy0, 1)
+    dy_p = ring(dy0, -1)
+    y_row = (lax.axis_index("reader") // 2).astype(I32).reshape(1, 1)
+
+    msg, src, piece = make_plan(
+        top_passages, probes, passage_home, y_row, question_emb, w_gate, w_up, w_out
     )
     piece = partner(piece)
-
-    msg, src = make_plan(top_passages, probes, passage_home, question_emb)
     asked = lax.all_to_all(msg, "index", 0, 0, tiled=True)
-    slots = asked[:, 6, :CAP].astype(I32)
-    blocks, piece, dyp, dy_next, dy_prev, dy_far = pick_slots(
-        slots, passage_states, piece, dyp, dy_next, dy_prev, dy_far
-    )
+    slots, piece, dyp, dy_m, dy_p = read_asked(asked, piece, dyp, dy_m, dy_p)
+    weights = (w_gate, w_up, w_out, piece, column(piece, -1), column(piece, 2), column(piece, 1))
+    dyp_m = ring(dyp, 1)
+    dyp_p = ring(dyp, -1)
+    (blocks,) = pick_slots(slots, passage_states)
+    blocks, dyp_m, dyp_p = send_after(blocks, dyp_m, dyp_p)
     recv = lax.all_to_all(blocks, "index", 0, 0, tiled=True)
-    dy_a = [dy0, dy_next, dy_prev, dy_far, dyp]
-    dy_b = [ring(dyp, 1), ring(dyp, -1), ring(dyp, 2)]
-    weights = (w_gate, w_up, w_out, piece, column(piece, -1), column(piece, 2), column(piece, 1))
-    gain_row = norm_gain.reshape(1, D)
-    n0 = norm_rows(src, recv, question_state, gain_row, *dy_b)
-    np_ = pair(n0)
-    n_a = [n0, ring(n0, 1), ring(n0, -1), ring(n0, 2), np_]
-    n_b = [ring(np_, 1), ring(np_, -1), ring(np_, 2)]
-
+    dy_a = [dy0, dy_m, dy_p, ring(dy0, 2), dyp]
+    dy_b = [dyp_m, dyp_p, ring(dyp, 2)]
     group_emb = asked[:, :6, :].reshape(NI, 768)
     every_score = (
         jnp.einsum("qe,cse->qcs", group_emb, codes, preferred_element_type=F32) * code_scale[None]
@@ -424,6 +489,12 @@
     local = asked[:, 6, 8 : 8 + NPROBE].astype(I32)
     hot = (local[:, :, None] == jnp.arange(CLUS_DEV, dtype=I32)[None, None, :]).astype(F32)
     picked = jnp.einsum("qpc,qcs->qps", hot, every_score, precision=lax.Precision.HIGHEST)
+
+    gain_row = norm_gain.reshape(1, D)
+    n0 = norm_rows(src, recv, question_state, gain_row, picked)
+    np_ = pair(n0)
+    n_a = [n0, ring(n0, 1), ring(n0, -1), ring(n0, 2), np_]
+    n_b = [ring(np_, 1), ring(np_, -1), ring(np_, 2)]
 
     wg2, wu2, d_rows_a, d_rows_b, d_act_a, d_act_b = make_ready(y_row, dy_a, dy_b, weights)
     acc_a, gain_a = layer(n_a, (wg2, wu2, d_rows_a, d_act_a), FIRST_TILE)
@@ -441,12 +512,11 @@
     gain128 = tail[NPROBE].reshape(NR, 1, 16)
     hi = gain128.astype(BF16)
     lo = (gain128 - hi.astype(F32)).astype(BF16)
-    gain_rows = jnp.pad(jnp.concatenate([hi, lo], axis=2), ((0, 0), (0, 7), (0, FS - 32)))
-    total = (own + from_partner.astype(F32)).astype(BF16)
-    out = lax.all_to_all(jnp.concatenate([total, gain_rows], axis=1), "reader", 0, 0, tiled=True)
-    out = jnp.sum(out.astype(F32), axis=0)
-    grad_out = out[:FS]
-    grad_gain = out[FS, :16] + out[FS, 16:32]
+    gain_rows = jnp.pad(jnp.concatenate([hi, lo], axis=2), ((0, 0), (0, 15), (0, FS - 32)))
+    out = lax.all_to_all(merge(own, from_partner, gain_rows), "reader", 0, 0, tiled=True)
+    grad_out = jnp.sum(out[:, :FS].astype(F32), axis=0)
+    gain_out = jnp.sum(out[:, FS, :32].astype(F32), axis=0)
+    grad_gain = gain_out[:16] + gain_out[16:]
     return probe_scores, grad_out, grad_gain
 
 

time: 183 us -> 178 us (0.973)
  starting transfers between devices: 44.6 us -> 36.8 us
  Pallas kernels: 38.3 us -> 45 us
  waiting for transfers between devices: 47.4 us -> 42.7 us
    ppermute x12, waiting for transfers between devices: 26.6 us -> 16.3 us  [ring(): return lax.ppermute(v, BOTH, pairs_of(ring_move(step)))]
    all_to_all x1, waiting for transfers between devices: 0.01 us -> 8.18 us  [shards(): recv = lax.all_to_all(blocks, 'index', 0, 0, tiled=True)]
    ppermute x2, waiting for transfers between devices: 4.5 us -> 0.01 us  [pair(): return lax.ppermute(v, BOTH, pairs_of(pair_move))]
    all_to_all x1, starting transfers between devices: 8.26 us -> 5.42 us  [shards(): recv = lax.all_to_all(blocks, 'index', 0, 0, tiled=True)]
    pallas_call x1 -> x4, Pallas kernels: 5.23 us -> 8.03 us  [the longest x1 5.48 us: make_ready(): pl.pallas_call(functools.partial(ready_kernel, len(d_a), len(d_b)), out_s...]
    pallas_call x1, Pallas kernels: 3.74 us -> 6.4 us  [pick_slots(): pl.pallas_call(pick_kernel, out_shape=(jax.ShapeDtypeStruct((NI * CAP, LP...]
    unnamed x46 -> x36, local copies, waits for them, and re-layouts: 3.48 us -> 5.99 us
    dynamic_slice x2 -> x0, local copies, waits for them, and re-layouts: 2.12 us -> none  [the longest x1 1.13 us: shards(): lax.dynamic_slice(w_up, (y * 512, 0), (512, FS))]
  transfers between devices with their start and end apart: 21 -> 21, of which waited for: 7 -> 8; matrix products, arithmetic and copies ran while one was open for 5% -> 4% of each run, Pallas kernels for 14% -> 17%
where the time goes in v3:
time: 178 us; the launch traced here: 176 us
  Pallas kernels  45 us (25%)
  waiting for transfers between devices  42.7 us (24%)
  starting transfers between devices  36.8 us (21%)
  blocking collectives  34.4 us (19%)
  local copies, waits for them, and re-layouts  6.83 us (4%)
  matrix products  5.66 us (3%)
  other arithmetic  4.14 us (2%)
    pallas_call x2, Pallas kernels, layer(): pl.pallas_call(functools.partial(layer_kernel, blocks, tile, last), out_s...  23.8 us
    all_to_all x1, blocking collectives, shards(): tail = lax.all_to_all(tail, 'index', 0, 0, tiled=True)  18 us
    all_to_all x1, blocking collectives, shards(): asked = lax.all_to_all(msg, 'index', 0, 0, tiled=True)  16.5 us
    ppermute x12, waiting for transfers between devices, ring(): return lax.ppermute(v, BOTH, pairs_of(ring_move(step)))  16.3 us
    ppermute x12, starting transfers between devices, ring(): return lax.ppermute(v, BOTH, pairs_of(ring_move(step)))  15.4 us
    all_to_all x1, waiting for transfers between devices, shards(): lax.all_to_all(merge(own, from_partner, gain_rows), 'reader', 0, 0, tiled...  15.2 us
    all_to_all x1, waiting for transfers between devices, shards(): recv = lax.all_to_all(blocks, 'index', 0, 0, tiled=True)  8.18 us
    all_to_all x1, starting transfers between devices, shards(): lax.all_to_all(merge(own, from_partner, gain_rows), 'reader', 0, 0, tiled...  6.44 us
  transfers between devices with their start and end apart: 21, of which 8 were waited for; matrix products, arithmetic and copies ran while one was open for 4% of the time, Pallas kernels for 17%

profile of v3, /device:TPU:1, one launch (start us, length us, event | category | flops | bytes accessed | tf_op | source)
XLA Modules:
  0.0 176.4 jit_solution(8751941617086206527)
XLA Ops:
  2.0 3.0 %plan.1 = (bf16[16,8,128]{2,1,0:T(8,128)(2,1)}, s32[1,20]{1,0:T(1,128)}, bf16[1536,256]{1,0:T(8,128)(2,1)}) custom-call(s32[1,20]{1,0:T(1,128)} %top_ref.1, s32[1,32]{1,0:T(1,128)} %probes_ref.1, s32[4096]{0:T(1024)} %home_ref.1, s32[1,1]{1,0:T(1,128)} %bitcast.y_ref.refs_0_, f32[8,128]{1,0:T(8,128)} %pad_convert_fusion.emb_ref, bf16[2048,256]{1,0:T(8,128)(2,1)} %refs_9_.1, ...), custom_call_target="tpu_custom_call" | custom-call | tf_op jit(solution)/shard_map/plan/pallas_call | solution.py:127
  5.0 3.4 %collective-permute-start = (bf16[1536,256]{1,0:T(8,128)(2,1)}, bf16[1536,256]{1,0:T(8,128)(2,1)}, u32[]{:S(2)}, u32[]{:S(2)}) collective-permute-start(bf16[1536,256]{1,0:T(8,128)(2,1)} %get-tuple-element.27), channel_id=1, source_target_pairs={{0,24},{1,97},{2,26},{3,99},{4,28},{5,101},{6,30},{7,103},{8,16},{... | collective-permute-start | bytes 2359304 | tf_op jit(solution)/shard_map/ppermute | solution.py:84
  11.1 2.1 %collective-permute-start.3 = (bf16[160,2048]{1,0:T(8,128)(2,1)}, bf16[160,2048]{1,0:T(8,128)(2,1)S(1)}, u32[]{:S(2)}, u32[]{:S(2)}) collective-permute-start(bf16[160,2048]{1,0:T(8,128)(2,1)} %fusion.refs_1_), channel_id=1, source_target_pairs={{0,96},{1,25},{2,98},{3,27},{4,100},{5,29},{6,102},{7,31},{8,104},... | collective-permute-start | bytes 1966088 | tf_op jit(solution)/shard_map/ppermute | solution.py:71
  13.2 16.5 %all_to_all.20.asked_ref = bf16[16,8,128]{2,1,0:T(8,128)(2,1)} all-to-all(bf16[16,8,128]{2,1,0:T(8,128)(2,1)} %get-tuple-element.25), channel_id=1, replica_groups=mesh['index'=16,'reader'=8] {'index'}, dimensions={0} | all-to-all | bytes 65536 | tf_op jit(solution)/shard_map/all_to_all | solution.py:475
  32.5 2.3 %collective-permute-start.5 = (bf16[160,2048]{1,0:T(8,128)(2,1)}, bf16[160,2048]{1,0:T(8,128)(2,1)S(1)}, u32[]{:S(2)}, u32[]{:S(2)}) collective-permute-start(bf16[160,2048]{1,0:T(8,128)(2,1)} %get-tuple-element.29.refs_5_), channel_id=1, source_target_pairs={{0,96},{1,25},{2,98},{3,27},{4,100},{5,29},{6,102},{7,31},{8,104},... | collective-permute-start | bytes 1966088 | tf_op jit(solution)/shard_map/ppermute | solution.py:71
  34.8 6.4 %pick.1.refs_0_ = bf16[48,8,2048]{2,1,0:T(8,128)(2,1)} custom-call(s32[16,128]{1,0:T(8,128)} %get-tuple-element.28.slot_ref, bf16[256,8,2048]{2,1,0:T(8,128)(2,1)} %states_ref.1), custom_call_target="tpu_custom_call" | custom-call | bytes 3145728 | tf_op jit(solution)/shard_map/pick/pallas_call | solution.py:194
  41.2 2.1 %collective-permute-done.4.refs_1_ = bf16[160,2048]{1,0:T(8,128)(2,1)S(1)} collective-permute-done((bf16[160,2048]{1,0:T(8,128)(2,1)}, bf16[160,2048]{1,0:T(8,128)(2,1)S(1)}, u32[]{:S(2)}, u32[]{:S(2)}) %collective-permute-start.4) | collective-permute-done | bytes 655392 | tf_op jit(solution)/shard_map/ppermute | solution.py:71
  44.9 5.4 %all-to-all-start.1 = ((bf16[48,8,2048]{2,1,0:T(8,128)(2,1)}), bf16[48,8,2048]{2,1,0:T(8,128)(2,1)}, u32[]{:S(2)}, u32[]{:S(2)}) async-start(bf16[48,8,2048]{2,1,0:T(8,128)(2,1)} %get-tuple-element.30), calls=%async_computation.1 | async-start | bytes 3145728 | tf_op jit(solution)/shard_map/all_to_all | solution.py:482
  50.4 2.8 %collective-permute-start.10 = (bf16[160,2048]{1,0:T(8,128)(2,1)}, bf16[160,2048]{1,0:T(8,128)(2,1)}, u32[]{:S(2)}, u32[]{:S(2)}) collective-permute-start(bf16[160,2048]{1,0:T(8,128)(2,1)} %fusion.refs_1_), channel_id=1, source_target_pairs={{0,64},{1,17},{2,66},{3,19},{4,68},{5,21},{6,70},{7,23},{8,72},{9,... | collective-permute-start | bytes 1966088 | tf_op jit(solution)/shard_map/ppermute | solution.py:71
  53.3 2.8 %collective-permute-start.12 = (bf16[1536,256]{1,0:T(8,128)(2,1)}, bf16[1536,256]{1,0:T(8,128)(2,1)}, u32[]{:S(2)}, u32[]{:S(2)}) collective-permute-start(bf16[1536,256]{1,0:T(8,128)(2,1)} %get-tuple-element.35.refs_12_), channel_id=1, source_target_pairs={{0,6},{1,7},{2,0},{3,1},{4,2},{5,3},{6,4},{7,5},{8,14},{9,15},{10,... | collective-permute-start | bytes 2359304 | tf_op jit(solution)/shard_map/ppermute | solution.py:67
  56.8 4.6 %fusion.11 = f32[16,32,128]{2,0,1:T(8,128)S(1)} fusion(bf16[16,768,1]{1,0,2:T(8,128)(2,1)S(1)} %reshape.80, bf16[32,128,768]{2,1,0:T(8,128)(2,1)} %param.16), kind=kOutput, calls=%fused_computation.25 | convolution fusion | flops 100663296 | bytes 6578176 | tf_op jit(solution)/shard_map/qe,cse->qcs/dot_general | solution.py:487
  63.2 8.2 %all-to-all-done.1.recv_ref = bf16[48,8,2048]{2,1,0:T(8,128)(2,1)} async-done(((bf16[48,8,2048]{2,1,0:T(8,128)(2,1)}), bf16[48,8,2048]{2,1,0:T(8,128)(2,1)}, u32[]{:S(2)}, u32[]{:S(2)}) %all-to-all-start.1) | async-done | bytes 1572896 | tf_op jit(solution)/shard_map/all_to_all | solution.py:482
  71.4 3.8 %norm.1.refs_0_ = bf16[160,2048]{1,0:T(8,128)(2,1)} custom-call(s32[1,20]{1,0:T(1,128)} %get-tuple-element.26.src_ref, bf16[48,8,2048]{2,1,0:T(8,128)(2,1)} %all-to-all-done.1.recv_ref, bf16[1,2048]{1,0:T(2,128)(2,1)} %state_ref.1, f32[1,2048]{1,0:T(1,128)} %bitcast.17, f32[16,32,128]{2,1,0:T(8,128)} %fusion.1.refs_0_), custom_call_target="tpu_custom_call" | custom-call | tf_op jit(solution)/shard_map/norm/pallas_call | solution.py:229
  75.2 4.4 %collective-permute-done.10.refs_4_ = bf16[160,2048]{1,0:T(8,128)(2,1)} collective-permute-done((bf16[160,2048]{1,0:T(8,128)(2,1)}, bf16[160,2048]{1,0:T(8,128)(2,1)}, u32[]{:S(2)}, u32[]{:S(2)}) %collective-permute-start.10) | collective-permute-done | bytes 655392 | tf_op jit(solution)/shard_map/ppermute | solution.py:71
  80.0 8.0 %collective-permute-done.11.refs_8_ = bf16[160,2048]{1,0:T(8,128)(2,1)} collective-permute-done((bf16[160,2048]{1,0:T(8,128)(2,1)}, bf16[160,2048]{1,0:T(8,128)(2,1)}, u32[]{:S(2)}, u32[]{:S(2)}) %collective-permute-start.11) | collective-permute-done | bytes 655392 | tf_op jit(solution)/shard_map/ppermute | solution.py:71
  91.2 3.0 %collective-permute-done.14.refs_15_ = bf16[1536,256]{1,0:T(8,128)(2,1)} collective-permute-done((bf16[1536,256]{1,0:T(8,128)(2,1)}, bf16[1536,256]{1,0:T(8,128)(2,1)}, u32[]{:S(2)}, u32[]{:S(2)}) %collective-permute-start.14) | collective-permute-done | bytes 786464 | tf_op jit(solution)/shard_map/ppermute | solution.py:67
  97.5 5.5 %ready.1 = (bf16[2048,512]{1,0:T(8,128)(2,1)S(1)}, bf16[2048,512]{1,0:T(8,128)(2,1)S(1)}, bf16[800,2048]{1,0:T(8,128)(2,1)S(1)}, bf16[480,2048]{1,0:T(8,128)(2,1...) custom-call(s32[1,1]{1,0:T(1,128)} %bitcast.y_ref.refs_0_, bf16[160,2048]{1,0:T(8,128)(2,1)} %fusion.refs_1_, ...), custom_call_target="tpu_custom_call" | custom-call | flops 1000 | bytes 1000 | tf_op jit(solution)/shard_map/ready/pallas_call | solution.py:306
  103.3 2.4 %collective-permute-start.8 = (bf16[160,2048]{1,0:T(8,128)(2,1)S(1)}, bf16[160,2048]{1,0:T(8,128)(2,1)S(1)}, u32[]{:S(2)}, u32[]{:S(2)}) collective-permute-start(bf16[160,2048]{1,0:T(8,128)(2,1)S(1)} %collective-permute-done.6.refs_4_), channel_id=1, source_target_pairs={{0,96},{1,25},{2,98},{3,27},{4,100},{5,29},{6,102},{7,31},{8,104},... | collective-permute-start | bytes 1966088 | tf_op jit(solution)/shard_map/ppermute | solution.py:71
  107.4 14.1 %layer_first.1 = (f32[8,512,256]{2,1,0:T(8,128)S(1)}, f32[1,2048]{1,0:T(1,128)S(1)}) custom-call(bf16[160,2048]{1,0:T(8,128)(2,1)S(1)} %copy-done.11, bf16[160,2048]{1,0:T(8,128)(2,1)S(1)} %collective-permute-done.15.refs_1_, bf16[160,2048]{1,0:T(8,128)(2,1)S(1)} %collective-permute-done.16.refs_2_, bf16[160,2048]{1,0:T(8,128)(2,1)S(1)} %collective-permute-done.17.refs_3_, ...), custom_call_target="tpu_custom_call" | custom-call | flops 8388608000 | bytes 6553600 | tf_op jit(solution)/shard_map/layer_first/pallas_call | solution.py:407
  121.7 9.6 %layer_last.1 = (f32[8,256,256]{2,1,0:T(8,128)S(1)}, bf16[8,256,256]{2,1,0:T(8,128)(2,1)}, f32[1,2048]{1,0:T(1,128)S(1)}) custom-call(bf16[160,2048]{1,0:T(8,128)(2,1)S(1)} %collective-permute-done.7.refs_0_, bf16[160,2048]{1,0:T(8,128)(2,1)S(1)} %collective-permute-done.8.refs_1_, bf16[160,2048]{1,0:T(8,128)(2,1)S(1)} %collective-permute-done.9.refs_2_, ...), custom_call_target="tpu_custom_call" | custom-call | flops 5033164800 | bytes 3932160 | tf_op jit(solution)/shard_map/layer_last/pallas_call | solution.py:407
  131.3 1.9 %collective-permute-start.18 = (bf16[8,256,256]{2,1,0:T(8,128)(2,1)}, bf16[8,256,256]{2,1,0:T(8,128)(2,1)S(1)}, u32[]{:S(2)}, u32[]{:S(2)}) collective-permute-start(bf16[8,256,256]{2,1,0:T(8,128)(2,1)} %get-tuple-element.46), channel_id=1, source_target_pairs={{0,24},{1,97},{2,26},{3,99},{4,28},{5,101},{6,30},{7,103},{8,16},{... | collective-permute-start | bytes 3145736 | tf_op jit(solution)/shard_map/ppermute | solution.py:84
  133.4 18.0 %all_to_all.21 = f32[16,40,128]{2,1,0:T(8,128)S(1)} all-to-all(f32[16,40,128]{2,1,0:T(8,128)S(1)} %maximum_maximum_fusion), channel_id=1, replica_groups=mesh['index'=16,'reader'=8] {'index'}, dimensions={0} | all-to-all | bytes 655360 | tf_op jit(solution)/shard_map/all_to_all | solution.py:509
  152.7 6.4 %all-to-all-start.3 = ((bf16[8,272,256]{2,1,0:T(8,128)(2,1)}), bf16[8,272,256]{2,1,0:T(8,128)(2,1)S(1)}, u32[]{:S(2)}, u32[]{:S(2)}) async-start(bf16[8,272,256]{2,1,0:T(8,128)(2,1)} %merge.1), calls=%async_computation.3 | async-start | bytes 2228224 | tf_op jit(solution)/shard_map/all_to_all | solution.py:516
  159.8 15.2 %all-to-all-done.3 = bf16[8,272,256]{2,1,0:T(8,128)(2,1)S(1)} async-done(((bf16[8,272,256]{2,1,0:T(8,128)(2,1)}), bf16[8,272,256]{2,1,0:T(8,128)(2,1)S(1)}, u32[]{:S(2)}, u32[]{:S(2)}) %all-to-all-start.3) | async-done | bytes 1114144 | tf_op jit(solution)/shard_map/all_to_all | solution.py:516
  (85 shorter events, 23.7 us)
Async XLA Ops:
  5.0 24.7 %collective-permute-start = (bf16[1536,256]{1,0:T(8,128)(2,1)}, bf16[1536,256]{1,0:T(8,128)(2,1)}, u32[]{:S(2)}, u32[]{:S(2)}) collective-permute-start(bf16[1536,256]{1,0:T(8,128)(2,1)} %get-tuple-element.27), channel_id=1, source_target_pairs={{0,24},{1,97},{2,26},{3,99},{4,28},{5,101},{6,30},{7,103},{8,16},{... | collective-permute-start | bytes 2359304 | tf_op jit(solution)/shard_map/ppermute | solution.py:84
  9.5 20.2 %collective-permute-start.1 = (bf16[160,2048]{1,0:T(8,128)(2,1)}, bf16[160,2048]{1,0:T(8,128)(2,1)}, u32[]{:S(2)}, u32[]{:S(2)}) collective-permute-start(bf16[160,2048]{1,0:T(8,128)(2,1)} %fusion.refs_1_), channel_id=1, source_target_pairs={{0,8},{1,33},{2,10},{3,35},{4,12},{5,37},{6,14},{7,39},{8,0},{9,41... | collective-permute-start | bytes 1966088 | tf_op jit(solution)/shard_map/ppermute | solution.py:80
  9.5 20.2 %collective-permute-start.2 = (bf16[160,2048]{1,0:T(8,128)(2,1)}, bf16[160,2048]{1,0:T(8,128)(2,1)S(1)}, u32[]{:S(2)}, u32[]{:S(2)}) collective-permute-start(bf16[160,2048]{1,0:T(8,128)(2,1)} %fusion.refs_1_), channel_id=1, source_target_pairs={{0,32},{1,9},{2,34},{3,11},{4,36},{5,13},{6,38},{7,15},{8,40},{9,1... | collective-permute-start | bytes 1966088 | tf_op jit(solution)/shard_map/ppermute | solution.py:71
  11.1 18.6 %collective-permute-start.3 = (bf16[160,2048]{1,0:T(8,128)(2,1)}, bf16[160,2048]{1,0:T(8,128)(2,1)S(1)}, u32[]{:S(2)}, u32[]{:S(2)}) collective-permute-start(bf16[160,2048]{1,0:T(8,128)(2,1)} %fusion.refs_1_), channel_id=1, source_target_pairs={{0,96},{1,25},{2,98},{3,27},{4,100},{5,29},{6,102},{7,31},{8,104},... | collective-permute-start | bytes 1966088 | tf_op jit(solution)/shard_map/ppermute | solution.py:71
  32.1 11.2 %collective-permute-start.4 = (bf16[160,2048]{1,0:T(8,128)(2,1)}, bf16[160,2048]{1,0:T(8,128)(2,1)S(1)}, u32[]{:S(2)}, u32[]{:S(2)}) collective-permute-start(bf16[160,2048]{1,0:T(8,128)(2,1)} %get-tuple-element.29.refs_5_), channel_id=1, source_target_pairs={{0,32},{1,9},{2,34},{3,11},{4,36},{5,13},{6,38},{7,15},{8,40},{9,1... | collective-permute-start | bytes 1966088 | tf_op jit(solution)/shard_map/ppermute | solution.py:71
  32.5 10.8 %collective-permute-start.5 = (bf16[160,2048]{1,0:T(8,128)(2,1)}, bf16[160,2048]{1,0:T(8,128)(2,1)S(1)}, u32[]{:S(2)}, u32[]{:S(2)}) collective-permute-start(bf16[160,2048]{1,0:T(8,128)(2,1)} %get-tuple-element.29.refs_5_), channel_id=1, source_target_pairs={{0,96},{1,25},{2,98},{3,27},{4,100},{5,29},{6,102},{7,31},{8,104},... | collective-permute-start | bytes 1966088 | tf_op jit(solution)/shard_map/ppermute | solution.py:71
  44.9 26.4 %all-to-all-start.1 = ((bf16[48,8,2048]{2,1,0:T(8,128)(2,1)}), bf16[48,8,2048]{2,1,0:T(8,128)(2,1)}, u32[]{:S(2)}, u32[]{:S(2)}) async-start(bf16[48,8,2048]{2,1,0:T(8,128)(2,1)} %get-tuple-element.30), calls=%async_computation.1 | async-start | bytes 3145728 | tf_op jit(solution)/shard_map/all_to_all | solution.py:482
  50.4 29.3 %collective-permute-start.10 = (bf16[160,2048]{1,0:T(8,128)(2,1)}, bf16[160,2048]{1,0:T(8,128)(2,1)}, u32[]{:S(2)}, u32[]{:S(2)}) collective-permute-start(bf16[160,2048]{1,0:T(8,128)(2,1)} %fusion.refs_1_), channel_id=1, source_target_pairs={{0,64},{1,17},{2,66},{3,19},{4,68},{5,21},{6,70},{7,23},{8,72},{9,... | collective-permute-start | bytes 1966088 | tf_op jit(solution)/shard_map/ppermute | solution.py:71
  53.3 35.9 %collective-permute-start.12 = (bf16[1536,256]{1,0:T(8,128)(2,1)}, bf16[1536,256]{1,0:T(8,128)(2,1)}, u32[]{:S(2)}, u32[]{:S(2)}) collective-permute-start(bf16[1536,256]{1,0:T(8,128)(2,1)} %get-tuple-element.35.refs_12_), channel_id=1, source_target_pairs={{0,6},{1,7},{2,0},{3,1},{4,2},{5,3},{6,4},{7,5},{8,14},{9,15},{10,... | collective-permute-start | bytes 2359304 | tf_op jit(solution)/shard_map/ppermute | solution.py:67
  56.1 34.7 %collective-permute-start.13 = (bf16[1536,256]{1,0:T(8,128)(2,1)}, bf16[1536,256]{1,0:T(8,128)(2,1)}, u32[]{:S(2)}, u32[]{:S(2)}) collective-permute-start(bf16[1536,256]{1,0:T(8,128)(2,1)} %get-tuple-element.35.refs_12_), channel_id=1, source_target_pairs={{0,4},{1,5},{2,6},{3,7},{4,0},{5,1},{6,2},{7,3},{8,12},{9,13},{10,... | collective-permute-start | bytes 2359304 | tf_op jit(solution)/shard_map/ppermute | solution.py:67
  56.5 31.5 %collective-permute-start.11 = (bf16[160,2048]{1,0:T(8,128)(2,1)}, bf16[160,2048]{1,0:T(8,128)(2,1)}, u32[]{:S(2)}, u32[]{:S(2)}) collective-permute-start(bf16[160,2048]{1,0:T(8,128)(2,1)} %get-tuple-element.29.refs_5_), channel_id=1, source_target_pairs={{0,64},{1,17},{2,66},{3,19},{4,68},{5,21},{6,70},{7,23},{8,72},{9,... | collective-permute-start | bytes 1966088 | tf_op jit(solution)/shard_map/ppermute | solution.py:71
  56.8 37.4 %copy-start.2 = (bf16[256,2048]{1,0:T(8,128)(2,1)S(1)}, bf16[256,2048]{1,0:T(8,128)(2,1)}, u32[]{:S(2)}) copy-start(bf16[256,2048]{1,0:T(8,128)(2,1)} %refs_11_.1) | copy-start | bytes 3145732
  61.4 32.8 %copy-start = (bf16[2048,256]{1,0:T(8,128)(2,1)S(1)}, bf16[2048,256]{1,0:T(8,128)(2,1)}, u32[]{:S(2)}) copy-start(bf16[2048,256]{1,0:T(8,128)(2,1)} %refs_9_.1) | copy-start | bytes 3145732
  61.4 32.8 %copy-start.1 = (bf16[2048,256]{1,0:T(8,128)(2,1)S(1)}, bf16[2048,256]{1,0:T(8,128)(2,1)}, u32[]{:S(2)}) copy-start(bf16[2048,256]{1,0:T(8,128)(2,1)} %refs_10_.1) | copy-start | bytes 3145732
  61.4 32.8 %collective-permute-start.14 = (bf16[1536,256]{1,0:T(8,128)(2,1)}, bf16[1536,256]{1,0:T(8,128)(2,1)}, u32[]{:S(2)}, u32[]{:S(2)}) collective-permute-start(bf16[1536,256]{1,0:T(8,128)(2,1)} %get-tuple-element.35.refs_12_), channel_id=1, source_target_pairs={{0,2},{1,3},{2,4},{3,5},{4,6},{5,7},{6,0},{7,1},{8,10},{9,11},{10,... | collective-permute-start | bytes 2359304 | tf_op jit(solution)/shard_map/ppermute | solution.py:67
  79.6 23.3 %collective-permute-start.6 = (bf16[160,2048]{1,0:T(8,128)(2,1)}, bf16[160,2048]{1,0:T(8,128)(2,1)S(1)}, u32[]{:S(2)}, u32[]{:S(2)}) collective-permute-start(bf16[160,2048]{1,0:T(8,128)(2,1)} %norm.1.refs_0_), channel_id=1, source_target_pairs={{0,8},{1,33},{2,10},{3,35},{4,12},{5,37},{6,14},{7,39},{8,0},{9,41... | collective-permute-start | bytes 1966088 | tf_op jit(solution)/shard_map/ppermute | solution.py:80
  88.0 17.7 %collective-permute-start.15 = (bf16[160,2048]{1,0:T(8,128)(2,1)}, bf16[160,2048]{1,0:T(8,128)(2,1)S(1)}, u32[]{:S(2)}, u32[]{:S(2)}) collective-permute-start(bf16[160,2048]{1,0:T(8,128)(2,1)} %norm.1.refs_0_), channel_id=1, source_target_pairs={{0,32},{1,9},{2,34},{3,11},{4,36},{5,13},{6,38},{7,15},{8,40},{9,1... | collective-permute-start | bytes 1966088 | tf_op jit(solution)/shard_map/ppermute | solution.py:71
  89.1 16.6 %collective-permute-start.16 = (bf16[160,2048]{1,0:T(8,128)(2,1)}, bf16[160,2048]{1,0:T(8,128)(2,1)S(1)}, u32[]{:S(2)}, u32[]{:S(2)}) collective-permute-start(bf16[160,2048]{1,0:T(8,128)(2,1)} %norm.1.refs_0_), channel_id=1, source_target_pairs={{0,96},{1,25},{2,98},{3,27},{4,100},{5,29},{6,102},{7,31},{8,104},... | collective-permute-start | bytes 1966088 | tf_op jit(solution)/shard_map/ppermute | solution.py:71
  90.7 16.7 %collective-permute-start.17 = (bf16[160,2048]{1,0:T(8,128)(2,1)}, bf16[160,2048]{1,0:T(8,128)(2,1)S(1)}, u32[]{:S(2)}, u32[]{:S(2)}) collective-permute-start(bf16[160,2048]{1,0:T(8,128)(2,1)} %norm.1.refs_0_), channel_id=1, source_target_pairs={{0,64},{1,17},{2,66},{3,19},{4,68},{5,21},{6,70},{7,23},{8,72},{9,... | collective-permute-start | bytes 1966088 | tf_op jit(solution)/shard_map/ppermute | solution.py:71
  103.0 18.6 %collective-permute-start.7 = (bf16[160,2048]{1,0:T(8,128)(2,1)S(1)}, bf16[160,2048]{1,0:T(8,128)(2,1)S(1)}, u32[]{:S(2)}, u32[]{:S(2)}) collective-permute-start(bf16[160,2048]{1,0:T(8,128)(2,1)S(1)} %collective-permute-done.6.refs_4_), channel_id=1, source_target_pairs={{0,32},{1,9},{2,34},{3,11},{4,36},{5,13},{6,38},{7,15},{8,40},{9,1... | collective-permute-start | bytes 1966088 | tf_op jit(solution)/shard_map/ppermute | solution.py:71
  103.3 18.2 %collective-permute-start.8 = (bf16[160,2048]{1,0:T(8,128)(2,1)S(1)}, bf16[160,2048]{1,0:T(8,128)(2,1)S(1)}, u32[]{:S(2)}, u32[]{:S(2)}) collective-permute-start(bf16[160,2048]{1,0:T(8,128)(2,1)S(1)} %collective-permute-done.6.refs_4_), channel_id=1, source_target_pairs={{0,96},{1,25},{2,98},{3,27},{4,100},{5,29},{6,102},{7,31},{8,104},... | collective-permute-start | bytes 1966088 | tf_op jit(solution)/shard_map/ppermute | solution.py:71
  105.7 15.9 %collective-permute-start.9 = (bf16[160,2048]{1,0:T(8,128)(2,1)S(1)}, bf16[160,2048]{1,0:T(8,128)(2,1)S(1)}, u32[]{:S(2)}, u32[]{:S(2)}) collective-permute-start(bf16[160,2048]{1,0:T(8,128)(2,1)S(1)} %collective-permute-done.6.refs_4_), channel_id=1, source_target_pairs={{0,64},{1,17},{2,66},{3,19},{4,68},{5,21},{6,70},{7,23},{8,72},{9,... | collective-permute-start | bytes 1966088 | tf_op jit(solution)/shard_map/ppermute | solution.py:71
  131.3 20.2 %collective-permute-start.18 = (bf16[8,256,256]{2,1,0:T(8,128)(2,1)}, bf16[8,256,256]{2,1,0:T(8,128)(2,1)S(1)}, u32[]{:S(2)}, u32[]{:S(2)}) collective-permute-start(bf16[8,256,256]{2,1,0:T(8,128)(2,1)} %get-tuple-element.46), channel_id=1, source_target_pairs={{0,24},{1,97},{2,26},{3,99},{4,28},{5,101},{6,30},{7,103},{8,16},{... | collective-permute-start | bytes 3145736 | tf_op jit(solution)/shard_map/ppermute | solution.py:84
  152.7 22.2 %all-to-all-start.3 = ((bf16[8,272,256]{2,1,0:T(8,128)(2,1)}), bf16[8,272,256]{2,1,0:T(8,128)(2,1)S(1)}, u32[]{:S(2)}, u32[]{:S(2)}) async-start(bf16[8,272,256]{2,1,0:T(8,128)(2,1)} %merge.1), calls=%async_computation.3 | async-start | bytes 2228224 | tf_op jit(solution)/shard_map/all_to_all | solution.py:516
  (15 other events, 94.9 us)

commit v4 on v3

--- a/solution.py
+++ b/solution.py
@@ -113,7 +113,10 @@
     for k in range(NPROBE):
         c = probes_ref[0, k]
         vec = jnp.where((owner_id == c // CLUS_DEV) & (lane_id == 8 + k), c % CLUS_DEV, vec)
-    emb = jnp.broadcast_to(emb_ref[...][None], shape)
+    emb = jnp.zeros(shape, F32)
+    for c in range(6):
+        part_c = emb_ref[:, c * 128 : (c + 1) * 128].astype(F32)
+        emb = jnp.where(row_id == c, jnp.broadcast_to(part_c[None], shape), emb)
     msg_ref[...] = jnp.where(row_id == 6, vec.astype(F32), emb).astype(BF16)
     for copy in cuts:
         copy.wait()
@@ -121,7 +124,6 @@
 
 def make_plan(top, probes, home, y, emb, w_gate, w_up, w_out):
     any_ = pl.BlockSpec(memory_space=pl.ANY)
-    emb8 = jnp.pad(emb.astype(F32).reshape(6, 128), ((0, 2), (0, 0)))
     smem = pl.BlockSpec(memory_space=pltpu.SMEM)
     vmem = pl.BlockSpec(memory_space=pltpu.VMEM)
     return pl.pallas_call(
@@ -136,7 +138,7 @@
         scratch_shapes=[pltpu.SemaphoreType.DMA((4,))],
         compiler_params=pltpu.CompilerParams(vmem_limit_bytes=60 * 1024 * 1024),
         name="plan",
-    )(top, probes, home, y, emb8, w_gate, w_up, w_out)
+    )(top, probes, home, y, emb, w_gate, w_up, w_out)
 
 
 def ask_kernel(asked_ref, *refs):
@@ -164,17 +166,17 @@
     pass
 
 
-def send_after(value, *passed):
+def send_after(value, *after):
     any_ = pl.BlockSpec(memory_space=pl.ANY)
-    args = (value, *passed)
     return pl.pallas_call(
         send_kernel,
-        out_shape=tuple(jax.ShapeDtypeStruct(v.shape, v.dtype) for v in args),
-        in_specs=[any_] * len(args),
-        out_specs=tuple(any_ for _ in args),
-        input_output_aliases={i: i for i in range(len(args))},
+        out_shape=jax.ShapeDtypeStruct(value.shape, value.dtype),
+        in_specs=[any_] * (1 + len(after)),
+        out_specs=any_,
+        input_output_aliases={0: 0},
+        compiler_params=pltpu.CompilerParams(vmem_limit_bytes=60 * 1024 * 1024),
         name="send",
-    )(*args)
+    )(value, *after)
 
 
 def pick_kernel(slot_ref, states_ref, *refs):
@@ -478,7 +480,7 @@
     dyp_m = ring(dyp, 1)
     dyp_p = ring(dyp, -1)
     (blocks,) = pick_slots(slots, passage_states)
-    blocks, dyp_m, dyp_p = send_after(blocks, dyp_m, dyp_p)
+    blocks = send_after(blocks, dyp_m, dyp_p)
     recv = lax.all_to_all(blocks, "index", 0, 0, tiled=True)
     dy_a = [dy0, dy_m, dy_p, ring(dy0, 2), dyp]
     dy_b = [dyp_m, dyp_p, ring(dyp, 2)]
@@ -489,6 +491,7 @@
     local = asked[:, 6, 8 : 8 + NPROBE].astype(I32)
     hot = (local[:, :, None] == jnp.arange(CLUS_DEV, dtype=I32)[None, None, :]).astype(F32)
     picked = jnp.einsum("qpc,qcs->qps", hot, every_score, precision=lax.Precision.HIGHEST)
+    picked = picked.astype(BF16)
 
     gain_row = norm_gain.reshape(1, D)
     n0 = norm_rows(src, recv, question_state, gain_row, picked)
@@ -503,13 +506,14 @@
     )
 
     from_partner = partner(par)
-    tail = jnp.concatenate(
-        [picked, gain_part.reshape(NI, 1, 128), jnp.zeros((NI, 7, 128), F32)], axis=1
-    )
+    gain_own = gain_part.reshape(NI, 1, 128)
+    gain_hi = gain_own.astype(BF16)
+    gain_lo = (gain_own - gain_hi.astype(F32)).astype(BF16)
+    tail = jnp.concatenate([picked, gain_hi, gain_lo, jnp.zeros((NI, 6, 128), BF16)], axis=1)
     tail = lax.all_to_all(tail, "index", 0, 0, tiled=True)
-    tail = jnp.sum(tail, axis=0)
+    tail = jnp.sum(tail.astype(F32), axis=0)
     probe_scores = tail[None, :NPROBE]
-    gain128 = tail[NPROBE].reshape(NR, 1, 16)
+    gain128 = (tail[NPROBE] + tail[NPROBE + 1]).reshape(NR, 1, 16)
     hi = gain128.astype(BF16)
     lo = (gain128 - hi.astype(F32)).astype(BF16)
     gain_rows = jnp.pad(jnp.concatenate([hi, lo], axis=2), ((0, 0), (0, 15), (0, FS - 32)))

time: 178 us -> 175 us (0.983)
  no operation moved by 1% of the time
where the time goes in v4:
time: 175 us; the launch traced here: 173 us
  Pallas kernels  44.6 us (25%)
  waiting for transfers between devices  43.2 us (25%)
  starting transfers between devices  36.5 us (21%)
  blocking collectives  32.9 us (19%)
  local copies, waits for them, and re-layouts  6.91 us (4%)
  matrix products  5.61 us (3%)
  other arithmetic  2.82 us (2%)
    pallas_call x2, Pallas kernels, layer(): pl.pallas_call(functools.partial(layer_kernel, blocks, tile, last), out_s...  23.7 us
    ppermute x12, waiting for transfers between devices, ring(): return lax.ppermute(v, BOTH, pairs_of(ring_move(step)))  16.8 us
    all_to_all x1, blocking collectives, shards(): asked = lax.all_to_all(msg, 'index', 0, 0, tiled=True)  16.5 us
    all_to_all x1, blocking collectives, shards(): tail = lax.all_to_all(tail, 'index', 0, 0, tiled=True)  16.5 us
    ppermute x12, starting transfers between devices, ring(): return lax.ppermute(v, BOTH, pairs_of(ring_move(step)))  15.4 us
    all_to_all x1, waiting for transfers between devices, shards(): lax.all_to_all(merge(own, from_partner, gain_rows), 'reader', 0, 0, tiled...  15.2 us
    all_to_all x1, waiting for transfers between devices, shards(): recv = lax.all_to_all(blocks, 'index', 0, 0, tiled=True)  8.23 us
    all_to_all x1, starting transfers between devices, shards(): lax.all_to_all(merge(own, from_partner, gain_rows), 'reader', 0, 0, tiled...  6.23 us
  transfers between devices with their start and end apart: 21, of which 8 were waited for; matrix products, arithmetic and copies ran while one was open for 4% of the time, Pallas kernels for 17%

profile of v4, /device:TPU:1, one launch (start us, length us, event | category | flops | bytes accessed | tf_op | source)
XLA Modules:
  0.0 173.4 jit_solution(8071436722040045462)
XLA Ops:
  0.7 3.1 %plan.1 = (bf16[16,8,128]{2,1,0:T(8,128)(2,1)}, s32[1,20]{1,0:T(1,128)}, bf16[1536,256]{1,0:T(8,128)(2,1)}) custom-call(s32[1,20]{1,0:T(1,128)} %top_ref.1, s32[1,32]{1,0:T(1,128)} %probes_ref.1, s32[4096]{0:T(1024)} %home_ref.1, s32[1,1]{1,0:T(1,128)} %bitcast.y_ref.refs_0_, bf16[1,768]{1,0:T(2,128)(2,1)} %emb_ref.1, bf16[2048,256]{1,0:T(8,128)(2,1)} %refs_9_.1, ...), custom_call_target="tpu_custom_call" | custom-call | tf_op jit(solution)/shard_map/plan/pallas_call | solution.py:129
  3.8 3.4 %collective-permute-start = (bf16[1536,256]{1,0:T(8,128)(2,1)}, bf16[1536,256]{1,0:T(8,128)(2,1)}, u32[]{:S(2)}, u32[]{:S(2)}) collective-permute-start(bf16[1536,256]{1,0:T(8,128)(2,1)} %get-tuple-element.24), channel_id=1, source_target_pairs={{0,24},{1,97},{2,26},{3,99},{4,28},{5,101},{6,30},{7,103},{8,16},{... | collective-permute-start | bytes 2359304 | tf_op jit(solution)/shard_map/ppermute | solution.py:84
  9.9 2.1 %collective-permute-start.3 = (bf16[160,2048]{1,0:T(8,128)(2,1)}, bf16[160,2048]{1,0:T(8,128)(2,1)S(1)}, u32[]{:S(2)}, u32[]{:S(2)}) collective-permute-start(bf16[160,2048]{1,0:T(8,128)(2,1)} %fusion.refs_1_), channel_id=1, source_target_pairs={{0,96},{1,25},{2,98},{3,27},{4,100},{5,29},{6,102},{7,31},{8,104},... | collective-permute-start | bytes 1966088 | tf_op jit(solution)/shard_map/ppermute | solution.py:71
  12.0 16.5 %all_to_all.20.asked_ref = bf16[16,8,128]{2,1,0:T(8,128)(2,1)} all-to-all(bf16[16,8,128]{2,1,0:T(8,128)(2,1)} %get-tuple-element.22), channel_id=1, replica_groups=mesh['index'=16,'reader'=8] {'index'}, dimensions={0} | all-to-all | bytes 65536 | tf_op jit(solution)/shard_map/all_to_all | solution.py:477
  31.3 2.3 %collective-permute-start.5 = (bf16[160,2048]{1,0:T(8,128)(2,1)}, bf16[160,2048]{1,0:T(8,128)(2,1)S(1)}, u32[]{:S(2)}, u32[]{:S(2)}) collective-permute-start(bf16[160,2048]{1,0:T(8,128)(2,1)} %get-tuple-element.26.refs_5_), channel_id=1, source_target_pairs={{0,96},{1,25},{2,98},{3,27},{4,100},{5,29},{6,102},{7,31},{8,104},... | collective-permute-start | bytes 1966088 | tf_op jit(solution)/shard_map/ppermute | solution.py:71
  33.6 5.9 %pick.1.refs_0_ = bf16[48,8,2048]{2,1,0:T(8,128)(2,1)} custom-call(s32[16,128]{1,0:T(8,128)} %get-tuple-element.25.slot_ref, bf16[256,8,2048]{2,1,0:T(8,128)(2,1)} %states_ref.1), custom_call_target="tpu_custom_call" | custom-call | bytes 3145728 | tf_op jit(solution)/shard_map/pick/pallas_call | solution.py:196
  39.4 2.6 %collective-permute-done.4.refs_1_.refs_6_ = bf16[160,2048]{1,0:T(8,128)(2,1)S(1)} collective-permute-done((bf16[160,2048]{1,0:T(8,128)(2,1)}, bf16[160,2048]{1,0:T(8,128)(2,1)S(1)}, u32[]{:S(2)}, u32[]{:S(2)}) %collective-permute-start.4) | collective-permute-done | bytes 655392 | tf_op jit(solution)/shard_map/ppermute | solution.py:71
  43.8 5.3 %all-to-all-start.1 = ((bf16[48,8,2048]{2,1,0:T(8,128)(2,1)}), bf16[48,8,2048]{2,1,0:T(8,128)(2,1)}, u32[]{:S(2)}, u32[]{:S(2)}) async-start(bf16[48,8,2048]{2,1,0:T(8,128)(2,1)} %send.1), calls=%async_computation.1 | async-start | bytes 3145728 | tf_op jit(solution)/shard_map/all_to_all | solution.py:484
  49.2 2.8 %collective-permute-start.10 = (bf16[160,2048]{1,0:T(8,128)(2,1)}, bf16[160,2048]{1,0:T(8,128)(2,1)}, u32[]{:S(2)}, u32[]{:S(2)}) collective-permute-start(bf16[160,2048]{1,0:T(8,128)(2,1)} %fusion.refs_1_), channel_id=1, source_target_pairs={{0,64},{1,17},{2,66},{3,19},{4,68},{5,21},{6,70},{7,23},{8,72},{9,... | collective-permute-start | bytes 1966088 | tf_op jit(solution)/shard_map/ppermute | solution.py:71
  52.0 2.8 %collective-permute-start.12 = (bf16[1536,256]{1,0:T(8,128)(2,1)}, bf16[1536,256]{1,0:T(8,128)(2,1)}, u32[]{:S(2)}, u32[]{:S(2)}) collective-permute-start(bf16[1536,256]{1,0:T(8,128)(2,1)} %get-tuple-element.29.refs_12_), channel_id=1, source_target_pairs={{0,6},{1,7},{2,0},{3,1},{4,2},{5,3},{6,4},{7,5},{8,14},{9,15},{10,... | collective-permute-start | bytes 2359304 | tf_op jit(solution)/shard_map/ppermute | solution.py:67
  55.6 4.6 %fusion.12 = f32[16,32,128]{2,0,1:T(8,128)S(1)} fusion(bf16[16,768,1]{1,0,2:T(8,128)(2,1)S(1)} %reshape.126, bf16[32,128,768]{2,1,0:T(8,128)(2,1)} %param.16), kind=kOutput, calls=%fused_computation.29 | convolution fusion | flops 100663296 | bytes 6578176 | tf_op jit(solution)/shard_map/qe,cse->qcs/dot_general | solution.py:489
  61.9 8.2 %all-to-all-done.1.recv_ref = bf16[48,8,2048]{2,1,0:T(8,128)(2,1)} async-done(((bf16[48,8,2048]{2,1,0:T(8,128)(2,1)}), bf16[48,8,2048]{2,1,0:T(8,128)(2,1)}, u32[]{:S(2)}, u32[]{:S(2)}) %all-to-all-start.1) | async-done | bytes 1572896 | tf_op jit(solution)/shard_map/all_to_all | solution.py:484
  70.2 3.8 %norm.1.refs_0_ = bf16[160,2048]{1,0:T(8,128)(2,1)} custom-call(s32[1,20]{1,0:T(1,128)} %get-tuple-element.23.src_ref, bf16[48,8,2048]{2,1,0:T(8,128)(2,1)} %all-to-all-done.1.recv_ref, bf16[1,2048]{1,0:T(2,128)(2,1)} %state_ref.1, f32[1,2048]{1,0:T(1,128)} %bitcast.23, bf16[16,32,128]{2,1,0:T(8,128)(2,1)} %convolution_convert_fusion.refs_0_), custom_call_target="tpu_custom_call" | custom-call | tf_op jit(solution)/shard_map/norm/pallas_call | solution.py:231
  74.0 4.4 %collective-permute-done.10.refs_4_ = bf16[160,2048]{1,0:T(8,128)(2,1)} collective-permute-done((bf16[160,2048]{1,0:T(8,128)(2,1)}, bf16[160,2048]{1,0:T(8,128)(2,1)}, u32[]{:S(2)}, u32[]{:S(2)}) %collective-permute-start.10) | collective-permute-done | bytes 655392 | tf_op jit(solution)/shard_map/ppermute | solution.py:71
  78.8 8.0 %collective-permute-done.11.refs_8_ = bf16[160,2048]{1,0:T(8,128)(2,1)} collective-permute-done((bf16[160,2048]{1,0:T(8,128)(2,1)}, bf16[160,2048]{1,0:T(8,128)(2,1)}, u32[]{:S(2)}, u32[]{:S(2)}) %collective-permute-start.11) | collective-permute-done | bytes 655392 | tf_op jit(solution)/shard_map/ppermute | solution.py:71
  90.0 3.0 %collective-permute-done.14.refs_15_ = bf16[1536,256]{1,0:T(8,128)(2,1)} collective-permute-done((bf16[1536,256]{1,0:T(8,128)(2,1)}, bf16[1536,256]{1,0:T(8,128)(2,1)}, u32[]{:S(2)}, u32[]{:S(2)}) %collective-permute-start.14) | collective-permute-done | bytes 786464 | tf_op jit(solution)/shard_map/ppermute | solution.py:67
  96.3 5.5 %ready.1 = (bf16[2048,512]{1,0:T(8,128)(2,1)S(1)}, bf16[2048,512]{1,0:T(8,128)(2,1)S(1)}, bf16[800,2048]{1,0:T(8,128)(2,1)S(1)}, bf16[480,2048]{1,0:T(8,128)(2,1...) custom-call(s32[1,1]{1,0:T(1,128)} %bitcast.y_ref.refs_0_, bf16[160,2048]{1,0:T(8,128)(2,1)} %fusion.refs_1_, ...), custom_call_target="tpu_custom_call" | custom-call | flops 1000 | bytes 1000 | tf_op jit(solution)/shard_map/ready/pallas_call | solution.py:308
  102.1 2.4 %collective-permute-start.8 = (bf16[160,2048]{1,0:T(8,128)(2,1)S(1)}, bf16[160,2048]{1,0:T(8,128)(2,1)S(1)}, u32[]{:S(2)}, u32[]{:S(2)}) collective-permute-start(bf16[160,2048]{1,0:T(8,128)(2,1)S(1)} %collective-permute-done.6.refs_4_), channel_id=1, source_target_pairs={{0,96},{1,25},{2,98},{3,27},{4,100},{5,29},{6,102},{7,31},{8,104},... | collective-permute-start | bytes 1966088 | tf_op jit(solution)/shard_map/ppermute | solution.py:71
  106.2 14.1 %layer_first.1 = (f32[8,512,256]{2,1,0:T(8,128)S(1)}, f32[1,2048]{1,0:T(1,128)S(1)}) custom-call(bf16[160,2048]{1,0:T(8,128)(2,1)S(1)} %copy-done.11, bf16[160,2048]{1,0:T(8,128)(2,1)S(1)} %collective-permute-done.15.refs_1_, bf16[160,2048]{1,0:T(8,128)(2,1)S(1)} %collective-permute-done.16.refs_2_, bf16[160,2048]{1,0:T(8,128)(2,1)S(1)} %collective-permute-done.17.refs_3_, ...), custom_call_target="tpu_custom_call" | custom-call | flops 8388608000 | bytes 6553600 | tf_op jit(solution)/shard_map/layer_first/pallas_call | solution.py:409
  120.5 9.6 %layer_last.1 = (f32[8,256,256]{2,1,0:T(8,128)S(1)}, bf16[8,256,256]{2,1,0:T(8,128)(2,1)}, f32[1,2048]{1,0:T(1,128)S(1)}) custom-call(bf16[160,2048]{1,0:T(8,128)(2,1)S(1)} %collective-permute-done.7.refs_0_, bf16[160,2048]{1,0:T(8,128)(2,1)S(1)} %collective-permute-done.8.refs_1_, bf16[160,2048]{1,0:T(8,128)(2,1)S(1)} %collective-permute-done.9.refs_2_, ...), custom_call_target="tpu_custom_call" | custom-call | flops 5033164800 | bytes 3932160 | tf_op jit(solution)/shard_map/layer_last/pallas_call | solution.py:409
  130.1 1.9 %collective-permute-start.18 = (bf16[8,256,256]{2,1,0:T(8,128)(2,1)}, bf16[8,256,256]{2,1,0:T(8,128)(2,1)S(1)}, u32[]{:S(2)}, u32[]{:S(2)}) collective-permute-start(bf16[8,256,256]{2,1,0:T(8,128)(2,1)} %get-tuple-element.40), channel_id=1, source_target_pairs={{0,24},{1,97},{2,26},{3,99},{4,28},{5,101},{6,30},{7,103},{8,16},{... | collective-permute-start | bytes 3145736 | tf_op jit(solution)/shard_map/ppermute | solution.py:84
  132.1 16.5 %all_to_all.21 = bf16[16,40,128]{2,1,0:T(8,128)(2,1)S(1)} all-to-all(bf16[16,40,128]{2,1,0:T(8,128)(2,1)S(1)} %maximum_maximum_fusion), channel_id=1, replica_groups=mesh['index'=16,'reader'=8] {'index'}, dimensions={0} | all-to-all | bytes 327680 | tf_op jit(solution)/shard_map/all_to_all | solution.py:513
  149.9 6.2 %all-to-all-start.3 = ((bf16[8,272,256]{2,1,0:T(8,128)(2,1)}), bf16[8,272,256]{2,1,0:T(8,128)(2,1)S(1)}, u32[]{:S(2)}, u32[]{:S(2)}) async-start(bf16[8,272,256]{2,1,0:T(8,128)(2,1)} %merge.1), calls=%async_computation.3 | async-start | bytes 2228224 | tf_op jit(solution)/shard_map/all_to_all | solution.py:520
  156.8 15.2 %all-to-all-done.3 = bf16[8,272,256]{2,1,0:T(8,128)(2,1)S(1)} async-done(((bf16[8,272,256]{2,1,0:T(8,128)(2,1)}), bf16[8,272,256]{2,1,0:T(8,128)(2,1)S(1)}, u32[]{:S(2)}, u32[]{:S(2)}) %all-to-all-start.3) | async-done | bytes 1114144 | tf_op jit(solution)/shard_map/all_to_all | solution.py:520
  (85 shorter events, 22.4 us)
Async XLA Ops:
  3.8 24.7 %collective-permute-start = (bf16[1536,256]{1,0:T(8,128)(2,1)}, bf16[1536,256]{1,0:T(8,128)(2,1)}, u32[]{:S(2)}, u32[]{:S(2)}) collective-permute-start(bf16[1536,256]{1,0:T(8,128)(2,1)} %get-tuple-element.24), channel_id=1, source_target_pairs={{0,24},{1,97},{2,26},{3,99},{4,28},{5,101},{6,30},{7,103},{8,16},{... | collective-permute-start | bytes 2359304 | tf_op jit(solution)/shard_map/ppermute | solution.py:84
  8.2 20.2 %collective-permute-start.1 = (bf16[160,2048]{1,0:T(8,128)(2,1)}, bf16[160,2048]{1,0:T(8,128)(2,1)}, u32[]{:S(2)}, u32[]{:S(2)}) collective-permute-start(bf16[160,2048]{1,0:T(8,128)(2,1)} %fusion.refs_1_), channel_id=1, source_target_pairs={{0,8},{1,33},{2,10},{3,35},{4,12},{5,37},{6,14},{7,39},{8,0},{9,41... | collective-permute-start | bytes 1966088 | tf_op jit(solution)/shard_map/ppermute | solution.py:80
  8.2 20.2 %collective-permute-start.2 = (bf16[160,2048]{1,0:T(8,128)(2,1)}, bf16[160,2048]{1,0:T(8,128)(2,1)S(1)}, u32[]{:S(2)}, u32[]{:S(2)}) collective-permute-start(bf16[160,2048]{1,0:T(8,128)(2,1)} %fusion.refs_1_), channel_id=1, source_target_pairs={{0,32},{1,9},{2,34},{3,11},{4,36},{5,13},{6,38},{7,15},{8,40},{9,1... | collective-permute-start | bytes 1966088 | tf_op jit(solution)/shard_map/ppermute | solution.py:71
  9.9 18.6 %collective-permute-start.3 = (bf16[160,2048]{1,0:T(8,128)(2,1)}, bf16[160,2048]{1,0:T(8,128)(2,1)S(1)}, u32[]{:S(2)}, u32[]{:S(2)}) collective-permute-start(bf16[160,2048]{1,0:T(8,128)(2,1)} %fusion.refs_1_), channel_id=1, source_target_pairs={{0,96},{1,25},{2,98},{3,27},{4,100},{5,29},{6,102},{7,31},{8,104},... | collective-permute-start | bytes 1966088 | tf_op jit(solution)/shard_map/ppermute | solution.py:71
  30.9 11.2 %collective-permute-start.4 = (bf16[160,2048]{1,0:T(8,128)(2,1)}, bf16[160,2048]{1,0:T(8,128)(2,1)S(1)}, u32[]{:S(2)}, u32[]{:S(2)}) collective-permute-start(bf16[160,2048]{1,0:T(8,128)(2,1)} %get-tuple-element.26.refs_5_), channel_id=1, source_target_pairs={{0,32},{1,9},{2,34},{3,11},{4,36},{5,13},{6,38},{7,15},{8,40},{9,1... | collective-permute-start | bytes 1966088 | tf_op jit(solution)/shard_map/ppermute | solution.py:71
  31.3 10.8 %collective-permute-start.5 = (bf16[160,2048]{1,0:T(8,128)(2,1)}, bf16[160,2048]{1,0:T(8,128)(2,1)S(1)}, u32[]{:S(2)}, u32[]{:S(2)}) collective-permute-start(bf16[160,2048]{1,0:T(8,128)(2,1)} %get-tuple-element.26.refs_5_), channel_id=1, source_target_pairs={{0,96},{1,25},{2,98},{3,27},{4,100},{5,29},{6,102},{7,31},{8,104},... | collective-permute-start | bytes 1966088 | tf_op jit(solution)/shard_map/ppermute | solution.py:71
  43.8 26.3 %all-to-all-start.1 = ((bf16[48,8,2048]{2,1,0:T(8,128)(2,1)}), bf16[48,8,2048]{2,1,0:T(8,128)(2,1)}, u32[]{:S(2)}, u32[]{:S(2)}) async-start(bf16[48,8,2048]{2,1,0:T(8,128)(2,1)} %send.1), calls=%async_computation.1 | async-start | bytes 3145728 | tf_op jit(solution)/shard_map/all_to_all | solution.py:484
  49.2 29.3 %collective-permute-start.10 = (bf16[160,2048]{1,0:T(8,128)(2,1)}, bf16[160,2048]{1,0:T(8,128)(2,1)}, u32[]{:S(2)}, u32[]{:S(2)}) collective-permute-start(bf16[160,2048]{1,0:T(8,128)(2,1)} %fusion.refs_1_), channel_id=1, source_target_pairs={{0,64},{1,17},{2,66},{3,19},{4,68},{5,21},{6,70},{7,23},{8,72},{9,... | collective-permute-start | bytes 1966088 | tf_op jit(solution)/shard_map/ppermute | solution.py:71
  52.0 35.9 %collective-permute-start.12 = (bf16[1536,256]{1,0:T(8,128)(2,1)}, bf16[1536,256]{1,0:T(8,128)(2,1)}, u32[]{:S(2)}, u32[]{:S(2)}) collective-permute-start(bf16[1536,256]{1,0:T(8,128)(2,1)} %get-tuple-element.29.refs_12_), channel_id=1, source_target_pairs={{0,6},{1,7},{2,0},{3,1},{4,2},{5,3},{6,4},{7,5},{8,14},{9,15},{10,... | collective-permute-start | bytes 2359304 | tf_op jit(solution)/shard_map/ppermute | solution.py:67
  54.8 34.7 %collective-permute-start.13 = (bf16[1536,256]{1,0:T(8,128)(2,1)}, bf16[1536,256]{1,0:T(8,128)(2,1)}, u32[]{:S(2)}, u32[]{:S(2)}) collective-permute-start(bf16[1536,256]{1,0:T(8,128)(2,1)} %get-tuple-element.29.refs_12_), channel_id=1, source_target_pairs={{0,4},{1,5},{2,6},{3,7},{4,0},{5,1},{6,2},{7,3},{8,12},{9,13},{10,... | collective-permute-start | bytes 2359304 | tf_op jit(solution)/shard_map/ppermute | solution.py:67
  55.3 31.5 %collective-permute-start.11 = (bf16[160,2048]{1,0:T(8,128)(2,1)}, bf16[160,2048]{1,0:T(8,128)(2,1)}, u32[]{:S(2)}, u32[]{:S(2)}) collective-permute-start(bf16[160,2048]{1,0:T(8,128)(2,1)} %get-tuple-element.26.refs_5_), channel_id=1, source_target_pairs={{0,64},{1,17},{2,66},{3,19},{4,68},{5,21},{6,70},{7,23},{8,72},{9,... | collective-permute-start | bytes 1966088 | tf_op jit(solution)/shard_map/ppermute | solution.py:71
  55.6 37.4 %copy-start.2 = (bf16[256,2048]{1,0:T(8,128)(2,1)S(1)}, bf16[256,2048]{1,0:T(8,128)(2,1)}, u32[]{:S(2)}) copy-start(bf16[256,2048]{1,0:T(8,128)(2,1)} %refs_11_.1) | copy-start | bytes 3145732
  60.2 32.8 %copy-start = (bf16[2048,256]{1,0:T(8,128)(2,1)S(1)}, bf16[2048,256]{1,0:T(8,128)(2,1)}, u32[]{:S(2)}) copy-start(bf16[2048,256]{1,0:T(8,128)(2,1)} %refs_9_.1) | copy-start | bytes 3145732
  60.2 32.8 %copy-start.1 = (bf16[2048,256]{1,0:T(8,128)(2,1)S(1)}, bf16[2048,256]{1,0:T(8,128)(2,1)}, u32[]{:S(2)}) copy-start(bf16[2048,256]{1,0:T(8,128)(2,1)} %refs_10_.1) | copy-start | bytes 3145732
  60.2 32.8 %collective-permute-start.14 = (bf16[1536,256]{1,0:T(8,128)(2,1)}, bf16[1536,256]{1,0:T(8,128)(2,1)}, u32[]{:S(2)}, u32[]{:S(2)}) collective-permute-start(bf16[1536,256]{1,0:T(8,128)(2,1)} %get-tuple-element.29.refs_12_), channel_id=1, source_target_pairs={{0,2},{1,3},{2,4},{3,5},{4,6},{5,7},{6,0},{7,1},{8,10},{9,11},{10,... | collective-permute-start | bytes 2359304 | tf_op jit(solution)/shard_map/ppermute | solution.py:67
  78.4 23.3 %collective-permute-start.6 = (bf16[160,2048]{1,0:T(8,128)(2,1)}, bf16[160,2048]{1,0:T(8,128)(2,1)S(1)}, u32[]{:S(2)}, u32[]{:S(2)}) collective-permute-start(bf16[160,2048]{1,0:T(8,128)(2,1)} %norm.1.refs_0_), channel_id=1, source_target_pairs={{0,8},{1,33},{2,10},{3,35},{4,12},{5,37},{6,14},{7,39},{8,0},{9,41... | collective-permute-start | bytes 1966088 | tf_op jit(solution)/shard_map/ppermute | solution.py:80
  86.8 17.7 %collective-permute-start.15 = (bf16[160,2048]{1,0:T(8,128)(2,1)}, bf16[160,2048]{1,0:T(8,128)(2,1)S(1)}, u32[]{:S(2)}, u32[]{:S(2)}) collective-permute-start(bf16[160,2048]{1,0:T(8,128)(2,1)} %norm.1.refs_0_), channel_id=1, source_target_pairs={{0,32},{1,9},{2,34},{3,11},{4,36},{5,13},{6,38},{7,15},{8,40},{9,1... | collective-permute-start | bytes 1966088 | tf_op jit(solution)/shard_map/ppermute | solution.py:71
  87.9 16.6 %collective-permute-start.16 = (bf16[160,2048]{1,0:T(8,128)(2,1)}, bf16[160,2048]{1,0:T(8,128)(2,1)S(1)}, u32[]{:S(2)}, u32[]{:S(2)}) collective-permute-start(bf16[160,2048]{1,0:T(8,128)(2,1)} %norm.1.refs_0_), channel_id=1, source_target_pairs={{0,96},{1,25},{2,98},{3,27},{4,100},{5,29},{6,102},{7,31},{8,104},... | collective-permute-start | bytes 1966088 | tf_op jit(solution)/shard_map/ppermute | solution.py:71
  89.5 16.7 %collective-permute-start.17 = (bf16[160,2048]{1,0:T(8,128)(2,1)}, bf16[160,2048]{1,0:T(8,128)(2,1)S(1)}, u32[]{:S(2)}, u32[]{:S(2)}) collective-permute-start(bf16[160,2048]{1,0:T(8,128)(2,1)} %norm.1.refs_0_), channel_id=1, source_target_pairs={{0,64},{1,17},{2,66},{3,19},{4,68},{5,21},{6,70},{7,23},{8,72},{9,... | collective-permute-start | bytes 1966088 | tf_op jit(solution)/shard_map/ppermute | solution.py:71
  101.8 18.6 %collective-permute-start.7 = (bf16[160,2048]{1,0:T(8,128)(2,1)S(1)}, bf16[160,2048]{1,0:T(8,128)(2,1)S(1)}, u32[]{:S(2)}, u32[]{:S(2)}) collective-permute-start(bf16[160,2048]{1,0:T(8,128)(2,1)S(1)} %collective-permute-done.6.refs_4_), channel_id=1, source_target_pairs={{0,32},{1,9},{2,34},{3,11},{4,36},{5,13},{6,38},{7,15},{8,40},{9,1... | collective-permute-start | bytes 1966088 | tf_op jit(solution)/shard_map/ppermute | solution.py:71
  102.1 18.2 %collective-permute-start.8 = (bf16[160,2048]{1,0:T(8,128)(2,1)S(1)}, bf16[160,2048]{1,0:T(8,128)(2,1)S(1)}, u32[]{:S(2)}, u32[]{:S(2)}) collective-permute-start(bf16[160,2048]{1,0:T(8,128)(2,1)S(1)} %collective-permute-done.6.refs_4_), channel_id=1, source_target_pairs={{0,96},{1,25},{2,98},{3,27},{4,100},{5,29},{6,102},{7,31},{8,104},... | collective-permute-start | bytes 1966088 | tf_op jit(solution)/shard_map/ppermute | solution.py:71
  104.5 15.9 %collective-permute-start.9 = (bf16[160,2048]{1,0:T(8,128)(2,1)S(1)}, bf16[160,2048]{1,0:T(8,128)(2,1)S(1)}, u32[]{:S(2)}, u32[]{:S(2)}) collective-permute-start(bf16[160,2048]{1,0:T(8,128)(2,1)S(1)} %collective-permute-done.6.refs_4_), channel_id=1, source_target_pairs={{0,64},{1,17},{2,66},{3,19},{4,68},{5,21},{6,70},{7,23},{8,72},{9,... | collective-permute-start | bytes 1966088 | tf_op jit(solution)/shard_map/ppermute | solution.py:71
  130.1 18.7 %collective-permute-start.18 = (bf16[8,256,256]{2,1,0:T(8,128)(2,1)}, bf16[8,256,256]{2,1,0:T(8,128)(2,1)S(1)}, u32[]{:S(2)}, u32[]{:S(2)}) collective-permute-start(bf16[8,256,256]{2,1,0:T(8,128)(2,1)} %get-tuple-element.40), channel_id=1, source_target_pairs={{0,24},{1,97},{2,26},{3,99},{4,28},{5,101},{6,30},{7,103},{8,16},{... | collective-permute-start | bytes 3145736 | tf_op jit(solution)/shard_map/ppermute | solution.py:84
  149.9 22.0 %all-to-all-start.3 = ((bf16[8,272,256]{2,1,0:T(8,128)(2,1)}), bf16[8,272,256]{2,1,0:T(8,128)(2,1)S(1)}, u32[]{:S(2)}, u32[]{:S(2)}) async-start(bf16[8,272,256]{2,1,0:T(8,128)(2,1)} %merge.1), calls=%async_computation.3 | async-start | bytes 2228224 | tf_op jit(solution)/shard_map/all_to_all | solution.py:520
  (15 other events, 92.4 us)

commit v5 on v4

--- a/solution.py
+++ b/solution.py
@@ -141,25 +141,26 @@
     )(top, probes, home, y, emb, w_gate, w_up, w_out)
 
 
-def ask_kernel(asked_ref, *refs):
-    slot_ref = refs[len(refs) // 2]
+def ask_kernel(passed, asked_ref, *refs):
+    slot_ref = refs[-1 - passed]
     slot_ref[...] = asked_ref[:, 6, :].astype(F32).astype(I32)
 
 
-def read_asked(asked, *passed):
+def read_asked(asked, passed, after):
     any_ = pl.BlockSpec(memory_space=pl.ANY)
     vmem = pl.BlockSpec(memory_space=pltpu.VMEM)
     return pl.pallas_call(
-        ask_kernel,
+        functools.partial(ask_kernel, len(passed)),
         out_shape=(
             jax.ShapeDtypeStruct((NI, 128), I32),
             *(jax.ShapeDtypeStruct(v.shape, v.dtype) for v in passed),
         ),
-        in_specs=[vmem] + [any_] * len(passed),
+        in_specs=[vmem] + [any_] * (len(passed) + len(after)),
         out_specs=(vmem, *(any_ for _ in passed)),
         input_output_aliases={1 + i: 1 + i for i in range(len(passed))},
+        compiler_params=pltpu.CompilerParams(vmem_limit_bytes=48 * 1024 * 1024),
         name="ask",
-    )(asked, *passed)
+    )(asked, *passed, *after)
 
 
 def send_kernel(*refs):
@@ -475,7 +476,7 @@
     )
     piece = partner(piece)
     asked = lax.all_to_all(msg, "index", 0, 0, tiled=True)
-    slots, piece, dyp, dy_m, dy_p = read_asked(asked, piece, dyp, dy_m, dy_p)
+    slots, piece, dyp = read_asked(asked, (piece, dyp), (dy_m, dy_p))
     weights = (w_gate, w_up, w_out, piece, column(piece, -1), column(piece, 2), column(piece, 1))
     dyp_m = ring(dyp, 1)
     dyp_p = ring(dyp, -1)

time: 175 us -> 173 us (0.989)
  waiting for transfers between devices: 43.2 us -> 40.4 us
  starting transfers between devices: 36.5 us -> 38.6 us
  transfers between devices with their start and end apart: 21 -> 21, of which waited for: 8 -> 7; matrix products, arithmetic and copies ran while one was open for 4% -> 5% of each run, Pallas kernels for 17% -> 17%
where the time goes in v5:
time: 173 us; the launch traced here: 172 us
  Pallas kernels  43.8 us (25%)
  waiting for transfers between devices  40.4 us (23%)
  starting transfers between devices  38.6 us (22%)
  blocking collectives  33.5 us (19%)
  local copies, waits for them, and re-layouts  6.61 us (4%)
  matrix products  5.61 us (3%)
  other arithmetic  2.82 us (2%)
    pallas_call x2, Pallas kernels, layer(): pl.pallas_call(functools.partial(layer_kernel, blocks, tile, last), out_s...  23.7 us
    all_to_all x1, blocking collectives, shards(): asked = lax.all_to_all(msg, 'index', 0, 0, tiled=True)  17.6 us
    ppermute x12, starting transfers between devices, ring(): return lax.ppermute(v, BOTH, pairs_of(ring_move(step)))  17.2 us
    all_to_all x1, blocking collectives, shards(): tail = lax.all_to_all(tail, 'index', 0, 0, tiled=True)  15.9 us
    ppermute x12, waiting for transfers between devices, ring(): return lax.ppermute(v, BOTH, pairs_of(ring_move(step)))  15.7 us
    all_to_all x1, waiting for transfers between devices, shards(): lax.all_to_all(merge(own, from_partner, gain_rows), 'reader', 0, 0, tiled...  15.2 us
    all_to_all x1, waiting for transfers between devices, shards(): recv = lax.all_to_all(blocks, 'index', 0, 0, tiled=True)  7.38 us
    pallas_call x1, Pallas kernels, pick_slots(): pl.pallas_call(pick_kernel, out_shape=(jax.ShapeDtypeStruct((NI * CAP, LP...  6.41 us
  transfers between devices with their start and end apart: 21, of which 7 were waited for; matrix products, arithmetic and copies ran while one was open for 5% of the time, Pallas kernels for 17%

profile of v5, /device:TPU:1, one launch (start us, length us, event | category | flops | bytes accessed | tf_op | source)
XLA Modules:
  0.0 172.2 jit_solution(5286772210940222763)
XLA Ops:
  0.7 3.1 %plan.1 = (bf16[16,8,128]{2,1,0:T(8,128)(2,1)}, s32[1,20]{1,0:T(1,128)}, bf16[1536,256]{1,0:T(8,128)(2,1)}) custom-call(s32[1,20]{1,0:T(1,128)} %top_ref.1, s32[1,32]{1,0:T(1,128)} %probes_ref.1, s32[4096]{0:T(1024)} %home_ref.1, s32[1,1]{1,0:T(1,128)} %bitcast.y_ref.refs_0_, bf16[1,768]{1,0:T(2,128)(2,1)} %emb_ref.1, bf16[2048,256]{1,0:T(8,128)(2,1)} %refs_9_.1, ...), custom_call_target="tpu_custom_call" | custom-call | tf_op jit(solution)/shard_map/plan/pallas_call | solution.py:129
  3.8 3.4 %collective-permute-start = (bf16[1536,256]{1,0:T(8,128)(2,1)}, bf16[1536,256]{1,0:T(8,128)(2,1)}, u32[]{:S(2)}, u32[]{:S(2)}) collective-permute-start(bf16[1536,256]{1,0:T(8,128)(2,1)} %get-tuple-element.22), channel_id=1, source_target_pairs={{0,24},{1,97},{2,26},{3,99},{4,28},{5,101},{6,30},{7,103},{8,16},{... | collective-permute-start | bytes 2359304 | tf_op jit(solution)/shard_map/ppermute | solution.py:84
  9.9 2.1 %collective-permute-start.3 = (bf16[160,2048]{1,0:T(8,128)(2,1)}, bf16[160,2048]{1,0:T(8,128)(2,1)S(1)}, u32[]{:S(2)}, u32[]{:S(2)}) collective-permute-start(bf16[160,2048]{1,0:T(8,128)(2,1)} %fusion.refs_1_), channel_id=1, source_target_pairs={{0,96},{1,25},{2,98},{3,27},{4,100},{5,29},{6,102},{7,31},{8,104},... | collective-permute-start | bytes 1966088 | tf_op jit(solution)/shard_map/ppermute | solution.py:71
  12.0 17.6 %all_to_all.20.asked_ref = bf16[16,8,128]{2,1,0:T(8,128)(2,1)S(1)} all-to-all(bf16[16,8,128]{2,1,0:T(8,128)(2,1)} %get-tuple-element.20), channel_id=1, replica_groups=mesh['index'=16,'reader'=8] {'index'}, dimensions={0} | all-to-all | bytes 65536 | tf_op jit(solution)/shard_map/all_to_all | solution.py:478
  30.9 2.1 %collective-permute-start.5 = (bf16[160,2048]{1,0:T(8,128)(2,1)}, bf16[160,2048]{1,0:T(8,128)(2,1)S(1)}, u32[]{:S(2)}, u32[]{:S(2)}) collective-permute-start(bf16[160,2048]{1,0:T(8,128)(2,1)} %get-tuple-element.24.refs_5_), channel_id=1, source_target_pairs={{0,96},{1,25},{2,98},{3,27},{4,100},{5,29},{6,102},{7,31},{8,104},... | collective-permute-start | bytes 1966088 | tf_op jit(solution)/shard_map/ppermute | solution.py:71
  33.1 6.4 %pick.1.refs_0_ = bf16[48,8,2048]{2,1,0:T(8,128)(2,1)} custom-call(s32[16,128]{1,0:T(8,128)} %copy-done.13, bf16[256,8,2048]{2,1,0:T(8,128)(2,1)} %states_ref.1), custom_call_target="tpu_custom_call" | custom-call | bytes 3145728 | tf_op jit(solution)/shard_map/pick/pallas_call | solution.py:197
  39.5 2.1 %collective-permute-done.4.refs_1_.refs_6_ = bf16[160,2048]{1,0:T(8,128)(2,1)S(1)} collective-permute-done((bf16[160,2048]{1,0:T(8,128)(2,1)}, bf16[160,2048]{1,0:T(8,128)(2,1)S(1)}, u32[]{:S(2)}, u32[]{:S(2)}) %collective-permute-start.4) | collective-permute-done | bytes 655392 | tf_op jit(solution)/shard_map/ppermute | solution.py:71
  43.3 4.6 %all-to-all-start.1 = ((bf16[48,8,2048]{2,1,0:T(8,128)(2,1)}), bf16[48,8,2048]{2,1,0:T(8,128)(2,1)}, u32[]{:S(2)}, u32[]{:S(2)}) async-start(bf16[48,8,2048]{2,1,0:T(8,128)(2,1)} %send.1), calls=%async_computation.1 | async-start | bytes 3145728 | tf_op jit(solution)/shard_map/all_to_all | solution.py:485
  47.9 2.8 %collective-permute-start.10 = (bf16[160,2048]{1,0:T(8,128)(2,1)}, bf16[160,2048]{1,0:T(8,128)(2,1)}, u32[]{:S(2)}, u32[]{:S(2)}) collective-permute-start(bf16[160,2048]{1,0:T(8,128)(2,1)} %fusion.refs_1_), channel_id=1, source_target_pairs={{0,64},{1,17},{2,66},{3,19},{4,68},{5,21},{6,70},{7,23},{8,72},{9,... | collective-permute-start | bytes 1966088 | tf_op jit(solution)/shard_map/ppermute | solution.py:71
  50.8 2.8 %collective-permute-start.12 = (bf16[1536,256]{1,0:T(8,128)(2,1)}, bf16[1536,256]{1,0:T(8,128)(2,1)}, u32[]{:S(2)}, u32[]{:S(2)}) collective-permute-start(bf16[1536,256]{1,0:T(8,128)(2,1)} %get-tuple-element.25.refs_12_), channel_id=1, source_target_pairs={{0,6},{1,7},{2,0},{3,1},{4,2},{5,3},{6,4},{7,5},{8,14},{9,15},{10,... | collective-permute-start | bytes 2359304 | tf_op jit(solution)/shard_map/ppermute | solution.py:67
  54.4 4.6 %fusion.12 = f32[16,32,128]{2,0,1:T(8,128)S(1)} fusion(bf16[16,768,1]{1,0,2:T(8,128)(2,1)S(1)} %reshape.126, bf16[32,128,768]{2,1,0:T(8,128)(2,1)} %param.16), kind=kOutput, calls=%fused_computation.29 | convolution fusion | flops 100663296 | bytes 6578176 | tf_op jit(solution)/shard_map/qe,cse->qcs/dot_general | solution.py:490
  60.7 7.4 %all-to-all-done.1.recv_ref = bf16[48,8,2048]{2,1,0:T(8,128)(2,1)} async-done(((bf16[48,8,2048]{2,1,0:T(8,128)(2,1)}), bf16[48,8,2048]{2,1,0:T(8,128)(2,1)}, u32[]{:S(2)}, u32[]{:S(2)}) %all-to-all-start.1) | async-done | bytes 1572896 | tf_op jit(solution)/shard_map/all_to_all | solution.py:485
  68.1 3.8 %norm.1.refs_0_ = bf16[160,2048]{1,0:T(8,128)(2,1)} custom-call(s32[1,20]{1,0:T(1,128)} %get-tuple-element.21.src_ref, bf16[48,8,2048]{2,1,0:T(8,128)(2,1)} %all-to-all-done.1.recv_ref, bf16[1,2048]{1,0:T(2,128)(2,1)} %state_ref.1, f32[1,2048]{1,0:T(1,128)} %bitcast.24, bf16[16,32,128]{2,1,0:T(8,128)(2,1)} %convolution_convert_fusion.refs_0_), custom_call_target="tpu_custom_call" | custom-call | tf_op jit(solution)/shard_map/norm/pallas_call | solution.py:232
  71.9 4.9 %collective-permute-done.10.refs_4_ = bf16[160,2048]{1,0:T(8,128)(2,1)} collective-permute-done((bf16[160,2048]{1,0:T(8,128)(2,1)}, bf16[160,2048]{1,0:T(8,128)(2,1)}, u32[]{:S(2)}, u32[]{:S(2)}) %collective-permute-start.10) | collective-permute-done | bytes 655392 | tf_op jit(solution)/shard_map/ppermute | solution.py:71
  77.5 7.3 %collective-permute-done.11.refs_8_ = bf16[160,2048]{1,0:T(8,128)(2,1)} collective-permute-done((bf16[160,2048]{1,0:T(8,128)(2,1)}, bf16[160,2048]{1,0:T(8,128)(2,1)}, u32[]{:S(2)}, u32[]{:S(2)}) %collective-permute-start.11) | collective-permute-done | bytes 655392 | tf_op jit(solution)/shard_map/ppermute | solution.py:71
  87.5 2.1 %collective-permute-start.17 = (bf16[160,2048]{1,0:T(8,128)(2,1)}, bf16[160,2048]{1,0:T(8,128)(2,1)S(1)}, u32[]{:S(2)}, u32[]{:S(2)}) collective-permute-start(bf16[160,2048]{1,0:T(8,128)(2,1)} %norm.1.refs_0_), channel_id=1, source_target_pairs={{0,64},{1,17},{2,66},{3,19},{4,68},{5,21},{6,70},{7,23},{8,72},{9,... | collective-permute-start | bytes 1966088 | tf_op jit(solution)/shard_map/ppermute | solution.py:71
  95.0 5.5 %ready.1 = (bf16[2048,512]{1,0:T(8,128)(2,1)S(1)}, bf16[2048,512]{1,0:T(8,128)(2,1)S(1)}, bf16[800,2048]{1,0:T(8,128)(2,1)S(1)}, bf16[480,2048]{1,0:T(8,128)(2,1...) custom-call(s32[1,1]{1,0:T(1,128)} %bitcast.y_ref.refs_0_, bf16[160,2048]{1,0:T(8,128)(2,1)} %fusion.refs_1_, ...), custom_call_target="tpu_custom_call" | custom-call | flops 1000 | bytes 1000 | tf_op jit(solution)/shard_map/ready/pallas_call | solution.py:309
  100.9 2.4 %collective-permute-start.8 = (bf16[160,2048]{1,0:T(8,128)(2,1)S(1)}, bf16[160,2048]{1,0:T(8,128)(2,1)S(1)}, u32[]{:S(2)}, u32[]{:S(2)}) collective-permute-start(bf16[160,2048]{1,0:T(8,128)(2,1)S(1)} %collective-permute-done.6.refs_4_), channel_id=1, source_target_pairs={{0,96},{1,25},{2,98},{3,27},{4,100},{5,29},{6,102},{7,31},{8,104},... | collective-permute-start | bytes 1966088 | tf_op jit(solution)/shard_map/ppermute | solution.py:71
  104.8 14.1 %layer_first.1 = (f32[8,512,256]{2,1,0:T(8,128)S(1)}, f32[1,2048]{1,0:T(1,128)S(1)}) custom-call(bf16[160,2048]{1,0:T(8,128)(2,1)S(1)} %copy-done.11, bf16[160,2048]{1,0:T(8,128)(2,1)S(1)} %collective-permute-done.15.refs_1_, bf16[160,2048]{1,0:T(8,128)(2,1)S(1)} %collective-permute-done.16.refs_2_, bf16[160,2048]{1,0:T(8,128)(2,1)S(1)} %collective-permute-done.17.refs_3_, ...), custom_call_target="tpu_custom_call" | custom-call | flops 8388608000 | bytes 6553600 | tf_op jit(solution)/shard_map/layer_first/pallas_call | solution.py:410
  119.0 9.6 %layer_last.1 = (f32[8,256,256]{2,1,0:T(8,128)S(1)}, bf16[8,256,256]{2,1,0:T(8,128)(2,1)}, f32[1,2048]{1,0:T(1,128)S(1)}) custom-call(bf16[160,2048]{1,0:T(8,128)(2,1)S(1)} %collective-permute-done.7.refs_0_, bf16[160,2048]{1,0:T(8,128)(2,1)S(1)} %collective-permute-done.8.refs_1_, bf16[160,2048]{1,0:T(8,128)(2,1)S(1)} %collective-permute-done.9.refs_2_, ...), custom_call_target="tpu_custom_call" | custom-call | flops 5033164800 | bytes 3932160 | tf_op jit(solution)/shard_map/layer_last/pallas_call | solution.py:410
  128.6 2.7 %collective-permute-start.18 = (bf16[8,256,256]{2,1,0:T(8,128)(2,1)}, bf16[8,256,256]{2,1,0:T(8,128)(2,1)S(1)}, u32[]{:S(2)}, u32[]{:S(2)}) collective-permute-start(bf16[8,256,256]{2,1,0:T(8,128)(2,1)} %get-tuple-element.36), channel_id=1, source_target_pairs={{0,24},{1,97},{2,26},{3,99},{4,28},{5,101},{6,30},{7,103},{8,16},{... | collective-permute-start | bytes 3145736 | tf_op jit(solution)/shard_map/ppermute | solution.py:84
  131.4 15.9 %all_to_all.21 = bf16[16,40,128]{2,1,0:T(8,128)(2,1)S(1)} all-to-all(bf16[16,40,128]{2,1,0:T(8,128)(2,1)S(1)} %maximum_maximum_fusion), channel_id=1, replica_groups=mesh['index'=16,'reader'=8] {'index'}, dimensions={0} | all-to-all | bytes 327680 | tf_op jit(solution)/shard_map/all_to_all | solution.py:514
  148.7 6.2 %all-to-all-start.3 = ((bf16[8,272,256]{2,1,0:T(8,128)(2,1)}), bf16[8,272,256]{2,1,0:T(8,128)(2,1)S(1)}, u32[]{:S(2)}, u32[]{:S(2)}) async-start(bf16[8,272,256]{2,1,0:T(8,128)(2,1)} %merge.1), calls=%async_computation.3 | async-start | bytes 2228224 | tf_op jit(solution)/shard_map/all_to_all | solution.py:521
  155.5 15.2 %all-to-all-done.3 = bf16[8,272,256]{2,1,0:T(8,128)(2,1)S(1)} async-done(((bf16[8,272,256]{2,1,0:T(8,128)(2,1)}), bf16[8,272,256]{2,1,0:T(8,128)(2,1)S(1)}, u32[]{:S(2)}, u32[]{:S(2)}) %all-to-all-start.3) | async-done | bytes 1114144 | tf_op jit(solution)/shard_map/all_to_all | solution.py:521
  (85 shorter events, 22.5 us)
Async XLA Ops:
  3.8 25.8 %collective-permute-start = (bf16[1536,256]{1,0:T(8,128)(2,1)}, bf16[1536,256]{1,0:T(8,128)(2,1)}, u32[]{:S(2)}, u32[]{:S(2)}) collective-permute-start(bf16[1536,256]{1,0:T(8,128)(2,1)} %get-tuple-element.22), channel_id=1, source_target_pairs={{0,24},{1,97},{2,26},{3,99},{4,28},{5,101},{6,30},{7,103},{8,16},{... | collective-permute-start | bytes 2359304 | tf_op jit(solution)/shard_map/ppermute | solution.py:84
  8.2 21.3 %collective-permute-start.2 = (bf16[160,2048]{1,0:T(8,128)(2,1)}, bf16[160,2048]{1,0:T(8,128)(2,1)S(1)}, u32[]{:S(2)}, u32[]{:S(2)}) collective-permute-start(bf16[160,2048]{1,0:T(8,128)(2,1)} %fusion.refs_1_), channel_id=1, source_target_pairs={{0,32},{1,9},{2,34},{3,11},{4,36},{5,13},{6,38},{7,15},{8,40},{9,1... | collective-permute-start | bytes 1966088 | tf_op jit(solution)/shard_map/ppermute | solution.py:71
  9.9 19.7 %collective-permute-start.3 = (bf16[160,2048]{1,0:T(8,128)(2,1)}, bf16[160,2048]{1,0:T(8,128)(2,1)S(1)}, u32[]{:S(2)}, u32[]{:S(2)}) collective-permute-start(bf16[160,2048]{1,0:T(8,128)(2,1)} %fusion.refs_1_), channel_id=1, source_target_pairs={{0,96},{1,25},{2,98},{3,27},{4,100},{5,29},{6,102},{7,31},{8,104},... | collective-permute-start | bytes 1966088 | tf_op jit(solution)/shard_map/ppermute | solution.py:71
  12.0 17.6 %collective-permute-start.1 = (bf16[160,2048]{1,0:T(8,128)(2,1)}, bf16[160,2048]{1,0:T(8,128)(2,1)}, u32[]{:S(2)}, u32[]{:S(2)}) collective-permute-start(bf16[160,2048]{1,0:T(8,128)(2,1)} %fusion.refs_1_), channel_id=1, source_target_pairs={{0,8},{1,33},{2,10},{3,35},{4,12},{5,37},{6,14},{7,39},{8,0},{9,41... | collective-permute-start | bytes 1966088 | tf_op jit(solution)/shard_map/ppermute | solution.py:80
  30.4 11.2 %collective-permute-start.4 = (bf16[160,2048]{1,0:T(8,128)(2,1)}, bf16[160,2048]{1,0:T(8,128)(2,1)S(1)}, u32[]{:S(2)}, u32[]{:S(2)}) collective-permute-start(bf16[160,2048]{1,0:T(8,128)(2,1)} %get-tuple-element.24.refs_5_), channel_id=1, source_target_pairs={{0,32},{1,9},{2,34},{3,11},{4,36},{5,13},{6,38},{7,15},{8,40},{9,1... | collective-permute-start | bytes 1966088 | tf_op jit(solution)/shard_map/ppermute | solution.py:71
  30.9 10.6 %collective-permute-start.5 = (bf16[160,2048]{1,0:T(8,128)(2,1)}, bf16[160,2048]{1,0:T(8,128)(2,1)S(1)}, u32[]{:S(2)}, u32[]{:S(2)}) collective-permute-start(bf16[160,2048]{1,0:T(8,128)(2,1)} %get-tuple-element.24.refs_5_), channel_id=1, source_target_pairs={{0,96},{1,25},{2,98},{3,27},{4,100},{5,29},{6,102},{7,31},{8,104},... | collective-permute-start | bytes 1966088 | tf_op jit(solution)/shard_map/ppermute | solution.py:71
  43.3 24.8 %all-to-all-start.1 = ((bf16[48,8,2048]{2,1,0:T(8,128)(2,1)}), bf16[48,8,2048]{2,1,0:T(8,128)(2,1)}, u32[]{:S(2)}, u32[]{:S(2)}) async-start(bf16[48,8,2048]{2,1,0:T(8,128)(2,1)} %send.1), calls=%async_computation.1 | async-start | bytes 3145728 | tf_op jit(solution)/shard_map/all_to_all | solution.py:485
  47.9 28.9 %collective-permute-start.10 = (bf16[160,2048]{1,0:T(8,128)(2,1)}, bf16[160,2048]{1,0:T(8,128)(2,1)}, u32[]{:S(2)}, u32[]{:S(2)}) collective-permute-start(bf16[160,2048]{1,0:T(8,128)(2,1)} %fusion.refs_1_), channel_id=1, source_target_pairs={{0,64},{1,17},{2,66},{3,19},{4,68},{5,21},{6,70},{7,23},{8,72},{9,... | collective-permute-start | bytes 1966088 | tf_op jit(solution)/shard_map/ppermute | solution.py:71
  50.8 35.3 %collective-permute-start.12 = (bf16[1536,256]{1,0:T(8,128)(2,1)}, bf16[1536,256]{1,0:T(8,128)(2,1)}, u32[]{:S(2)}, u32[]{:S(2)}) collective-permute-start(bf16[1536,256]{1,0:T(8,128)(2,1)} %get-tuple-element.25.refs_12_), channel_id=1, source_target_pairs={{0,6},{1,7},{2,0},{3,1},{4,2},{5,3},{6,4},{7,5},{8,14},{9,15},{10,... | collective-permute-start | bytes 2359304 | tf_op jit(solution)/shard_map/ppermute | solution.py:67
  53.6 33.9 %collective-permute-start.13 = (bf16[1536,256]{1,0:T(8,128)(2,1)}, bf16[1536,256]{1,0:T(8,128)(2,1)}, u32[]{:S(2)}, u32[]{:S(2)}) collective-permute-start(bf16[1536,256]{1,0:T(8,128)(2,1)} %get-tuple-element.25.refs_12_), channel_id=1, source_target_pairs={{0,4},{1,5},{2,6},{3,7},{4,0},{5,1},{6,2},{7,3},{8,12},{9,13},{10,... | collective-permute-start | bytes 2359304 | tf_op jit(solution)/shard_map/ppermute | solution.py:67
  54.1 30.7 %collective-permute-start.11 = (bf16[160,2048]{1,0:T(8,128)(2,1)}, bf16[160,2048]{1,0:T(8,128)(2,1)}, u32[]{:S(2)}, u32[]{:S(2)}) collective-permute-start(bf16[160,2048]{1,0:T(8,128)(2,1)} %get-tuple-element.24.refs_5_), channel_id=1, source_target_pairs={{0,64},{1,17},{2,66},{3,19},{4,68},{5,21},{6,70},{7,23},{8,72},{9,... | collective-permute-start | bytes 1966088 | tf_op jit(solution)/shard_map/ppermute | solution.py:71
  54.4 37.4 %copy-start.2 = (bf16[256,2048]{1,0:T(8,128)(2,1)S(1)}, bf16[256,2048]{1,0:T(8,128)(2,1)}, u32[]{:S(2)}) copy-start(bf16[256,2048]{1,0:T(8,128)(2,1)} %refs_11_.1) | copy-start | bytes 3145732
  59.0 32.8 %copy-start = (bf16[2048,256]{1,0:T(8,128)(2,1)S(1)}, bf16[2048,256]{1,0:T(8,128)(2,1)}, u32[]{:S(2)}) copy-start(bf16[2048,256]{1,0:T(8,128)(2,1)} %refs_9_.1) | copy-start | bytes 3145732
  59.0 32.8 %copy-start.1 = (bf16[2048,256]{1,0:T(8,128)(2,1)S(1)}, bf16[2048,256]{1,0:T(8,128)(2,1)}, u32[]{:S(2)}) copy-start(bf16[2048,256]{1,0:T(8,128)(2,1)} %refs_10_.1) | copy-start | bytes 3145732
  59.0 32.8 %collective-permute-start.14 = (bf16[1536,256]{1,0:T(8,128)(2,1)}, bf16[1536,256]{1,0:T(8,128)(2,1)}, u32[]{:S(2)}, u32[]{:S(2)}) collective-permute-start(bf16[1536,256]{1,0:T(8,128)(2,1)} %get-tuple-element.25.refs_12_), channel_id=1, source_target_pairs={{0,2},{1,3},{2,4},{3,5},{4,6},{5,7},{6,0},{7,1},{8,10},{9,11},{10,... | collective-permute-start | bytes 2359304 | tf_op jit(solution)/shard_map/ppermute | solution.py:67
  76.8 23.7 %collective-permute-start.6 = (bf16[160,2048]{1,0:T(8,128)(2,1)}, bf16[160,2048]{1,0:T(8,128)(2,1)S(1)}, u32[]{:S(2)}, u32[]{:S(2)}) collective-permute-start(bf16[160,2048]{1,0:T(8,128)(2,1)} %norm.1.refs_0_), channel_id=1, source_target_pairs={{0,8},{1,33},{2,10},{3,35},{4,12},{5,37},{6,14},{7,39},{8,0},{9,41... | collective-permute-start | bytes 1966088 | tf_op jit(solution)/shard_map/ppermute | solution.py:80
  84.8 18.5 %collective-permute-start.15 = (bf16[160,2048]{1,0:T(8,128)(2,1)}, bf16[160,2048]{1,0:T(8,128)(2,1)S(1)}, u32[]{:S(2)}, u32[]{:S(2)}) collective-permute-start(bf16[160,2048]{1,0:T(8,128)(2,1)} %norm.1.refs_0_), channel_id=1, source_target_pairs={{0,32},{1,9},{2,34},{3,11},{4,36},{5,13},{6,38},{7,15},{8,40},{9,1... | collective-permute-start | bytes 1966088 | tf_op jit(solution)/shard_map/ppermute | solution.py:71
  86.1 17.2 %collective-permute-start.16 = (bf16[160,2048]{1,0:T(8,128)(2,1)}, bf16[160,2048]{1,0:T(8,128)(2,1)S(1)}, u32[]{:S(2)}, u32[]{:S(2)}) collective-permute-start(bf16[160,2048]{1,0:T(8,128)(2,1)} %norm.1.refs_0_), channel_id=1, source_target_pairs={{0,96},{1,25},{2,98},{3,27},{4,100},{5,29},{6,102},{7,31},{8,104},... | collective-permute-start | bytes 1966088 | tf_op jit(solution)/shard_map/ppermute | solution.py:71
  87.5 17.3 %collective-permute-start.17 = (bf16[160,2048]{1,0:T(8,128)(2,1)}, bf16[160,2048]{1,0:T(8,128)(2,1)S(1)}, u32[]{:S(2)}, u32[]{:S(2)}) collective-permute-start(bf16[160,2048]{1,0:T(8,128)(2,1)} %norm.1.refs_0_), channel_id=1, source_target_pairs={{0,64},{1,17},{2,66},{3,19},{4,68},{5,21},{6,70},{7,23},{8,72},{9,... | collective-permute-start | bytes 1966088 | tf_op jit(solution)/shard_map/ppermute | solution.py:71
  100.5 18.4 %collective-permute-start.7 = (bf16[160,2048]{1,0:T(8,128)(2,1)S(1)}, bf16[160,2048]{1,0:T(8,128)(2,1)S(1)}, u32[]{:S(2)}, u32[]{:S(2)}) collective-permute-start(bf16[160,2048]{1,0:T(8,128)(2,1)S(1)} %collective-permute-done.6.refs_4_), channel_id=1, source_target_pairs={{0,32},{1,9},{2,34},{3,11},{4,36},{5,13},{6,38},{7,15},{8,40},{9,1... | collective-permute-start | bytes 1966088 | tf_op jit(solution)/shard_map/ppermute | solution.py:71
  100.9 18.0 %collective-permute-start.8 = (bf16[160,2048]{1,0:T(8,128)(2,1)S(1)}, bf16[160,2048]{1,0:T(8,128)(2,1)S(1)}, u32[]{:S(2)}, u32[]{:S(2)}) collective-permute-start(bf16[160,2048]{1,0:T(8,128)(2,1)S(1)} %collective-permute-done.6.refs_4_), channel_id=1, source_target_pairs={{0,96},{1,25},{2,98},{3,27},{4,100},{5,29},{6,102},{7,31},{8,104},... | collective-permute-start | bytes 1966088 | tf_op jit(solution)/shard_map/ppermute | solution.py:71
  103.3 15.7 %collective-permute-start.9 = (bf16[160,2048]{1,0:T(8,128)(2,1)S(1)}, bf16[160,2048]{1,0:T(8,128)(2,1)S(1)}, u32[]{:S(2)}, u32[]{:S(2)}) collective-permute-start(bf16[160,2048]{1,0:T(8,128)(2,1)S(1)} %collective-permute-done.6.refs_4_), channel_id=1, source_target_pairs={{0,64},{1,17},{2,66},{3,19},{4,68},{5,21},{6,70},{7,23},{8,72},{9,... | collective-permute-start | bytes 1966088 | tf_op jit(solution)/shard_map/ppermute | solution.py:71
  128.6 19.0 %collective-permute-start.18 = (bf16[8,256,256]{2,1,0:T(8,128)(2,1)}, bf16[8,256,256]{2,1,0:T(8,128)(2,1)S(1)}, u32[]{:S(2)}, u32[]{:S(2)}) collective-permute-start(bf16[8,256,256]{2,1,0:T(8,128)(2,1)} %get-tuple-element.36), channel_id=1, source_target_pairs={{0,24},{1,97},{2,26},{3,99},{4,28},{5,101},{6,30},{7,103},{8,16},{... | collective-permute-start | bytes 3145736 | tf_op jit(solution)/shard_map/ppermute | solution.py:84
  148.7 22.0 %all-to-all-start.3 = ((bf16[8,272,256]{2,1,0:T(8,128)(2,1)}), bf16[8,272,256]{2,1,0:T(8,128)(2,1)S(1)}, u32[]{:S(2)}, u32[]{:S(2)}) async-start(bf16[8,272,256]{2,1,0:T(8,128)(2,1)} %merge.1), calls=%async_computation.3 | async-start | bytes 2228224 | tf_op jit(solution)/shard_map/all_to_all | solution.py:521
  (15 other events, 86.6 us)

commit v6 on v5

--- a/solution.py
+++ b/solution.py
@@ -476,7 +476,7 @@
     )
     piece = partner(piece)
     asked = lax.all_to_all(msg, "index", 0, 0, tiled=True)
-    slots, piece, dyp = read_asked(asked, (piece, dyp), (dy_m, dy_p))
+    slots, piece = read_asked(asked, (piece,), (dyp, dy_m, dy_p))
     weights = (w_gate, w_up, w_out, piece, column(piece, -1), column(piece, 2), column(piece, 1))
     dyp_m = ring(dyp, 1)
     dyp_p = ring(dyp, -1)

time: 173 us -> 178 us (1.029)
  starting transfers between devices: 38.6 us -> 43.9 us
  waiting for transfers between devices: 40.4 us -> 38.3 us
    ppermute x12, waiting for transfers between devices: 15.7 us -> 10.4 us  [ring(): return lax.ppermute(v, BOTH, pairs_of(ring_move(step)))]
    all_to_all x1, waiting for transfers between devices: 7.38 us -> 10.1 us  [shards(): recv = lax.all_to_all(blocks, 'index', 0, 0, tiled=True)]
    ppermute x2, starting transfers between devices: 0.67 us -> 2.72 us  [pair(): return lax.ppermute(v, BOTH, pairs_of(pair_move))]
    unnamed x36 -> x32, local copies, waits for them, and re-layouts: 5.79 us -> 7.31 us
  transfers between devices with their start and end apart: 21 -> 21, of which waited for: 7 -> 6; matrix products, arithmetic and copies ran while one was open for 5% -> 4% of each run, Pallas kernels for 17% -> 18%
where the time goes in v6:
time: 178 us
  starting transfers between devices  43.9 us (25%)
  Pallas kernels  43.2 us (24%)
  waiting for transfers between devices  38.3 us (22%)
  blocking collectives  34 us (19%)
  local copies, waits for them, and re-layouts  8.13 us (5%)
  matrix products  5.61 us (3%)
  other arithmetic  3.92 us (2%)
    pallas_call x2, Pallas kernels, layer(): pl.pallas_call(functools.partial(layer_kernel, blocks, tile, last), out_s...  23.8 us
    ppermute x12, starting transfers between devices, ring(): return lax.ppermute(v, BOTH, pairs_of(ring_move(step)))  18.8 us
    all_to_all x1, blocking collectives, shards(): asked = lax.all_to_all(msg, 'index', 0, 0, tiled=True)  18.3 us
    all_to_all x1, blocking collectives, shards(): tail = lax.all_to_all(tail, 'index', 0, 0, tiled=True)  15.7 us
    all_to_all x1, waiting for transfers between devices, shards(): lax.all_to_all(merge(own, from_partner, gain_rows), 'reader', 0, 0, tiled...  15.2 us
    ppermute x12, waiting for transfers between devices, ring(): return lax.ppermute(v, BOTH, pairs_of(ring_move(step)))  10.4 us
    all_to_all x1, waiting for transfers between devices, shards(): recv = lax.all_to_all(blocks, 'index', 0, 0, tiled=True)  10.1 us
    all_to_all x1, starting transfers between devices, shards(): lax.all_to_all(merge(own, from_partner, gain_rows), 'reader', 0, 0, tiled...  7.33 us
  transfers between devices with their start and end apart: 21, of which 6 were waited for; matrix products, arithmetic and copies ran while one was open for 4% of the time, Pallas kernels for 18%

profile of v6, /device:TPU:1, one launch (start us, length us, event | category | flops | bytes accessed | tf_op | source)
XLA Modules:
  0.0 177.9 jit_solution(9560701265644125091)
XLA Ops:
  0.6 2.1 %fusion.refs_1_ = bf16[160,2048]{1,0:T(8,128)(2,1)} fusion(bf16[1,20,8,2048]{3,2,1,0:T(8,128)(2,1)} %param.27, f32[20]{0:T(128)} %bitcast.29), kind=kLoop, calls=%fused_computation.3 | loop fusion | flops 983040 | bytes 1310800 | tf_op jit(solution)/shard_map/reshape | solution.py:468
  2.7 2.0 %collective-permute-start.1 = (bf16[160,2048]{1,0:T(8,128)(2,1)}, bf16[160,2048]{1,0:T(8,128)(2,1)}, u32[]{:S(2)}, u32[]{:S(2)}) collective-permute-start(bf16[160,2048]{1,0:T(8,128)(2,1)} %fusion.refs_1_), channel_id=1, source_target_pairs={{0,8},{1,33},{2,10},{3,35},{4,12},{5,37},{6,14},{7,39},{8,0},{9,41... | collective-permute-start | bytes 1966088 | tf_op jit(solution)/shard_map/ppermute | solution.py:80
  4.8 3.0 %plan.1 = (bf16[16,8,128]{2,1,0:T(8,128)(2,1)}, s32[1,20]{1,0:T(1,128)}, bf16[1536,256]{1,0:T(8,128)(2,1)}) custom-call(s32[1,20]{1,0:T(1,128)} %top_ref.1, s32[1,32]{1,0:T(1,128)} %probes_ref.1, s32[4096]{0:T(1024)} %home_ref.1, s32[1,1]{1,0:T(1,128)} %bitcast.y_ref.refs_0_, bf16[1,768]{1,0:T(2,128)(2,1)} %emb_ref.1, bf16[2048,256]{1,0:T(8,128)(2,1)} %refs_9_.1, ...), custom_call_target="tpu_custom_call" | custom-call | tf_op jit(solution)/shard_map/plan/pallas_call | solution.py:129
  11.3 2.1 %collective-permute-start.3 = (bf16[160,2048]{1,0:T(8,128)(2,1)}, bf16[160,2048]{1,0:T(8,128)(2,1)S(1)}, u32[]{:S(2)}, u32[]{:S(2)}) collective-permute-start(bf16[160,2048]{1,0:T(8,128)(2,1)} %fusion.refs_1_), channel_id=1, source_target_pairs={{0,96},{1,25},{2,98},{3,27},{4,100},{5,29},{6,102},{7,31},{8,104},... | collective-permute-start | bytes 1966088 | tf_op jit(solution)/shard_map/ppermute | solution.py:71
  15.3 2.7 %collective-permute-start.5 = (bf16[160,2048]{1,0:T(8,128)(2,1)}, bf16[160,2048]{1,0:T(8,128)(2,1)S(1)}, u32[]{:S(2)}, u32[]{:S(2)}) collective-permute-start(bf16[160,2048]{1,0:T(8,128)(2,1)} %collective-permute-done.1.refs_1_.refs_5_), channel_id=1, source_target_pairs={{0,96},{1,25},{2,98},{3,27},{4,100},{5,29},{6,102},{7,31},{8,104},... | collective-permute-start | bytes 1966088 | tf_op jit(solution)/shard_map/ppermute | solution.py:71
  18.0 18.3 %all_to_all.20.asked_ref = bf16[16,8,128]{2,1,0:T(8,128)(2,1)S(1)} all-to-all(bf16[16,8,128]{2,1,0:T(8,128)(2,1)} %get-tuple-element.19), channel_id=1, replica_groups=mesh['index'=16,'reader'=8] {'index'}, dimensions={0} | all-to-all | bytes 65536 | tf_op jit(solution)/shard_map/all_to_all | solution.py:478
  38.7 5.9 %pick.1.refs_0_ = bf16[48,8,2048]{2,1,0:T(8,128)(2,1)} custom-call(s32[16,128]{1,0:T(8,128)} %copy-done.13, bf16[256,8,2048]{2,1,0:T(8,128)(2,1)} %states_ref.1), custom_call_target="tpu_custom_call" | custom-call | bytes 3145728 | tf_op jit(solution)/shard_map/pick/pallas_call | solution.py:197
  46.3 6.2 %all-to-all-start.1 = ((bf16[48,8,2048]{2,1,0:T(8,128)(2,1)}), bf16[48,8,2048]{2,1,0:T(8,128)(2,1)}, u32[]{:S(2)}, u32[]{:S(2)}) async-start(bf16[48,8,2048]{2,1,0:T(8,128)(2,1)} %send.1), calls=%async_computation.1 | async-start | bytes 3145728 | tf_op jit(solution)/shard_map/all_to_all | solution.py:485
  52.6 2.8 %collective-permute-start.10 = (bf16[160,2048]{1,0:T(8,128)(2,1)}, bf16[160,2048]{1,0:T(8,128)(2,1)}, u32[]{:S(2)}, u32[]{:S(2)}) collective-permute-start(bf16[160,2048]{1,0:T(8,128)(2,1)} %fusion.refs_1_), channel_id=1, source_target_pairs={{0,64},{1,17},{2,66},{3,19},{4,68},{5,21},{6,70},{7,23},{8,72},{9,... | collective-permute-start | bytes 1966088 | tf_op jit(solution)/shard_map/ppermute | solution.py:71
  55.4 2.8 %collective-permute-start.12 = (bf16[1536,256]{1,0:T(8,128)(2,1)}, bf16[1536,256]{1,0:T(8,128)(2,1)}, u32[]{:S(2)}, u32[]{:S(2)}) collective-permute-start(bf16[1536,256]{1,0:T(8,128)(2,1)} %get-tuple-element.23.refs_12_), channel_id=1, source_target_pairs={{0,6},{1,7},{2,0},{3,1},{4,2},{5,3},{6,4},{7,5},{8,14},{9,15},{10,... | collective-permute-start | bytes 2359304 | tf_op jit(solution)/shard_map/ppermute | solution.py:67
  59.0 4.6 %fusion.12 = f32[16,32,128]{2,0,1:T(8,128)S(1)} fusion(bf16[16,768,1]{1,0,2:T(8,128)(2,1)S(1)} %reshape.126, bf16[32,128,768]{2,1,0:T(8,128)(2,1)} %param.16), kind=kOutput, calls=%fused_computation.29 | convolution fusion | flops 100663296 | bytes 6578176 | tf_op jit(solution)/shard_map/qe,cse->qcs/dot_general | solution.py:490
  65.3 10.1 %all-to-all-done.1.recv_ref = bf16[48,8,2048]{2,1,0:T(8,128)(2,1)} async-done(((bf16[48,8,2048]{2,1,0:T(8,128)(2,1)}), bf16[48,8,2048]{2,1,0:T(8,128)(2,1)}, u32[]{:S(2)}, u32[]{:S(2)}) %all-to-all-start.1) | async-done | bytes 1572896 | tf_op jit(solution)/shard_map/all_to_all | solution.py:485
  75.5 3.8 %norm.1.refs_0_ = bf16[160,2048]{1,0:T(8,128)(2,1)} custom-call(s32[1,20]{1,0:T(1,128)} %get-tuple-element.20.src_ref, bf16[48,8,2048]{2,1,0:T(8,128)(2,1)} %all-to-all-done.1.recv_ref, bf16[1,2048]{1,0:T(2,128)(2,1)} %state_ref.1, f32[1,2048]{1,0:T(1,128)} %bitcast.24, bf16[16,32,128]{2,1,0:T(8,128)(2,1)} %convolution_convert_fusion.refs_0_), custom_call_target="tpu_custom_call" | custom-call | tf_op jit(solution)/shard_map/norm/pallas_call | solution.py:232
  81.9 7.2 %collective-permute-done.11.refs_8_ = bf16[160,2048]{1,0:T(8,128)(2,1)} collective-permute-done((bf16[160,2048]{1,0:T(8,128)(2,1)}, bf16[160,2048]{1,0:T(8,128)(2,1)}, u32[]{:S(2)}, u32[]{:S(2)}) %collective-permute-start.11) | collective-permute-done | bytes 655392 | tf_op jit(solution)/shard_map/ppermute | solution.py:71
  89.7 2.4 %collective-permute-start.16 = (bf16[160,2048]{1,0:T(8,128)(2,1)}, bf16[160,2048]{1,0:T(8,128)(2,1)S(1)}, u32[]{:S(2)}, u32[]{:S(2)}) collective-permute-start(bf16[160,2048]{1,0:T(8,128)(2,1)} %norm.1.refs_0_), channel_id=1, source_target_pairs={{0,96},{1,25},{2,98},{3,27},{4,100},{5,29},{6,102},{7,31},{8,104},... | collective-permute-start | bytes 1966088 | tf_op jit(solution)/shard_map/ppermute | solution.py:71
  93.8 2.6 %collective-permute-done.14.refs_15_ = bf16[1536,256]{1,0:T(8,128)(2,1)} collective-permute-done((bf16[1536,256]{1,0:T(8,128)(2,1)}, bf16[1536,256]{1,0:T(8,128)(2,1)}, u32[]{:S(2)}, u32[]{:S(2)}) %collective-permute-start.14) | collective-permute-done | bytes 786464 | tf_op jit(solution)/shard_map/ppermute | solution.py:67
  99.7 5.5 %ready.1 = (bf16[2048,512]{1,0:T(8,128)(2,1)S(1)}, bf16[2048,512]{1,0:T(8,128)(2,1)S(1)}, bf16[800,2048]{1,0:T(8,128)(2,1)S(1)}, bf16[480,2048]{1,0:T(8,128)(2,1...) custom-call(s32[1,1]{1,0:T(1,128)} %bitcast.y_ref.refs_0_, bf16[160,2048]{1,0:T(8,128)(2,1)} %fusion.refs_1_, ...), custom_call_target="tpu_custom_call" | custom-call | flops 1000 | bytes 1000 | tf_op jit(solution)/shard_map/ready/pallas_call | solution.py:309
  105.5 2.4 %collective-permute-start.8 = (bf16[160,2048]{1,0:T(8,128)(2,1)S(1)}, bf16[160,2048]{1,0:T(8,128)(2,1)S(1)}, u32[]{:S(2)}, u32[]{:S(2)}) collective-permute-start(bf16[160,2048]{1,0:T(8,128)(2,1)S(1)} %collective-permute-done.6.refs_4_), channel_id=1, source_target_pairs={{0,96},{1,25},{2,98},{3,27},{4,100},{5,29},{6,102},{7,31},{8,104},... | collective-permute-start | bytes 1966088 | tf_op jit(solution)/shard_map/ppermute | solution.py:71
  109.2 14.1 %layer_first.1 = (f32[8,512,256]{2,1,0:T(8,128)S(1)}, f32[1,2048]{1,0:T(1,128)S(1)}) custom-call(bf16[160,2048]{1,0:T(8,128)(2,1)S(1)} %copy-done.11, bf16[160,2048]{1,0:T(8,128)(2,1)S(1)} %collective-permute-done.15.refs_1_, bf16[160,2048]{1,0:T(8,128)(2,1)S(1)} %collective-permute-done.16.refs_2_, bf16[160,2048]{1,0:T(8,128)(2,1)S(1)} %collective-permute-done.17.refs_3_, ...), custom_call_target="tpu_custom_call" | custom-call | flops 8388608000 | bytes 6553600 | tf_op jit(solution)/shard_map/layer_first/pallas_call | solution.py:410
  123.4 9.6 %layer_last.1 = (f32[8,256,256]{2,1,0:T(8,128)S(1)}, bf16[8,256,256]{2,1,0:T(8,128)(2,1)}, f32[1,2048]{1,0:T(1,128)S(1)}) custom-call(bf16[160,2048]{1,0:T(8,128)(2,1)S(1)} %collective-permute-done.7.refs_0_, bf16[160,2048]{1,0:T(8,128)(2,1)S(1)} %collective-permute-done.8.refs_1_, bf16[160,2048]{1,0:T(8,128)(2,1)S(1)} %collective-permute-done.9.refs_2_, ...), custom_call_target="tpu_custom_call" | custom-call | flops 5033164800 | bytes 3932160 | tf_op jit(solution)/shard_map/layer_last/pallas_call | solution.py:410
  133.1 3.0 %collective-permute-start.18 = (bf16[8,256,256]{2,1,0:T(8,128)(2,1)}, bf16[8,256,256]{2,1,0:T(8,128)(2,1)S(1)}, u32[]{:S(2)}, u32[]{:S(2)}) collective-permute-start(bf16[8,256,256]{2,1,0:T(8,128)(2,1)} %get-tuple-element.34), channel_id=1, source_target_pairs={{0,24},{1,97},{2,26},{3,99},{4,28},{5,101},{6,30},{7,103},{8,16},{... | collective-permute-start | bytes 3145736 | tf_op jit(solution)/shard_map/ppermute | solution.py:84
  136.2 15.7 %all_to_all.21 = bf16[16,40,128]{2,1,0:T(8,128)(2,1)S(1)} all-to-all(bf16[16,40,128]{2,1,0:T(8,128)(2,1)S(1)} %maximum_maximum_fusion), channel_id=1, replica_groups=mesh['index'=16,'reader'=8] {'index'}, dimensions={0} | all-to-all | bytes 327680 | tf_op jit(solution)/shard_map/all_to_all | solution.py:514
  153.3 7.3 %all-to-all-start.3 = ((bf16[8,272,256]{2,1,0:T(8,128)(2,1)}), bf16[8,272,256]{2,1,0:T(8,128)(2,1)S(1)}, u32[]{:S(2)}, u32[]{:S(2)}) async-start(bf16[8,272,256]{2,1,0:T(8,128)(2,1)} %merge.1), calls=%async_computation.3 | async-start | bytes 2228224 | tf_op jit(solution)/shard_map/all_to_all | solution.py:521
  161.3 15.2 %all-to-all-done.3 = bf16[8,272,256]{2,1,0:T(8,128)(2,1)S(1)} async-done(((bf16[8,272,256]{2,1,0:T(8,128)(2,1)}), bf16[8,272,256]{2,1,0:T(8,128)(2,1)S(1)}, u32[]{:S(2)}, u32[]{:S(2)}) %all-to-all-start.3) | async-done | bytes 1114144 | tf_op jit(solution)/shard_map/all_to_all | solution.py:521
  (81 shorter events, 25.4 us)
Async XLA Ops:
  2.7 10.7 %collective-permute-start.1 = (bf16[160,2048]{1,0:T(8,128)(2,1)}, bf16[160,2048]{1,0:T(8,128)(2,1)}, u32[]{:S(2)}, u32[]{:S(2)}) collective-permute-start(bf16[160,2048]{1,0:T(8,128)(2,1)} %fusion.refs_1_), channel_id=1, source_target_pairs={{0,8},{1,33},{2,10},{3,35},{4,12},{5,37},{6,14},{7,39},{8,0},{9,41... | collective-permute-start | bytes 1966088 | tf_op jit(solution)/shard_map/ppermute | solution.py:80
  7.8 28.5 %collective-permute-start = (bf16[1536,256]{1,0:T(8,128)(2,1)}, bf16[1536,256]{1,0:T(8,128)(2,1)}, u32[]{:S(2)}, u32[]{:S(2)}) collective-permute-start(bf16[1536,256]{1,0:T(8,128)(2,1)} %get-tuple-element.21), channel_id=1, source_target_pairs={{0,24},{1,97},{2,26},{3,99},{4,28},{5,101},{6,30},{7,103},{8,16},{... | collective-permute-start | bytes 2359304 | tf_op jit(solution)/shard_map/ppermute | solution.py:84
  9.7 26.6 %collective-permute-start.2 = (bf16[160,2048]{1,0:T(8,128)(2,1)}, bf16[160,2048]{1,0:T(8,128)(2,1)S(1)}, u32[]{:S(2)}, u32[]{:S(2)}) collective-permute-start(bf16[160,2048]{1,0:T(8,128)(2,1)} %fusion.refs_1_), channel_id=1, source_target_pairs={{0,32},{1,9},{2,34},{3,11},{4,36},{5,13},{6,38},{7,15},{8,40},{9,1... | collective-permute-start | bytes 1966088 | tf_op jit(solution)/shard_map/ppermute | solution.py:71
  11.3 25.0 %collective-permute-start.3 = (bf16[160,2048]{1,0:T(8,128)(2,1)}, bf16[160,2048]{1,0:T(8,128)(2,1)S(1)}, u32[]{:S(2)}, u32[]{:S(2)}) collective-permute-start(bf16[160,2048]{1,0:T(8,128)(2,1)} %fusion.refs_1_), channel_id=1, source_target_pairs={{0,96},{1,25},{2,98},{3,27},{4,100},{5,29},{6,102},{7,31},{8,104},... | collective-permute-start | bytes 1966088 | tf_op jit(solution)/shard_map/ppermute | solution.py:71
  13.5 31.2 %collective-permute-start.4 = (bf16[160,2048]{1,0:T(8,128)(2,1)}, bf16[160,2048]{1,0:T(8,128)(2,1)S(1)}, u32[]{:S(2)}, u32[]{:S(2)}) collective-permute-start(bf16[160,2048]{1,0:T(8,128)(2,1)} %collective-permute-done.1.refs_1_.refs_5_), channel_id=1, source_target_pairs={{0,32},{1,9},{2,34},{3,11},{4,36},{5,13},{6,38},{7,15},{8,40},{9,1... | collective-permute-start | bytes 1966088 | tf_op jit(solution)/shard_map/ppermute | solution.py:71
  15.3 29.4 %collective-permute-start.5 = (bf16[160,2048]{1,0:T(8,128)(2,1)}, bf16[160,2048]{1,0:T(8,128)(2,1)S(1)}, u32[]{:S(2)}, u32[]{:S(2)}) collective-permute-start(bf16[160,2048]{1,0:T(8,128)(2,1)} %collective-permute-done.1.refs_1_.refs_5_), channel_id=1, source_target_pairs={{0,96},{1,25},{2,98},{3,27},{4,100},{5,29},{6,102},{7,31},{8,104},... | collective-permute-start | bytes 1966088 | tf_op jit(solution)/shard_map/ppermute | solution.py:71
  46.3 29.1 %all-to-all-start.1 = ((bf16[48,8,2048]{2,1,0:T(8,128)(2,1)}), bf16[48,8,2048]{2,1,0:T(8,128)(2,1)}, u32[]{:S(2)}, u32[]{:S(2)}) async-start(bf16[48,8,2048]{2,1,0:T(8,128)(2,1)} %send.1), calls=%async_computation.1 | async-start | bytes 3145728 | tf_op jit(solution)/shard_map/all_to_all | solution.py:485
  52.6 28.7 %collective-permute-start.10 = (bf16[160,2048]{1,0:T(8,128)(2,1)}, bf16[160,2048]{1,0:T(8,128)(2,1)}, u32[]{:S(2)}, u32[]{:S(2)}) collective-permute-start(bf16[160,2048]{1,0:T(8,128)(2,1)} %fusion.refs_1_), channel_id=1, source_target_pairs={{0,64},{1,17},{2,66},{3,19},{4,68},{5,21},{6,70},{7,23},{8,72},{9,... | collective-permute-start | bytes 1966088 | tf_op jit(solution)/shard_map/ppermute | solution.py:71
  55.4 34.2 %collective-permute-start.12 = (bf16[1536,256]{1,0:T(8,128)(2,1)}, bf16[1536,256]{1,0:T(8,128)(2,1)}, u32[]{:S(2)}, u32[]{:S(2)}) collective-permute-start(bf16[1536,256]{1,0:T(8,128)(2,1)} %get-tuple-element.23.refs_12_), channel_id=1, source_target_pairs={{0,6},{1,7},{2,0},{3,1},{4,2},{5,3},{6,4},{7,5},{8,14},{9,15},{10,... | collective-permute-start | bytes 2359304 | tf_op jit(solution)/shard_map/ppermute | solution.py:67
  58.2 33.8 %collective-permute-start.13 = (bf16[1536,256]{1,0:T(8,128)(2,1)}, bf16[1536,256]{1,0:T(8,128)(2,1)}, u32[]{:S(2)}, u32[]{:S(2)}) collective-permute-start(bf16[1536,256]{1,0:T(8,128)(2,1)} %get-tuple-element.23.refs_12_), channel_id=1, source_target_pairs={{0,4},{1,5},{2,6},{3,7},{4,0},{5,1},{6,2},{7,3},{8,12},{9,13},{10,... | collective-permute-start | bytes 2359304 | tf_op jit(solution)/shard_map/ppermute | solution.py:67
  58.7 30.4 %collective-permute-start.11 = (bf16[160,2048]{1,0:T(8,128)(2,1)}, bf16[160,2048]{1,0:T(8,128)(2,1)}, u32[]{:S(2)}, u32[]{:S(2)}) collective-permute-start(bf16[160,2048]{1,0:T(8,128)(2,1)} %collective-permute-done.1.refs_1_.refs_5_), channel_id=1, source_target_pairs={{0,64},{1,17},{2,66},{3,19},{4,68},{5,21},{6,70},{7,23},{8,72},{9,... | collective-permute-start | bytes 1966088 | tf_op jit(solution)/shard_map/ppermute | solution.py:71
  59.0 37.4 %copy-start.2 = (bf16[256,2048]{1,0:T(8,128)(2,1)S(1)}, bf16[256,2048]{1,0:T(8,128)(2,1)}, u32[]{:S(2)}) copy-start(bf16[256,2048]{1,0:T(8,128)(2,1)} %refs_11_.1) | copy-start | bytes 3145732
  63.6 32.8 %copy-start = (bf16[2048,256]{1,0:T(8,128)(2,1)S(1)}, bf16[2048,256]{1,0:T(8,128)(2,1)}, u32[]{:S(2)}) copy-start(bf16[2048,256]{1,0:T(8,128)(2,1)} %refs_9_.1) | copy-start | bytes 3145732
  63.6 32.8 %copy-start.1 = (bf16[2048,256]{1,0:T(8,128)(2,1)S(1)}, bf16[2048,256]{1,0:T(8,128)(2,1)}, u32[]{:S(2)}) copy-start(bf16[2048,256]{1,0:T(8,128)(2,1)} %refs_10_.1) | copy-start | bytes 3145732
  63.6 32.8 %collective-permute-start.14 = (bf16[1536,256]{1,0:T(8,128)(2,1)}, bf16[1536,256]{1,0:T(8,128)(2,1)}, u32[]{:S(2)}, u32[]{:S(2)}) collective-permute-start(bf16[1536,256]{1,0:T(8,128)(2,1)} %get-tuple-element.23.refs_12_), channel_id=1, source_target_pairs={{0,2},{1,3},{2,4},{3,5},{4,6},{5,7},{6,0},{7,1},{8,10},{9,11},{10,... | collective-permute-start | bytes 2359304 | tf_op jit(solution)/shard_map/ppermute | solution.py:67
  81.2 23.9 %collective-permute-start.6 = (bf16[160,2048]{1,0:T(8,128)(2,1)}, bf16[160,2048]{1,0:T(8,128)(2,1)S(1)}, u32[]{:S(2)}, u32[]{:S(2)}) collective-permute-start(bf16[160,2048]{1,0:T(8,128)(2,1)} %norm.1.refs_0_), channel_id=1, source_target_pairs={{0,8},{1,33},{2,10},{3,35},{4,12},{5,37},{6,14},{7,39},{8,0},{9,41... | collective-permute-start | bytes 1966088 | tf_op jit(solution)/shard_map/ppermute | solution.py:80
  89.1 18.8 %collective-permute-start.15 = (bf16[160,2048]{1,0:T(8,128)(2,1)}, bf16[160,2048]{1,0:T(8,128)(2,1)S(1)}, u32[]{:S(2)}, u32[]{:S(2)}) collective-permute-start(bf16[160,2048]{1,0:T(8,128)(2,1)} %norm.1.refs_0_), channel_id=1, source_target_pairs={{0,32},{1,9},{2,34},{3,11},{4,36},{5,13},{6,38},{7,15},{8,40},{9,1... | collective-permute-start | bytes 1966088 | tf_op jit(solution)/shard_map/ppermute | solution.py:71
  89.7 18.3 %collective-permute-start.16 = (bf16[160,2048]{1,0:T(8,128)(2,1)}, bf16[160,2048]{1,0:T(8,128)(2,1)S(1)}, u32[]{:S(2)}, u32[]{:S(2)}) collective-permute-start(bf16[160,2048]{1,0:T(8,128)(2,1)} %norm.1.refs_0_), channel_id=1, source_target_pairs={{0,96},{1,25},{2,98},{3,27},{4,100},{5,29},{6,102},{7,31},{8,104},... | collective-permute-start | bytes 1966088 | tf_op jit(solution)/shard_map/ppermute | solution.py:71
  92.0 17.2 %collective-permute-start.17 = (bf16[160,2048]{1,0:T(8,128)(2,1)}, bf16[160,2048]{1,0:T(8,128)(2,1)S(1)}, u32[]{:S(2)}, u32[]{:S(2)}) collective-permute-start(bf16[160,2048]{1,0:T(8,128)(2,1)} %norm.1.refs_0_), channel_id=1, source_target_pairs={{0,64},{1,17},{2,66},{3,19},{4,68},{5,21},{6,70},{7,23},{8,72},{9,... | collective-permute-start | bytes 1966088 | tf_op jit(solution)/shard_map/ppermute | solution.py:71
  105.2 18.2 %collective-permute-start.7 = (bf16[160,2048]{1,0:T(8,128)(2,1)S(1)}, bf16[160,2048]{1,0:T(8,128)(2,1)S(1)}, u32[]{:S(2)}, u32[]{:S(2)}) collective-permute-start(bf16[160,2048]{1,0:T(8,128)(2,1)S(1)} %collective-permute-done.6.refs_4_), channel_id=1, source_target_pairs={{0,32},{1,9},{2,34},{3,11},{4,36},{5,13},{6,38},{7,15},{8,40},{9,1... | collective-permute-start | bytes 1966088 | tf_op jit(solution)/shard_map/ppermute | solution.py:71
  105.5 17.8 %collective-permute-start.8 = (bf16[160,2048]{1,0:T(8,128)(2,1)S(1)}, bf16[160,2048]{1,0:T(8,128)(2,1)S(1)}, u32[]{:S(2)}, u32[]{:S(2)}) collective-permute-start(bf16[160,2048]{1,0:T(8,128)(2,1)S(1)} %collective-permute-done.6.refs_4_), channel_id=1, source_target_pairs={{0,96},{1,25},{2,98},{3,27},{4,100},{5,29},{6,102},{7,31},{8,104},... | collective-permute-start | bytes 1966088 | tf_op jit(solution)/shard_map/ppermute | solution.py:71
  107.9 15.5 %collective-permute-start.9 = (bf16[160,2048]{1,0:T(8,128)(2,1)S(1)}, bf16[160,2048]{1,0:T(8,128)(2,1)S(1)}, u32[]{:S(2)}, u32[]{:S(2)}) collective-permute-start(bf16[160,2048]{1,0:T(8,128)(2,1)S(1)} %collective-permute-done.6.refs_4_), channel_id=1, source_target_pairs={{0,64},{1,17},{2,66},{3,19},{4,68},{5,21},{6,70},{7,23},{8,72},{9,... | collective-permute-start | bytes 1966088 | tf_op jit(solution)/shard_map/ppermute | solution.py:71
  133.1 19.1 %collective-permute-start.18 = (bf16[8,256,256]{2,1,0:T(8,128)(2,1)}, bf16[8,256,256]{2,1,0:T(8,128)(2,1)S(1)}, u32[]{:S(2)}, u32[]{:S(2)}) collective-permute-start(bf16[8,256,256]{2,1,0:T(8,128)(2,1)} %get-tuple-element.34), channel_id=1, source_target_pairs={{0,24},{1,97},{2,26},{3,99},{4,28},{5,101},{6,30},{7,103},{8,16},{... | collective-permute-start | bytes 3145736 | tf_op jit(solution)/shard_map/ppermute | solution.py:84
  153.3 23.1 %all-to-all-start.3 = ((bf16[8,272,256]{2,1,0:T(8,128)(2,1)}), bf16[8,272,256]{2,1,0:T(8,128)(2,1)S(1)}, u32[]{:S(2)}, u32[]{:S(2)}) async-start(bf16[8,272,256]{2,1,0:T(8,128)(2,1)} %merge.1), calls=%async_computation.3 | async-start | bytes 2228224 | tf_op jit(solution)/shard_map/all_to_all | solution.py:521
  (13 other events, 70.4 us)
